TPU v7x, 32 devices: a whole 2x2x4 slice. The times are simulated.
32 devices in a mesh: section: 4 (over x, core), seq: 2 (over y), tp: 4 (over z).
Axes of the slice: x: 2, y: 2, z: 4, core: 2. Of those that a mesh axis runs over, the one named last changes fastest.
Arguments:
- streams: float32 [4, 4, 256, 1280], P('section', None, 'seq'), may hold values from -6 to 6
- head_streams: float32 [4, 256, 1280], P(None, 'seq'), may hold values from -6 to 6
- gains: float32 [4, 2, 1280], P('section'), may hold values from 0.1 to 1.9
- w_qkv: bfloat16 [4, 1280, 3, 1280], P('section', None, None, 'tp'), may hold values from -40 to 40
- w_out: bfloat16 [4, 1280, 1280], P('section', None, 'tp'), may hold values from -0.15625 to 0.15625
- w_up: bfloat16 [4, 1280, 5120], P('section', None, 'tp'), may hold values from -0.15625 to 0.15625
- w_down: bfloat16 [4, 1280, 5120], P('section', None, 'tp'), may hold values from -0.078125 to 0.078125
Outputs:
- recon: float32 [4, 4, 256, 1280], P('section', None, 'seq')
- grad_qkv: bfloat16 [4, 1280, 3, 1280], P('section', 'seq', None, 'tp')
- grad_out: bfloat16 [4, 1280, 1280], P('section', 'seq', 'tp')
- grad_up: bfloat16 [4, 1280, 5120], P('section', 'seq', 'tp')
- grad_down: bfloat16 [4, 1280, 5120], P('section', 'seq', 'tp')
All inputs are finite; a program needn't handle non-finite values.
Results may differ from a plain program's by a relative error of at most 0.028.
Values may be sent and summed in bfloat16 or wider, within the bound.
No kernel may reach another device: no remote copies, remote signals or barrier semaphores. Data moves between devices by JAX's collectives and lax.ppermute only.
A program may use at most 128 MiB of HBM per device.

v0:
```python
import jax
import jax.numpy as jnp
from jax import lax
from jax.sharding import PartitionSpec as P

HEAD_DIM = 64
TICKS = 2


def from_behind(shard, axis, by):
    length = lax.axis_size(axis)
    pairs = [(i, i + by) for i in range(length) if 0 <= i + by < length]
    return lax.ppermute(shard, axis, pairs)


def as_sent(shard):
    return jax.tree.map(lambda a: a.astype(jnp.bfloat16) if a.dtype == jnp.float32 else a, shard)


def layer_norm(values, gain):
    centre = values - jnp.mean(values, -1, keepdims=True)
    inv_std = lax.rsqrt(jnp.mean(centre * centre, -1, keepdims=True) + 1e-06)
    unit_vals = centre * inv_std
    return (unit_vals * gain, unit_vals, inv_std)


def norm_back(grad, gain, unit_vals, inv_std):
    scaled = grad * gain
    return inv_std * (
        scaled
        - jnp.mean(scaled, -1, keepdims=True)
        - unit_vals * jnp.mean(scaled * unit_vals, -1, keepdims=True)
    )


def gelu_tanh(values):
    return jax.nn.gelu(values, approximate=True)


def block_step(inputs, gain_pair, w_flat, w_out, w_up, w_down):
    upper, lower, grad_upper, grad_lower = (inputs[0], inputs[1], inputs[2], inputs[3])
    rows = upper.shape[0]
    local = w_out.shape[1]
    heads = local // HEAD_DIM
    normed_up, unit_up, inv_up = layer_norm(upper, gain_pair[1])
    normed_low = normed_up.astype(jnp.bfloat16)
    hidden_pre = jnp.dot(normed_low, w_up, preferred_element_type=jnp.float32)
    hidden = gelu_tanh(hidden_pre).astype(jnp.bfloat16)
    mlp_part = jnp.einsum("tf,df->td", hidden, w_down, preferred_element_type=jnp.float32)
    grad_lower_low = grad_lower.astype(jnp.bfloat16)
    grad_hidden = jnp.dot(grad_lower_low, w_down, preferred_element_type=jnp.float32)
    unused, pull = jax.vjp(gelu_tanh, hidden_pre)
    grad_pre = pull(grad_hidden)[0].astype(jnp.bfloat16)
    normed_part = jnp.einsum("tf,df->td", grad_pre, w_up, preferred_element_type=jnp.float32)
    mlp_out, grad_normed = lax.psum((mlp_part, normed_part), "tp")
    lower_in = lower - mlp_out
    normed_att, unit_att, inv_att = layer_norm(lower_in, gain_pair[0])
    att_low = normed_att.astype(jnp.bfloat16)
    projected = (
        jnp.dot(att_low, w_flat, preferred_element_type=jnp.float32)
        .astype(jnp.bfloat16)
        .reshape(rows, 3, local)
    )
    query = projected[:, 0]
    key_value = projected[:, 1:]
    gathered = lax.all_gather(key_value, "seq", axis=0, tiled=True)
    query_heads = query.reshape(rows, heads, HEAD_DIM)
    all_keys = gathered[:, 0].reshape(-1, heads, HEAD_DIM)
    all_values = gathered[:, 1].reshape(-1, heads, HEAD_DIM)
    scores = (
        jnp.einsum("qhd,khd->hqk", query_heads, all_keys, preferred_element_type=jnp.float32)
        * 0.125
    )
    top = jnp.max(scores, -1, keepdims=True)
    lse = top + jnp.log(jnp.sum(jnp.exp(scores - top), -1, keepdims=True))
    probs = jnp.exp(scores - lse)
    probs_low = probs.astype(jnp.bfloat16)
    mixed = (
        jnp.einsum("hqk,khd->qhd", probs_low, all_values, preferred_element_type=jnp.float32)
        .astype(jnp.bfloat16)
        .reshape(rows, local)
    )
    att_part = jnp.einsum("tc,dc->td", mixed, w_out, preferred_element_type=jnp.float32)
    upper_total = grad_upper + norm_back(grad_normed, gain_pair[1], unit_up, inv_up)
    total_low = upper_total.astype(jnp.bfloat16)
    grad_mixed = jnp.dot(total_low, w_out, preferred_element_type=jnp.float32).astype(jnp.bfloat16)
    grad_heads = grad_mixed.reshape(rows, heads, HEAD_DIM)
    grad_probs = jnp.einsum(
        "qhd,khd->hqk", grad_heads, all_values, preferred_element_type=jnp.float32
    )
    delta = jnp.sum(probs * grad_probs, -1, keepdims=True)
    grad_scores = (probs * (grad_probs - delta)).astype(jnp.bfloat16)
    grad_query = (
        (
            0.125
            * jnp.einsum("hqk,khd->qhd", grad_scores, all_keys, preferred_element_type=jnp.float32)
        )
        .astype(jnp.bfloat16)
        .reshape(rows, local)
    )
    grad_keys = 0.125 * jnp.einsum(
        "hqk,qhd->khd", grad_scores, query_heads, preferred_element_type=jnp.float32
    )
    grad_values = jnp.einsum(
        "hqk,qhd->khd", probs_low, grad_heads, preferred_element_type=jnp.float32
    )
    kv_grad = lax.psum_scatter(
        jnp.stack(
            [
                grad_keys.reshape(rows * lax.axis_size("seq"), local),
                grad_values.reshape(rows * lax.axis_size("seq"), local),
            ],
            1,
        ).astype(jnp.bfloat16),
        "seq",
        scatter_dimension=0,
        tiled=True,
    )
    grad_proj = jnp.concatenate([grad_query[:, None], kv_grad], 1).reshape(rows, 3 * local)
    att_grad_part = jnp.einsum("tc,dc->td", grad_proj, w_flat, preferred_element_type=jnp.float32)
    att_out, grad_att = (
        lax.psum(att_part.astype(jnp.bfloat16), "tp").astype(jnp.float32),
        lax.psum(att_grad_part.astype(jnp.bfloat16), "tp").astype(jnp.float32),
    )
    upper_in = upper - att_out
    grad_lower_in = grad_lower + norm_back(grad_att, gain_pair[0], unit_att, inv_att)
    result = jnp.stack([upper_in, lower_in, upper_total, grad_lower_in])
    terms = (
        jnp.dot(att_low.T, grad_proj, preferred_element_type=jnp.float32),
        jnp.dot(total_low.T, mixed, preferred_element_type=jnp.float32),
        jnp.dot(normed_low.T, grad_pre, preferred_element_type=jnp.float32),
        jnp.dot(grad_lower_low.T, hidden, preferred_element_type=jnp.float32),
    )
    return (result, terms)


def per_device(streams, head_streams, gains, w_qkv, w_out, w_up, w_down):
    gain_pair = gains[0]
    width = w_qkv.shape[1]
    local = w_qkv.shape[3]
    w_flat = w_qkv[0].reshape(width, 3 * local)
    inputs = streams[0]
    totals = None
    result = None
    for tick in range(TICKS):
        if tick > 0:
            received = from_behind(result.astype(jnp.bfloat16), "section", -1).astype(result.dtype)
            is_last = lax.axis_index("section") == lax.axis_size("section") - 1
            inputs = jnp.where(is_last, head_streams, received)
        result, terms = block_step(inputs, gain_pair, w_flat, w_out[0], w_up[0], w_down[0])
        totals = terms if totals is None else tuple((old + new for old, new in zip(totals, terms)))
    grad_qkv, grad_out, grad_up, grad_down = jax.tree.map(
        lambda part: part.astype(jnp.float32),
        lax.psum_scatter(as_sent(totals), "seq", scatter_dimension=0, tiled=True),
    )
    grad_qkv = grad_qkv.astype(jnp.bfloat16).reshape(-1, 3, local)[None]
    return (
        result[None],
        grad_qkv,
        grad_out.astype(jnp.bfloat16)[None],
        grad_up.astype(jnp.bfloat16)[None],
        grad_down.astype(jnp.bfloat16)[None],
    )


def solution(mesh):
    placed = (
        P("section", None, "seq", None),
        P(None, "seq", None),
        P("section", None, None),
        P("section", None, None, "tp"),
        P("section", None, "tp"),
        P("section", None, "tp"),
        P("section", None, "tp"),
    )
    return jax.shard_map(
        per_device,
        mesh=mesh,
        in_specs=placed,
        out_specs=(
            P("section", None, "seq", None),
            P("section", "seq", None, "tp"),
            P("section", "seq", "tp"),
            P("section", "seq", "tp"),
            P("section", "seq", "tp"),
        ),
        check_vma=False,
    )
```

profile of v0, /device:TPU:0, one launch (start us, length us, event | category | flops | bytes accessed | tf_op | source)
XLA Modules:
  0.0 490.9 jit_solution(11570977479607576781)
XLA Ops:
  10.7 2.8 fusion.16
  19.9 63.2 %all-reduce.11.cloned.1.call-done = (f32[128,1280]{1,0:T(8,128)}, f32[128,1280]{1,0:T(8,128)}) async-done(((f32[128,1280]{1,0:T(8,128)}, f32[128,1280]{1,0:T(8,128)}), (f32[128,1280]{1,0:T(8,128)}, f32[128,1280]{1,0:T(8,128)})) %all-reduce.11.cloned.1.call-update) | async-done | bytes 1310736 | tf_op jit(solution)/shard_map/psum | solution.py:55
  83.1 2.8 convert_bitcast_fusion
  88.5 2.9 convolution_convert_fusion.5
  91.5 6.6 %all_gather.6 = bf16[256,2,320]{0,2,1:T(8,128)(2,1)S(1)} all-gather(bf16[128,2,320]{0,2,1:T(8,128)(2,1)S(1)} %slice.84), channel_id=1, replica_groups=mesh['section'=4,'seq'=2,'tp'=4] {'seq'}, dimensions={0}, use_global_device_ids=true | all-gather | bytes 491520 | tf_op jit(solution)/shard_map/all_gather | solution.py:66
  109.6 6.9 %reduce-scatter.19.cloned.1.call-done = bf16[128,640]{1,0:T(8,128)(2,1)} async-done(((bf16[256,640]{1,0:T(8,128)(2,1)}), bf16[128,640]{1,0:T(8,128)(2,1)}) %reduce-scatter.19.cloned.1.call-update) | async-done | bytes 163856
  119.2 3.0 convolution_convert_fusion.2
  122.2 40.9 %all-reduce.15.cloned.1.call-done = (bf16[128,1280]{1,0:T(8,128)(2,1)}, bf16[128,1280]{1,0:T(8,128)(2,1)}) async-done(((bf16[128,1280]{1,0:T(8,128)(2,1)}, bf16[128,1280]{1,0:T(8,128)(2,1)}), (bf16[128,1280]{1,0:T(8,128)(2,1)}, bf16[128,1280]{1,0:T(8,128)(2,1)})) %all-reduce.15.cloned.1.call-update) | async-done | bytes 655376 | tf_op jit(solution)/shard_map/psum | solution.py:123
  169.2 4.0 collective-permute-done
  181.4 72.3 %all-reduce.9.cloned.1.call-done = (f32[128,1280]{1,0:T(8,128)}, f32[128,1280]{1,0:T(8,128)}) async-done(((f32[128,1280]{1,0:T(8,128)}, f32[128,1280]{1,0:T(8,128)}), (f32[128,1280]{1,0:T(8,128)}, f32[128,1280]{1,0:T(8,128)})) %all-reduce.9.cloned.1.call-update) | async-done | bytes 1310736 | tf_op jit(solution)/shard_map/psum | solution.py:55
  256.9 6.6 %all_gather.7 = bf16[256,2,320]{0,2,1:T(8,128)(2,1)S(1)} all-gather(bf16[128,2,320]{0,2,1:T(8,128)(2,1)S(1)} %slice.90), channel_id=1, replica_groups=mesh['section'=4,'seq'=2,'tp'=4] {'seq'}, dimensions={0}, use_global_device_ids=true | all-gather | bytes 491520 | tf_op jit(solution)/shard_map/all_gather | solution.py:66
  275.7 6.2 %reduce-scatter.21.cloned.1.call-done = bf16[128,640]{1,0:T(8,128)(2,1)} async-done(((bf16[256,640]{1,0:T(8,128)(2,1)}), bf16[128,640]{1,0:T(8,128)(2,1)}) %reduce-scatter.21.cloned.1.call-update) | async-done | bytes 163856
  291.6 2.6 convolution_bitcast_fusion
  294.2 2.9 fusion.1
  297.1 5.7 %copy.25 = bf16[1280,1280]{1,0:T(8,128)(2,1)} copy(bf16[1280,1280]{0,1:T(8,128)(2,1)} %fusion.1) | data formatting | bytes 6553600
  307.8 4.5 copy.21
  315.0 2.9 fusion
  317.9 9.6 %all-reduce.13.cloned.1.call-done = (bf16[128,1280]{1,0:T(8,128)(2,1)}, bf16[128,1280]{1,0:T(8,128)(2,1)}) async-done(((bf16[128,1280]{1,0:T(8,128)(2,1)}, bf16[128,1280]{1,0:T(8,128)(2,1)}), (bf16[128,1280]{1,0:T(8,128)(2,1)}, bf16[128,1280]{1,0:T(8,128)(2,1)})) %all-reduce.13.cloned.1.call-update) | async-done | bytes 655376 | tf_op jit(solution)/shard_map/psum | solution.py:123
  332.0 17.4 %reduce-scatter.25.cloned.1.call-done = bf16[640,320]{1,0:T(8,128)(2,1)} async-done(((bf16[1280,320]{1,0:T(8,128)(2,1)}), bf16[640,320]{1,0:T(8,128)(2,1)}) %reduce-scatter.25.cloned.1.call-update) | async-done | bytes 409616
  351.4 45.2 %reduce-scatter.27.cloned.1.call-done = bf16[640,1280]{1,0:T(8,128)(2,1)} async-done(((bf16[1280,1280]{1,0:T(8,128)(2,1)}), bf16[640,1280]{1,0:T(8,128)(2,1)}) %reduce-scatter.27.cloned.1.call-update) | async-done | bytes 1638416
  396.6 3.5 copy.26
  400.1 3.7 copy.15
  403.8 32.6 %reduce-scatter.23.cloned.1.call-done = bf16[640,960]{1,0:T(8,128)(2,1)} async-done(((bf16[1280,960]{1,0:T(8,128)(2,1)}), bf16[640,960]{1,0:T(8,128)(2,1)}) %reduce-scatter.23.cloned.1.call-update) | async-done | bytes 1228816
  438.8 45.2 %reduce-scatter.17.cloned.1.call-done = bf16[640,1280]{1,0:T(8,128)(2,1)} async-done(((bf16[1280,1280]{1,0:T(8,128)(2,1)}), bf16[640,1280]{1,0:T(8,128)(2,1)}) %reduce-scatter.17.cloned.1.call-update) | async-done | bytes 1638416 | tf_op jit(solution)/shard_map/reduce_scatter | solution.py:154
  (203 shorter events, 81.9 us)
Async XLA Ops:
  7.2 75.9 %all-reduce.11.cloned.1.call-start = ((), (), s32[]{:S(2)}) async-start(), calls=%async_computation.13 | async-start | bytes 2621440 | tf_op jit(solution)/shard_map/psum | solution.py:55
  10.7 88.2 %copy-start.37 = (f32[128]{0:T(128)}, f32[128]{0:T(128)S(1)}, u32[]{:S(2)}) copy-start(f32[128]{0:T(128)S(1)} %add_rsqrt_fusion.3) | copy-start | bytes 1540
  19.9 96.6 %reduce-scatter.19.cloned.1.call-start = ((), (), s32[]{:S(2)}) async-start(), calls=%async_computation.7 | async-start | bytes 491520
  87.2 77.4 %copy-start.39 = (f32[128]{0:T(128)}, f32[128]{0:T(128)S(1)}, u32[]{:S(2)}) copy-start(f32[128]{0:T(128)S(1)} %broadcast_multiply_fusion.10) | copy-start | bytes 1540
  88.5 76.1 %copy-start.47 = (f32[128]{0:T(128)}, f32[128]{0:T(128)S(1)}, u32[]{:S(2)}) copy-start(f32[128]{0:T(128)S(1)} %add_rsqrt_fusion.2) | copy-start | bytes 1540
  88.5 10.4 %copy-start.10 = (f32[1,4,128,1280]{3,2,1,0:T(8,128)S(1)}, f32[1,4,128,1280]{3,2,1,0:T(8,128)}, u32[]{:S(2)}) copy-start(f32[1,4,128,1280]{3,2,1,0:T(8,128)} %param.7) | copy-start | bytes 7864324
  88.5 10.4 %copy-start.23 = (f32[128,1280]{1,0:T(8,128)S(1)}, f32[128,1280]{1,0:T(8,128)}, u32[]{:S(2)}) copy-start(f32[128,1280]{1,0:T(8,128)} %get-tuple-element.27) | copy-start | bytes 1966084
  103.9 59.2 %all-reduce.15.cloned.1.call-start = ((), (), s32[]{:S(2)}) async-start(), calls=%async_computation.15 | async-start | bytes 1310720 | tf_op jit(solution)/shard_map/psum | solution.py:123
  107.3 10.9 %copy-start.33 = (bf16[5,64,128]{2,1,0:T(8,128)(2,1)}, bf16[5,64,128]{2,1,0:T(8,128)(2,1)S(1)}, u32[]{:S(2)}) copy-start(bf16[5,64,128]{2,1,0:T(8,128)(2,1)S(1)} %convolution_convert_fusion.11) | copy-start | bytes 245764
  122.2 131.6 %all-reduce.9.cloned.1.call-start = ((), (), s32[]{:S(2)}) async-start(), calls=%async_computation.12 | async-start | bytes 2621440 | tf_op jit(solution)/shard_map/psum | solution.py:55
  167.9 5.3 %collective-permute-start = (bf16[4,128,1280]{2,1,0:T(8,128)(2,1)}, bf16[4,128,1280]{2,1,0:T(8,128)(2,1)}, u32[]{:S(2)}, u32[]{:S(2)}) collective-permute-start(bf16[4,128,1280]{2,1,0:T(8,128)(2,1)} %pad_maximum_fusion), channel_id=1, source_target_pairs={{8,0},{16,8},{24,16},{9,1},{17,9},{25,17},{10,2},{18,10},{26,18},{... | collective-permute-start | bytes 3932168 | tf_op jit(solution)/shard_map/ppermute | solution.py:13
  175.1 78.6 %copy-start.41 = (f32[128]{0:T(128)}, f32[128]{0:T(128)S(1)}, u32[]{:S(2)}) copy-start(f32[128]{0:T(128)S(1)} %add_rsqrt_fusion.1) | copy-start | bytes 1540
  181.2 74.7 %copy-start.4 = (bf16[1,1280,3,320]{1,3,2,0:T(8,128)(2,1)S(1)}, bf16[1,1280,3,320]{1,3,2,0:T(8,128)(2,1)}, u32[]{:S(2)}) copy-start(bf16[1,1280,3,320]{1,3,2,0:T(8,128)(2,1)} %param.10) | copy-start | bytes 7372804
  181.2 100.7 %reduce-scatter.21.cloned.1.call-start = ((), (), s32[]{:S(2)}) async-start(), calls=%async_computation.8 | async-start | bytes 491520
  255.9 8.4 %copy-start.6 = (f32[4,128,1280]{2,1,0:T(8,128)S(1)}, f32[4,128,1280]{2,1,0:T(8,128)}, u32[]{:S(2)}) copy-start(f32[4,128,1280]{2,1,0:T(8,128)} %copy-done.5) | copy-start | bytes 7864324
  255.9 8.4 %copy-start.24 = (f32[128,1280]{1,0:T(8,128)S(1)}, f32[128,1280]{1,0:T(8,128)}, u32[]{:S(2)}) copy-start(f32[128,1280]{1,0:T(8,128)} %get-tuple-element.25) | copy-start | bytes 1966084
  269.3 58.2 %all-reduce.13.cloned.1.call-start = ((), (), s32[]{:S(2)}) async-start(), calls=%async_computation.14 | async-start | bytes 1310720 | tf_op jit(solution)/shard_map/psum | solution.py:123
  273.4 13.3 %copy-start.34 = (bf16[5,64,128]{2,1,0:T(8,128)(2,1)S(1)}, bf16[5,64,128]{2,1,0:T(8,128)(2,1)}, u32[]{:S(2)}) copy-start(bf16[5,64,128]{2,1,0:T(8,128)(2,1)} %copy-done.33) | copy-start | bytes 245764
  286.6 62.8 %reduce-scatter.25.cloned.1.call-start = ((), (), s32[]{:S(2)}) async-start(), calls=%async_computation.10 | async-start | bytes 1474560
  291.5 105.0 %reduce-scatter.27.cloned.1.call-start = ((), (), s32[]{:S(2)}) async-start(), calls=%async_computation.11 | async-start | bytes 4915200
  302.8 133.7 %reduce-scatter.23.cloned.1.call-start = ((), (), s32[]{:S(2)}) async-start(), calls=%async_computation.9 | async-start | bytes 3932160
  312.3 171.7 %reduce-scatter.17.cloned.1.call-start = ((), (), s32[]{:S(2)}) async-start(), calls=%async_computation.6 | async-start | bytes 4915200 | tf_op jit(solution)/shard_map/reduce_scatter | solution.py:154
  317.8 9.7 %copy-start.46 = (f32[128]{0:T(128)S(1)}, f32[128]{0:T(128)}, u32[]{:S(2)}) copy-start(f32[128]{0:T(128)} %copy-done.44) | copy-start | bytes 1540
  400.1 83.9 %copy-start.1 = (bf16[1,1280,1280]{2,1,0:T(8,128)(2,1)S(1)}, bf16[1,1280,1280]{2,1,0:T(8,128)(2,1)}, u32[]{:S(2)}) copy-start(bf16[1,1280,1280]{2,1,0:T(8,128)(2,1)} %param.13) | copy-start | bytes 9830404
  (35 other events, 99.1 us)
Sparse Core Ops, SparseCore 0:
  20.0 63.0 all-reduce.10
  104.0 12.3 reduce-scatter.18
  122.3 40.7 all-reduce.14
  181.3 72.3 all-reduce.8
  269.5 12.3 reduce-scatter.20
  286.7 40.7 all-reduce.12
  330.3 19.0 reduce-scatter.24
  351.7 44.7 reduce-scatter.26
  398.8 37.5 reduce-scatter.22
  439.2 44.7 reduce-scatter.16
where the time goes:
time: 492 us; the launch traced here: 491 us
  waiting for transfers between devices  344 us (70%)
  matrix products  54.7 us (11%)
  local copies, waits for them, and re-layouts  35.8 us (7%)
  other arithmetic  26.3 us (5%)
  between operations  15 us (3%)
  blocking collectives  13.3 us (3%)
    psum x2, waiting for transfers between devices, block_step(): mlp_out, grad_normed = lax.psum((mlp_part, normed_part), 'tp')  135 us
    unnamed x15, waiting for transfers between devices  109 us
    psum x2, waiting for transfers between devices, block_step(): lax.psum(att_grad_part.astype(jnp.bfloat16), 'tp').astype(jnp.float32)  50.5 us
    reduce_scatter x1, waiting for transfers between devices, per_device(): lax.psum_scatter(as_sent(totals), 'seq', scatter_dimension=0, tiled=True)  45.2 us
    unnamed x107, local copies, waits for them, and re-layouts  34.8 us
    all_gather x2, blocking collectives, block_step(): gathered = lax.all_gather(key_value, 'seq', axis=0, tiled=True)  13.3 us
  transfers between devices with their start and end apart: 11, of which 11 were waited for; matrix products, arithmetic and copies ran while one was open for 12% of the time, Pallas kernels for 0%

commit v1 on v0

v1 whole, which is shorter than its diff:
```python
import jax
import jax.numpy as jnp
from jax import lax
from jax.sharding import PartitionSpec as P

HEAD_DIM = 64
BF16 = jnp.bfloat16
F32 = jnp.float32


def swap(shard, axis, by):
    length = lax.axis_size(axis)
    return lax.ppermute(shard, axis, [(i, i ^ by) for i in range(length)])


def shift(shard, axis, by):
    length = lax.axis_size(axis)
    return lax.ppermute(shard, axis, [(i, (i + by) % length) for i in range(length)])


def from_behind(shard, axis, by):
    length = lax.axis_size(axis)
    pairs = [(i, i + by) for i in range(length) if 0 <= i + by < length]
    return lax.ppermute(shard, axis, pairs)


def is_pow2(length):
    return length & (length - 1) == 0


def side(axis, by):
    return (lax.axis_index(axis) // by) % 2 == 1


def sum_rows(part, axis):
    length = lax.axis_size(axis)
    if not is_pow2(length):
        return lax.psum_scatter(part, axis, scatter_dimension=0, tiled=True)
    by = 1
    while by < length:
        half = part.shape[0] // 2
        upper = side(axis, by)
        low, high = part[:half], part[half:]
        got = swap(jnp.where(upper, low, high).astype(BF16), axis, by)
        part = jnp.where(upper, high, low).astype(F32) + got.astype(F32)
        by *= 2
    return part


def own_rows(whole, axis):
    length = lax.axis_size(axis)
    rows = whole.shape[0] // length
    index = lax.axis_index(axis)
    if is_pow2(length):
        place, by = 0, 1
        while by < length:
            place = place * 2 + (index // by) % 2
            by *= 2
    else:
        place = index
    return lax.dynamic_slice_in_dim(whole, place * rows, rows, 0)


def all_rows(shard, axis):
    length = lax.axis_size(axis)
    if not is_pow2(length):
        return lax.all_gather(shard, axis, axis=0, tiled=True)
    by = length // 2
    while by >= 1:
        got = swap(shard, axis, by)
        upper = side(axis, by)
        shard = jnp.concatenate([jnp.where(upper, got, shard), jnp.where(upper, shard, got)], 0)
        by //= 2
    return shard


def sum_all(part, axis):
    return all_rows(sum_rows(part, axis).astype(BF16), axis).astype(F32)


def layer_norm(values, gain):
    centre = values - jnp.mean(values, -1, keepdims=True)
    inv_std = lax.rsqrt(jnp.mean(centre * centre, -1, keepdims=True) + 1e-06)
    unit_vals = centre * inv_std
    return (unit_vals * gain, unit_vals, inv_std)


def norm_back(grad, gain, unit_vals, inv_std):
    scaled = grad * gain
    return inv_std * (
        scaled
        - jnp.mean(scaled, -1, keepdims=True)
        - unit_vals * jnp.mean(scaled * unit_vals, -1, keepdims=True)
    )


def gelu_tanh(values):
    return jax.nn.gelu(values, approximate=True)


def dot(left, right):
    return jnp.dot(left, right, preferred_element_type=F32)


def dot_t(left, right):
    return lax.dot_general(left, right, (((1,), (1,)), ((), ())), preferred_element_type=F32)


def t_dot(left, right):
    return lax.dot_general(left, right, (((0,), (0,)), ((), ())), preferred_element_type=F32)


def mlp_forward(upper, gain, w_up, w_down):
    normed, unit_up, inv_up = layer_norm(upper, gain)
    normed_low = normed.astype(BF16)
    pre = dot(normed_low, w_up)
    hidden = gelu_tanh(pre).astype(BF16)
    return normed_low, unit_up, inv_up, pre, hidden, dot_t(hidden, w_down)


def mlp_backward(grad_lower, pre, w_up, w_down):
    grad_lower_low = grad_lower.astype(BF16)
    grad_hidden = dot(grad_lower_low, w_down)
    pull = jax.vjp(gelu_tanh, pre)[1]
    grad_pre = pull(grad_hidden)[0].astype(BF16)
    return grad_lower_low, grad_pre, dot_t(grad_pre, w_up)


def to_heads(values):
    return values.reshape(values.shape[0], -1, HEAD_DIM)


def gather_seq(shard):
    length = lax.axis_size("seq")
    return jnp.concatenate([shard] + [shift(shard, "seq", -by) for by in range(1, length)], 0)


def attend(query, all_keys, all_values):
    scores = (
        jnp.einsum("qhd,khd->hqk", to_heads(query), to_heads(all_keys), preferred_element_type=F32)
        * 0.125
    )
    top = jnp.max(scores, -1, keepdims=True)
    lse = top + jnp.log(jnp.sum(jnp.exp(scores - top), -1, keepdims=True))
    probs = jnp.exp(scores - lse)
    mixed = jnp.einsum(
        "hqk,khd->qhd", probs.astype(BF16), to_heads(all_values), preferred_element_type=F32
    )
    return probs, mixed.astype(BF16).reshape(query.shape)


def attend_back(query, all_keys, all_values, probs, grad_mixed):
    rows = query.shape[0]
    grad_heads = to_heads(grad_mixed)
    grad_probs = jnp.einsum(
        "qhd,khd->hqk", grad_heads, to_heads(all_values), preferred_element_type=F32
    )
    delta = jnp.sum(probs * grad_probs, -1, keepdims=True)
    grad_scores = (probs * (grad_probs - delta)).astype(BF16)
    grad_query = 0.125 * jnp.einsum(
        "hqk,khd->qhd", grad_scores, to_heads(all_keys), preferred_element_type=F32
    )
    grad_keys = 0.125 * jnp.einsum(
        "hqk,qhd->khd", grad_scores, to_heads(query), preferred_element_type=F32
    )
    grad_values = jnp.einsum(
        "hqk,qhd->khd", probs.astype(BF16), grad_heads, preferred_element_type=F32
    )
    kv_grad = jnp.concatenate(
        [grad_keys.reshape(-1, query.shape[1]), grad_values.reshape(-1, query.shape[1])], 1
    )
    own = kv_grad[:rows]
    for by in range(1, lax.axis_size("seq")):
        other = kv_grad[by * rows : (by + 1) * rows].astype(BF16)
        own = own + shift(other, "seq", by).astype(F32)
    return jnp.concatenate([grad_query.astype(BF16).reshape(query.shape), own.astype(BF16)], 1)


def send_factors(pairs):
    length = lax.axis_size("seq")
    place = lax.axis_index("seq")
    width = pairs[0][0].shape[1] // length

    def cut(whole, index):
        return lax.dynamic_slice_in_dim(whole, index * width, width, 1)

    lefts = [[cut(left, place)] for left, unused in pairs]
    rights = [[right] for unused, right in pairs]
    for by in range(1, length):
        target = (place + by) % length
        packed = jnp.concatenate(
            [cut(left, target) for left, unused in pairs] + [right for unused, right in pairs], 1
        )
        got = shift(packed, "seq", by)
        at = 0
        for number in range(len(pairs)):
            lefts[number].append(got[:, at : at + width])
            at += width
        for number, (unused, right) in enumerate(pairs):
            rights[number].append(got[:, at : at + right.shape[1]])
            at += right.shape[1]
    return list(zip(lefts, rights))


def per_device(streams, head_streams, gains, w_qkv, w_out, w_up, w_down):
    gain_att, gain_mlp = gains[0, 0], gains[0, 1]
    width, local = w_qkv.shape[1], w_qkv.shape[3]
    w_flat = w_qkv[0].reshape(width, 3 * local)
    w_out, w_up, w_down = w_out[0], w_up[0], w_down[0]
    is_last = lax.axis_index("section") == lax.axis_size("section") - 1

    def back_a_block(shard):
        return from_behind(shard.astype(BF16), "section", -1)

    upper, lower, grad_upper, grad_lower = (streams[0, i] for i in range(4))
    mlp_terms, att_terms = [], []
    for tick in range(2):
        normed_low, unit_up, inv_up, pre, hidden, mlp_part = mlp_forward(
            upper, gain_mlp, w_up, w_down
        )
        mlp_out = sum_all(mlp_part, "tp")
        grad_lower_low, grad_pre, normed_part = mlp_backward(grad_lower, pre, w_up, w_down)
        grad_normed = sum_all(normed_part, "tp")
        mlp_terms.append(send_factors([(normed_low, grad_pre), (grad_lower_low, hidden)]))

        lower_in = lower - mlp_out
        normed_att, unit_att, inv_att = layer_norm(lower_in, gain_att)
        att_low = normed_att.astype(BF16)
        projected = dot(att_low, w_flat).astype(BF16)
        query = projected[:, :local]
        gathered = gather_seq(projected[:, local:])
        all_keys, all_values = gathered[:, :local], gathered[:, local:]
        probs, mixed = attend(query, all_keys, all_values)
        att_part = dot_t(mixed, w_out)

        upper_total = grad_upper + norm_back(grad_normed, gain_mlp, unit_up, inv_up)
        total_low = upper_total.astype(BF16)
        grad_mixed = dot(total_low, w_out).astype(BF16)
        grad_proj = attend_back(query, all_keys, all_values, probs, grad_mixed)
        att_grad_part = dot_t(grad_proj, w_flat)
        att_terms.append(send_factors([(att_low, grad_proj), (total_low, mixed)]))

        if tick == 0:
            next_lower = jnp.where(is_last, head_streams[1], back_a_block(lower_in).astype(F32))
            next_grad_upper = jnp.where(
                is_last, head_streams[2], back_a_block(upper_total).astype(F32)
            )
            upper_rows = own_rows(upper, "tp") - sum_rows(att_part, "tp")
            next_upper = all_rows(back_a_block(upper_rows), "tp").astype(F32)
            grad_rows = own_rows(grad_lower, "tp") + norm_back(
                sum_rows(att_grad_part, "tp"),
                gain_att,
                own_rows(unit_att, "tp"),
                own_rows(inv_att, "tp"),
            )
            next_grad_lower = all_rows(back_a_block(grad_rows), "tp").astype(F32)
            upper = jnp.where(is_last, head_streams[0], next_upper)
            grad_lower = jnp.where(is_last, head_streams[3], next_grad_lower)
            lower, grad_upper = next_lower, next_grad_upper

    upper_in = upper - sum_all(att_part, "tp")
    grad_att = sum_all(att_grad_part, "tp")
    grad_lower_in = grad_lower + norm_back(grad_att, gain_att, unit_att, inv_att)
    recon = jnp.stack([upper_in, lower_in, upper_total, grad_lower_in])[None]

    def weight_grad(terms, number):
        left = jnp.concatenate([part for tick in terms for part in tick[number][0]], 0)
        right = jnp.concatenate([part for tick in terms for part in tick[number][1]], 0)
        return t_dot(left, right).astype(BF16)

    return (
        recon,
        weight_grad(att_terms, 0).reshape(-1, 3, local)[None],
        weight_grad(att_terms, 1)[None],
        weight_grad(mlp_terms, 0)[None],
        weight_grad(mlp_terms, 1)[None],
    )


def solution(mesh):
    placed = (
        P("section", None, "seq", None),
        P(None, "seq", None),
        P("section", None, None),
        P("section", None, None, "tp"),
        P("section", None, "tp"),
        P("section", None, "tp"),
        P("section", None, "tp"),
    )
    return jax.shard_map(
        per_device,
        mesh=mesh,
        in_specs=placed,
        out_specs=(
            P("section", None, "seq", None),
            P("section", "seq", None, "tp"),
            P("section", "seq", "tp"),
            P("section", "seq", "tp"),
            P("section", "seq", "tp"),
        ),
        check_vma=False,
    )
```

time: 492 us -> 248 us (0.50)
  waiting for transfers between devices: 344 us -> 61.1 us
  starting transfers between devices: 2.1 us -> 63 us
  matrix products: 54.7 us -> 35.2 us
  other arithmetic: 26.3 us -> 42 us
  blocking collectives: 13.3 us -> 0 us
  between operations: 15 us -> 2.22 us
  local copies, waits for them, and re-layouts: 35.8 us -> 43.1 us
    psum x4 -> x0, waiting for transfers between devices: 186 us -> none  [the longest x2 135 us: block_step(): mlp_out, grad_normed = lax.psum((mlp_part, normed_part), 'tp')]
    unnamed x15 -> x0, waiting for transfers between devices: 109 us -> none
    ppermute x0 -> x40, waiting for transfers between devices: none -> 61.1 us  [the longest x32 56 us: swap(): return lax.ppermute(shard, axis, [(i, i ^ by) for i in range(length)])]
    ppermute x0 -> x40, starting transfers between devices: none -> 57.7 us  [the longest x32 48.9 us: swap(): return lax.ppermute(shard, axis, [(i, i ^ by) for i in range(length)])]
    reduce_scatter x1 -> x0, waiting for transfers between devices: 45.2 us -> none  [per_device(): lax.psum_scatter(as_sent(totals), 'seq', scatter_dimension=0, tiled=True)]
    unnamed x107 -> x152, local copies, waits for them, and re-layouts: 34.8 us -> 6.8 us
    dot_general x36 -> x32, matrix products: 54.7 us -> 35.2 us  [the longest x8 8.3 us: dot(): return jnp.dot(left, right, preferred_element_type=F32)]
    convert_element_type x2 -> x32, other arithmetic: 0.47 us -> 17.3 us  [the longest x16 4.92 us: sum_rows(): got = swap(jnp.where(upper, low, high).astype(BF16), axis, by)]
  transfers between devices with their start and end apart: 11 -> 44, of which waited for: 11 -> 24; matrix products, arithmetic and copies ran while one was open for 12% -> 39% of each run, Pallas kernels for 0% -> 0%
where the time goes in v1:
time: 248 us; the launch traced here: 247 us
  starting transfers between devices  63 us (25%)
  waiting for transfers between devices  61.1 us (25%)
  local copies, waits for them, and re-layouts  43.1 us (17%)
  other arithmetic  42 us (17%)
  matrix products  35.2 us (14%)
    ppermute x32, waiting for transfers between devices, swap(): return lax.ppermute(shard, axis, [(i, i ^ by) for i in range(length)])  56 us
    ppermute x32, starting transfers between devices, swap(): return lax.ppermute(shard, axis, [(i, i ^ by) for i in range(length)])  48.9 us
    ppermute x8, starting transfers between devices, shift(): lax.ppermute(shard, axis, [(i, (i + by) % length) for i in range(length)])  8.74 us
    dot_general x8, matrix products, dot(): return jnp.dot(left, right, preferred_element_type=F32)  8.3 us
    dot_general x4, matrix products, t_dot(): lax.dot_general(left, right, (((0,), (0,)), ((), ())), preferred_element_...  8.07 us
    dynamic_slice x8, local copies, waits for them, and re-layouts, cut(): return lax.dynamic_slice_in_dim(whole, index * width, width, 1)  7.97 us
    dot_general x8, matrix products, dot_t(): lax.dot_general(left, right, (((1,), (1,)), ((), ())), preferred_element_...  7.43 us
    unnamed x152, local copies, waits for them, and re-layouts  6.8 us
  transfers between devices with their start and end apart: 44, of which 24 were waited for; matrix products, arithmetic and copies ran while one was open for 39% of the time, Pallas kernels for 0%

profile of v1, /device:TPU:0, one launch (start us, length us, event | category | flops | bytes accessed | tf_op | source)
XLA Modules:
  0.0 246.6 jit_solution(4918658444253593851)
XLA Ops:
  1.6 2.5 %fusion.188 = (f32[1,1,128,1280]{3,2,1,0:T(8,128)}, f32[128]{0:T(128)S(1)}, f32[1,1,128,1280]{3,2,1,0:T(8,128)}) fusion(f32[1,4,128,1280]{3,2,1,0:T(8,128)} %param.7), kind=kLoop, calls=%fused_computation.369 | loop fusion | flops 163712 | bytes 2621952 | tf_op jit(solution)/shard_map/slice | solution.py:215
  9.5 3.0 %collective-permute-start = (bf16[64,1280]{1,0:T(8,128)(2,1)}, bf16[64,1280]{1,0:T(8,128)(2,1)}, u32[]{:S(2)}, u32[]{:S(2)}) collective-permute-start(bf16[64,1280]{1,0:T(8,128)(2,1)} %select_convert_fusion.8), channel_id=1, source_target_pairs={{0,1},{1,0},{2,3},{3,2},{4,5},{5,4},{6,7},{7,6},{8,9},{9,8},{10,11... | collective-permute-start | bytes 491528 | tf_op jit(solution)/shard_map/ppermute | solution.py:13
  21.6 3.0 %collective-permute-start.1 = (bf16[32,1280]{1,0:T(8,128)(2,1)S(1)}, bf16[32,1280]{1,0:T(8,128)(2,1)S(1)}, u32[]{:S(2)}, u32[]{:S(2)}) collective-permute-start(bf16[32,1280]{1,0:T(8,128)(2,1)S(1)} %select_convert_fusion.16), channel_id=1, source_target_pairs={{0,2},{1,3},{2,0},{3,1},{4,6},{5,7},{6,4},{7,5},{8,10},{9,11},{10,... | collective-permute-start | bytes 245768 | tf_op jit(solution)/shard_map/ppermute | solution.py:13
  27.6 2.9 %collective-permute-start.2 = (bf16[32,1280]{1,0:T(8,128)(2,1)S(1)}, bf16[32,1280]{1,0:T(8,128)(2,1)S(1)}, u32[]{:S(2)}, u32[]{:S(2)}) collective-permute-start(bf16[32,1280]{1,0:T(8,128)(2,1)S(1)} %add_convert_fusion.7), channel_id=1, source_target_pairs={{0,2},{1,3},{2,0},{3,1},{4,6},{5,7},{6,4},{7,5},{8,10},{9,11},{10,... | collective-permute-start | bytes 245768 | tf_op jit(solution)/shard_map/ppermute | solution.py:13
  33.8 5.1 %collective-permute-start.3 = (bf16[64,1280]{1,0:T(8,128)(2,1)S(1)}, bf16[64,1280]{1,0:T(8,128)(2,1)S(1)}, u32[]{:S(2)}, u32[]{:S(2)}) collective-permute-start(bf16[64,1280]{1,0:T(8,128)(2,1)S(1)} %pad_maximum_fusion.12), channel_id=1, source_target_pairs={{0,1},{1,0},{2,3},{3,2},{4,5},{5,4},{6,7},{7,6},{8,9},{9,8},{10,11... | collective-permute-start | bytes 491528 | tf_op jit(solution)/shard_map/ppermute | solution.py:13
  41.4 2.7 %collective-permute-done.3 = bf16[64,1280]{1,0:T(8,128)(2,1)S(1)} collective-permute-done((bf16[64,1280]{1,0:T(8,128)(2,1)S(1)}, bf16[64,1280]{1,0:T(8,128)(2,1)S(1)}, u32[]{:S(2)}, u32[]{:S(2)}) %collective-permute-start.3) | collective-permute-done | bytes 163872 | tf_op jit(solution)/shard_map/ppermute | solution.py:13
  76.0 3.5 %collective-permute-start.6 = (bf16[32,1280]{1,0:T(8,128)(2,1)S(1)}, bf16[32,1280]{1,0:T(8,128)(2,1)S(1)}, u32[]{:S(2)}, u32[]{:S(2)}) collective-permute-start(bf16[32,1280]{1,0:T(8,128)(2,1)S(1)} %select_convert_fusion.15), channel_id=1, source_target_pairs={{0,2},{1,3},{2,0},{3,1},{4,6},{5,7},{6,4},{7,5},{8,10},{9,11},{10,... | collective-permute-start | bytes 245768 | tf_op jit(solution)/shard_map/ppermute | solution.py:13
  79.5 3.7 %collective-permute-done.25 = bf16[128,640]{1,0:T(8,128)(2,1)} collective-permute-done((bf16[128,640]{1,0:T(8,128)(2,1)}, bf16[128,640]{1,0:T(8,128)(2,1)}, u32[]{:S(2)}, u32[]{:S(2)}) %collective-permute-start.25) | collective-permute-done | bytes 163872 | tf_op jit(solution)/shard_map/ppermute | solution.py:18
  89.2 2.8 %collective-permute-done.26 = bf16[64,1280]{1,0:T(8,128)(2,1)S(1)} collective-permute-done((bf16[64,1280]{1,0:T(8,128)(2,1)S(1)}, bf16[64,1280]{1,0:T(8,128)(2,1)S(1)}, u32[]{:S(2)}, u32[]{:S(2)}) %collective-permute-start.26) | collective-permute-done | bytes 163872 | tf_op jit(solution)/shard_map/ppermute | solution.py:13
  92.1 3.3 %collective-permute-start.27 = (bf16[32,1280]{1,0:T(8,128)(2,1)S(1)}, bf16[32,1280]{1,0:T(8,128)(2,1)S(1)}, u32[]{:S(2)}, u32[]{:S(2)}) collective-permute-start(bf16[32,1280]{1,0:T(8,128)(2,1)S(1)} %select_convert_fusion.11), channel_id=1, source_target_pairs={{0,2},{1,3},{2,0},{3,1},{4,6},{5,7},{6,4},{7,5},{8,10},{9,11},{10,... | collective-permute-start | bytes 245768 | tf_op jit(solution)/shard_map/ppermute | solution.py:13
  97.2 2.6 %collective-permute-done.27 = bf16[32,1280]{1,0:T(8,128)(2,1)S(1)} collective-permute-done((bf16[32,1280]{1,0:T(8,128)(2,1)S(1)}, bf16[32,1280]{1,0:T(8,128)(2,1)S(1)}, u32[]{:S(2)}, u32[]{:S(2)}) %collective-permute-start.27) | collective-permute-done | bytes 81952 | tf_op jit(solution)/shard_map/ppermute | solution.py:13
  100.0 4.0 %collective-permute-done.8 = bf16[32,1280]{1,0:T(8,128)(2,1)S(1)} collective-permute-done((bf16[32,1280]{1,0:T(8,128)(2,1)S(1)}, bf16[32,1280]{1,0:T(8,128)(2,1)S(1)}, u32[]{:S(2)}, u32[]{:S(2)}) %collective-permute-start.8) | collective-permute-done | bytes 81952 | tf_op jit(solution)/shard_map/ppermute | solution.py:13
  113.2 3.1 %collective-permute-start.29 = (bf16[32,1280]{1,0:T(8,128)(2,1)}, bf16[32,1280]{1,0:T(8,128)(2,1)S(1)}, u32[]{:S(2)}, u32[]{:S(2)}) collective-permute-start(bf16[32,1280]{1,0:T(8,128)(2,1)} %collective-permute-done.28), channel_id=1, source_target_pairs={{0,2},{1,3},{2,0},{3,1},{4,6},{5,7},{6,4},{7,5},{8,10},{9,11},{10,... | collective-permute-start | bytes 245768 | tf_op jit(solution)/shard_map/ppermute | solution.py:13
  119.0 2.4 collective-permute-done.29
  125.7 2.9 %collective-permute-done.30 = bf16[64,1280]{1,0:T(8,128)(2,1)S(1)} collective-permute-done((bf16[64,1280]{1,0:T(8,128)(2,1)S(1)}, bf16[64,1280]{1,0:T(8,128)(2,1)S(1)}, u32[]{:S(2)}, u32[]{:S(2)}) %collective-permute-start.30) | collective-permute-done | bytes 163872 | tf_op jit(solution)/shard_map/ppermute | solution.py:13
  147.8 6.9 %collective-permute-done.32 = bf16[32,1280]{1,0:T(8,128)(2,1)S(1)} collective-permute-done((bf16[32,1280]{1,0:T(8,128)(2,1)S(1)}, bf16[32,1280]{1,0:T(8,128)(2,1)S(1)}, u32[]{:S(2)}, u32[]{:S(2)}) %collective-permute-start.32) | collective-permute-done | bytes 81952 | tf_op jit(solution)/shard_map/ppermute | solution.py:13
  156.7 3.5 %collective-permute-done.33 = bf16[32,1280]{1,0:T(8,128)(2,1)S(1)} collective-permute-done((bf16[32,1280]{1,0:T(8,128)(2,1)S(1)}, bf16[32,1280]{1,0:T(8,128)(2,1)S(1)}, u32[]{:S(2)}, u32[]{:S(2)}) %collective-permute-start.33) | collective-permute-done | bytes 81952 | tf_op jit(solution)/shard_map/ppermute | solution.py:13
  161.8 3.9 %collective-permute-done.34 = bf16[64,1280]{1,0:T(8,128)(2,1)S(1)} collective-permute-done((bf16[64,1280]{1,0:T(8,128)(2,1)S(1)}, bf16[64,1280]{1,0:T(8,128)(2,1)S(1)}, u32[]{:S(2)}, u32[]{:S(2)}) %collective-permute-start.34) | collective-permute-done | bytes 163872 | tf_op jit(solution)/shard_map/ppermute | solution.py:13
  166.1 2.5 %fusion.183 = (bf16[128,1280]{1,0:T(8,128)(2,1)S(1)}, f32[128,1280]{1,0:T(8,128)}, f32[128]{0:T(128)S(1)}, f32[128,1280]{1,0:T(8,128)S(1)}) fusion(f32[128]{0:T(128)S(1)} %broadcast_multiply_fusion.4, f32[128,1280]{1,0:T(8,128)S(1)} %get-tuple-element.24, f32[128]{0:T(128)S(1)} %broadcast_multiply_fusion.9, f32[128]{0:T(128)S(1)} %broadcast_multiply_fusion.5, ...), kind=kLoop, calls=%fused_computation.366 | loop fusion | flops 3768192 | bytes 4922881 | tf_op jit(solution)/shard_map/convert_element_type | solution.py:237
  200.2 3.5 %collective-permute-done.16 = bf16[64,1280]{1,0:T(8,128)(2,1)} collective-permute-done((bf16[64,1280]{1,0:T(8,128)(2,1)}, bf16[64,1280]{1,0:T(8,128)(2,1)}, u32[]{:S(2)}, u32[]{:S(2)}) %collective-permute-start.16) | collective-permute-done | bytes 163872 | tf_op jit(solution)/shard_map/ppermute | solution.py:13
  222.4 2.7 %collective-permute-start.38 = (bf16[32,1280]{1,0:T(8,128)(2,1)S(1)}, bf16[32,1280]{1,0:T(8,128)(2,1)S(1)}, u32[]{:S(2)}, u32[]{:S(2)}) collective-permute-start(bf16[32,1280]{1,0:T(8,128)(2,1)S(1)} %add_convert_fusion.2), channel_id=1, source_target_pairs={{0,2},{1,3},{2,0},{3,1},{4,6},{5,7},{6,4},{7,5},{8,10},{9,11},{10,... | collective-permute-start | bytes 245768 | tf_op jit(solution)/shard_map/ppermute | solution.py:13
  225.2 2.6 %collective-permute-done.38 = bf16[32,1280]{1,0:T(8,128)(2,1)S(1)} collective-permute-done((bf16[32,1280]{1,0:T(8,128)(2,1)S(1)}, bf16[32,1280]{1,0:T(8,128)(2,1)S(1)}, u32[]{:S(2)}, u32[]{:S(2)}) %collective-permute-start.38) | collective-permute-done | bytes 81952 | tf_op jit(solution)/shard_map/ppermute | solution.py:13
  230.7 2.6 %collective-permute-done.39 = bf16[64,1280]{1,0:T(8,128)(2,1)S(1)} collective-permute-done((bf16[64,1280]{1,0:T(8,128)(2,1)S(1)}, bf16[64,1280]{1,0:T(8,128)(2,1)S(1)}, u32[]{:S(2)}, u32[]{:S(2)}) %collective-permute-start.39) | collective-permute-done | bytes 163872 | tf_op jit(solution)/shard_map/ppermute | solution.py:13
  242.8 2.4 convolution_convert_fusion.2
  (386 shorter events, 166.3 us)
Async XLA Ops:
  9.5 10.9 %collective-permute-start = (bf16[64,1280]{1,0:T(8,128)(2,1)}, bf16[64,1280]{1,0:T(8,128)(2,1)}, u32[]{:S(2)}, u32[]{:S(2)}) collective-permute-start(bf16[64,1280]{1,0:T(8,128)(2,1)} %select_convert_fusion.8), channel_id=1, source_target_pairs={{0,1},{1,0},{2,3},{3,2},{4,5},{5,4},{6,7},{7,6},{8,9},{9,8},{10,11... | collective-permute-start | bytes 491528 | tf_op jit(solution)/shard_map/ppermute | solution.py:13
  16.6 8.0 %collective-permute-start.20 = (bf16[64,1280]{1,0:T(8,128)(2,1)S(1)}, bf16[64,1280]{1,0:T(8,128)(2,1)}, u32[]{:S(2)}, u32[]{:S(2)}) collective-permute-start(bf16[64,1280]{1,0:T(8,128)(2,1)S(1)} %select_convert_fusion.4), channel_id=1, source_target_pairs={{0,1},{1,0},{2,3},{3,2},{4,5},{5,4},{6,7},{7,6},{8,9},{9,8},{10,11... | collective-permute-start | bytes 491528 | tf_op jit(solution)/shard_map/ppermute | solution.py:13
  25.7 7.2 %collective-permute-start.21 = (bf16[32,1280]{1,0:T(8,128)(2,1)S(1)}, bf16[32,1280]{1,0:T(8,128)(2,1)S(1)}, u32[]{:S(2)}, u32[]{:S(2)}) collective-permute-start(bf16[32,1280]{1,0:T(8,128)(2,1)S(1)} %select_convert_fusion.12), channel_id=1, source_target_pairs={{0,2},{1,3},{2,0},{3,1},{4,6},{5,7},{6,4},{7,5},{8,10},{9,11},{10,... | collective-permute-start | bytes 245768 | tf_op jit(solution)/shard_map/ppermute | solution.py:13
  33.8 10.2 %collective-permute-start.3 = (bf16[64,1280]{1,0:T(8,128)(2,1)S(1)}, bf16[64,1280]{1,0:T(8,128)(2,1)S(1)}, u32[]{:S(2)}, u32[]{:S(2)}) collective-permute-start(bf16[64,1280]{1,0:T(8,128)(2,1)S(1)} %pad_maximum_fusion.12), channel_id=1, source_target_pairs={{0,1},{1,0},{2,3},{3,2},{4,5},{5,4},{6,7},{7,6},{8,9},{9,8},{10,11... | collective-permute-start | bytes 491528 | tf_op jit(solution)/shard_map/ppermute | solution.py:13
  39.0 7.0 %collective-permute-start.23 = (bf16[64,1280]{1,0:T(8,128)(2,1)S(1)}, bf16[64,1280]{1,0:T(8,128)(2,1)S(1)}, u32[]{:S(2)}, u32[]{:S(2)}) collective-permute-start(bf16[64,1280]{1,0:T(8,128)(2,1)S(1)} %pad_maximum_fusion.16), channel_id=1, source_target_pairs={{0,1},{1,0},{2,3},{3,2},{4,5},{5,4},{6,7},{7,6},{8,9},{9,8},{10,11... | collective-permute-start | bytes 491528 | tf_op jit(solution)/shard_map/ppermute | solution.py:13
  47.5 9.2 %collective-permute-start.4 = (bf16[128,640]{0,1:T(8,128)(2,1)S(1)}, bf16[128,640]{0,1:T(8,128)(2,1)S(1)}, u32[]{:S(2)}, u32[]{:S(2)}) collective-permute-start(bf16[128,640]{0,1:T(8,128)(2,1)S(1)} %slice.286), channel_id=1, source_target_pairs={{0,4},{4,0},{1,5},{5,1},{2,6},{6,2},{3,7},{7,3},{8,12},{12,8},{9,1... | collective-permute-start | bytes 491528 | tf_op jit(solution)/shard_map/ppermute | solution.py:18
  51.2 114.8 %collective-permute-start.24 = (bf16[128,1280]{1,0:T(8,128)(2,1)}, bf16[128,1280]{1,0:T(8,128)(2,1)}, u32[]{:S(2)}, u32[]{:S(2)}) collective-permute-start(bf16[128,1280]{1,0:T(8,128)(2,1)} %get-tuple-element.29), channel_id=1, source_target_pairs={{8,0},{16,8},{24,16},{9,1},{17,9},{25,17},{10,2},{18,10},{26,18},{... | collective-permute-start | bytes 983048 | tf_op jit(solution)/shard_map/ppermute | solution.py:24
  52.5 113.5 %collective-permute-start.10 = (bf16[128,1280]{1,0:T(8,128)(2,1)}, bf16[128,1280]{1,0:T(8,128)(2,1)}, u32[]{:S(2)}, u32[]{:S(2)}) collective-permute-start(bf16[128,1280]{1,0:T(8,128)(2,1)} %get-tuple-element.25), channel_id=1, source_target_pairs={{8,0},{16,8},{24,16},{9,1},{17,9},{25,17},{10,2},{18,10},{26,18},{... | collective-permute-start | bytes 983048 | tf_op jit(solution)/shard_map/ppermute | solution.py:24
  55.6 87.5 %collective-permute-start.42 = (bf16[128,3840]{1,0:T(8,128)(2,1)}, bf16[128,3840]{1,0:T(8,128)(2,1)}, u32[]{:S(2)}, u32[]{:S(2)}) collective-permute-start(bf16[128,3840]{1,0:T(8,128)(2,1)} %pad_maximum_fusion), channel_id=1, source_target_pairs={{0,4},{4,0},{1,5},{5,1},{2,6},{6,2},{3,7},{7,3},{8,12},{12,8},{9,1... | collective-permute-start | bytes 2949128 | tf_op jit(solution)/shard_map/ppermute | solution.py:18
  61.0 13.6 %collective-permute-start.5 = (bf16[64,1280]{1,0:T(8,128)(2,1)}, bf16[64,1280]{1,0:T(8,128)(2,1)}, u32[]{:S(2)}, u32[]{:S(2)}) collective-permute-start(bf16[64,1280]{1,0:T(8,128)(2,1)} %select_convert_fusion.7), channel_id=1, source_target_pairs={{0,1},{1,0},{2,3},{3,2},{4,5},{5,4},{6,7},{7,6},{8,9},{9,8},{10,11... | collective-permute-start | bytes 491528 | tf_op jit(solution)/shard_map/ppermute | solution.py:13
  70.3 13.0 %collective-permute-start.25 = (bf16[128,640]{1,0:T(8,128)(2,1)}, bf16[128,640]{1,0:T(8,128)(2,1)}, u32[]{:S(2)}, u32[]{:S(2)}) collective-permute-start(bf16[128,640]{1,0:T(8,128)(2,1)} %fusion.130), channel_id=1, source_target_pairs={{0,4},{4,0},{1,5},{5,1},{2,6},{6,2},{3,7},{7,3},{8,12},{12,8},{9,1... | collective-permute-start | bytes 491528 | tf_op jit(solution)/shard_map/ppermute | solution.py:18
  76.0 10.9 %collective-permute-start.6 = (bf16[32,1280]{1,0:T(8,128)(2,1)S(1)}, bf16[32,1280]{1,0:T(8,128)(2,1)S(1)}, u32[]{:S(2)}, u32[]{:S(2)}) collective-permute-start(bf16[32,1280]{1,0:T(8,128)(2,1)S(1)} %select_convert_fusion.15), channel_id=1, source_target_pairs={{0,2},{1,3},{2,0},{3,1},{4,6},{5,7},{6,4},{7,5},{8,10},{9,11},{10,... | collective-permute-start | bytes 245768 | tf_op jit(solution)/shard_map/ppermute | solution.py:13
  87.9 9.3 %collective-permute-start.7 = (bf16[32,1280]{1,0:T(8,128)(2,1)S(1)}, bf16[32,1280]{1,0:T(8,128)(2,1)S(1)}, u32[]{:S(2)}, u32[]{:S(2)}) collective-permute-start(bf16[32,1280]{1,0:T(8,128)(2,1)S(1)} %fusion.161), channel_id=1, source_target_pairs={{8,0},{16,8},{24,16},{9,1},{17,9},{25,17},{10,2},{18,10},{26,18},{... | collective-permute-start | bytes 245768 | tf_op jit(solution)/shard_map/ppermute | solution.py:24
  92.1 7.7 %collective-permute-start.27 = (bf16[32,1280]{1,0:T(8,128)(2,1)S(1)}, bf16[32,1280]{1,0:T(8,128)(2,1)S(1)}, u32[]{:S(2)}, u32[]{:S(2)}) collective-permute-start(bf16[32,1280]{1,0:T(8,128)(2,1)S(1)} %select_convert_fusion.11), channel_id=1, source_target_pairs={{0,2},{1,3},{2,0},{3,1},{4,6},{5,7},{6,4},{7,5},{8,10},{9,11},{10,... | collective-permute-start | bytes 245768 | tf_op jit(solution)/shard_map/ppermute | solution.py:13
  104.8 8.4 %collective-permute-start.9 = (bf16[64,1280]{1,0:T(8,128)(2,1)}, bf16[64,1280]{1,0:T(8,128)(2,1)}, u32[]{:S(2)}, u32[]{:S(2)}) collective-permute-start(bf16[64,1280]{1,0:T(8,128)(2,1)} %pad_maximum_fusion.13), channel_id=1, source_target_pairs={{0,1},{1,0},{2,3},{3,2},{4,5},{5,4},{6,7},{7,6},{8,9},{9,8},{10,11... | collective-permute-start | bytes 491528 | tf_op jit(solution)/shard_map/ppermute | solution.py:13
  112.6 22.8 %collective-permute-start.40 = (bf16[128,2560]{1,0:T(8,128)(2,1)}, bf16[128,2560]{1,0:T(8,128)(2,1)S(1)}, u32[]{:S(2)}, u32[]{:S(2)}) collective-permute-start(bf16[128,2560]{1,0:T(8,128)(2,1)} %concatenate.204), channel_id=1, source_target_pairs={{0,4},{4,0},{1,5},{5,1},{2,6},{6,2},{3,7},{7,3},{8,12},{12,8},{9,1... | collective-permute-start | bytes 1966088 | tf_op jit(solution)/shard_map/ppermute | solution.py:18
  113.2 8.2 %collective-permute-start.29 = (bf16[32,1280]{1,0:T(8,128)(2,1)}, bf16[32,1280]{1,0:T(8,128)(2,1)S(1)}, u32[]{:S(2)}, u32[]{:S(2)}) collective-permute-start(bf16[32,1280]{1,0:T(8,128)(2,1)} %collective-permute-done.28), channel_id=1, source_target_pairs={{0,2},{1,3},{2,0},{3,1},{4,6},{5,7},{6,4},{7,5},{8,10},{9,11},{10,... | collective-permute-start | bytes 245768 | tf_op jit(solution)/shard_map/ppermute | solution.py:13
  134.0 12.8 %collective-permute-start.31 = (bf16[64,1280]{1,0:T(8,128)(2,1)S(1)}, bf16[64,1280]{1,0:T(8,128)(2,1)S(1)}, u32[]{:S(2)}, u32[]{:S(2)}) collective-permute-start(bf16[64,1280]{1,0:T(8,128)(2,1)S(1)} %select_convert_fusion.2), channel_id=1, source_target_pairs={{0,1},{1,0},{2,3},{3,2},{4,5},{5,4},{6,7},{7,6},{8,9},{9,8},{10,11... | collective-permute-start | bytes 491528 | tf_op jit(solution)/shard_map/ppermute | solution.py:13
  146.9 7.7 %collective-permute-start.32 = (bf16[32,1280]{1,0:T(8,128)(2,1)S(1)}, bf16[32,1280]{1,0:T(8,128)(2,1)S(1)}, u32[]{:S(2)}, u32[]{:S(2)}) collective-permute-start(bf16[32,1280]{1,0:T(8,128)(2,1)S(1)} %select_convert_fusion.10), channel_id=1, source_target_pairs={{0,2},{1,3},{2,0},{3,1},{4,6},{5,7},{6,4},{7,5},{8,10},{9,11},{10,... | collective-permute-start | bytes 245768 | tf_op jit(solution)/shard_map/ppermute | solution.py:13
  169.8 7.2 %collective-permute-start.15 = (bf16[128,640]{0,1:T(8,128)(2,1)S(1)}, bf16[128,640]{0,1:T(8,128)(2,1)S(1)}, u32[]{:S(2)}, u32[]{:S(2)}) collective-permute-start(bf16[128,640]{0,1:T(8,128)(2,1)S(1)} %slice.298), channel_id=1, source_target_pairs={{0,4},{4,0},{1,5},{5,1},{2,6},{6,2},{3,7},{7,3},{8,12},{12,8},{9,1... | collective-permute-start | bytes 491528 | tf_op jit(solution)/shard_map/ppermute | solution.py:18
  174.3 61.4 %collective-permute-start.43 = (bf16[128,3840]{1,0:T(8,128)(2,1)}, bf16[128,3840]{1,0:T(8,128)(2,1)}, u32[]{:S(2)}, u32[]{:S(2)}) collective-permute-start(bf16[128,3840]{1,0:T(8,128)(2,1)} %pad_maximum_fusion.1), channel_id=1, source_target_pairs={{0,4},{4,0},{1,5},{5,1},{2,6},{6,2},{3,7},{7,3},{8,12},{12,8},{9,1... | collective-permute-start | bytes 2949128 | tf_op jit(solution)/shard_map/ppermute | solution.py:18
  193.4 12.2 %collective-permute-start.35 = (bf16[128,640]{1,0:T(8,128)(2,1)}, bf16[128,640]{1,0:T(8,128)(2,1)}, u32[]{:S(2)}, u32[]{:S(2)}) collective-permute-start(bf16[128,640]{1,0:T(8,128)(2,1)} %fusion.129), channel_id=1, source_target_pairs={{0,4},{4,0},{1,5},{5,1},{2,6},{6,2},{3,7},{7,3},{8,12},{12,8},{9,1... | collective-permute-start | bytes 491528 | tf_op jit(solution)/shard_map/ppermute | solution.py:18
  205.6 7.3 %collective-permute-start.17 = (bf16[32,1280]{1,0:T(8,128)(2,1)}, bf16[32,1280]{1,0:T(8,128)(2,1)}, u32[]{:S(2)}, u32[]{:S(2)}) collective-permute-start(bf16[32,1280]{1,0:T(8,128)(2,1)} %select_convert_fusion.13), channel_id=1, source_target_pairs={{0,2},{1,3},{2,0},{3,1},{4,6},{5,7},{6,4},{7,5},{8,10},{9,11},{10,... | collective-permute-start | bytes 245768 | tf_op jit(solution)/shard_map/ppermute | solution.py:13
  212.1 30.4 %collective-permute-start.41 = (bf16[128,2560]{1,0:T(8,128)(2,1)}, bf16[128,2560]{1,0:T(8,128)(2,1)S(1)}, u32[]{:S(2)}, u32[]{:S(2)}) collective-permute-start(bf16[128,2560]{1,0:T(8,128)(2,1)} %concatenate.205), channel_id=1, source_target_pairs={{0,4},{4,0},{1,5},{5,1},{2,6},{6,2},{3,7},{7,3},{8,12},{12,8},{9,1... | collective-permute-start | bytes 1966088 | tf_op jit(solution)/shard_map/ppermute | solution.py:18
  (97 other events, 645.1 us)

commit v2 on v0

v2 whole, which is shorter than its diff:
```python
import functools

import jax
import jax.numpy as jnp
from jax import lax
from jax.experimental import pallas as pl
from jax.experimental.pallas import tpu as pltpu
from jax.sharding import PartitionSpec as P

HEAD_DIM = 64
BF16 = jnp.bfloat16
F32 = jnp.float32
LIMIT = 24 * 1024 * 1024
CHUNKS = 4
BLOCK = 256
GELU_SCALE = 0.7978845608028654
GELU_CUBE = 0.044715


def swap(shard, axis, by):
    length = lax.axis_size(axis)
    return lax.ppermute(shard, axis, [(i, i ^ by) for i in range(length)])


def shift(shard, axis, by):
    length = lax.axis_size(axis)
    return lax.ppermute(shard, axis, [(i, (i + by) % length) for i in range(length)])


def back_a_block(shard):
    length = lax.axis_size("section")
    return lax.ppermute(shard, "section", [(i, i - 1) for i in range(1, length)])


def back_to_pair(shard):
    length, pairs = lax.axis_size("section"), lax.axis_size("tp")
    crossed = [
        (i * pairs + j, (i - 1) * pairs + (j ^ 1)) for i in range(1, length) for j in range(pairs)
    ]
    return back_a_block(shard), lax.ppermute(shard, ("section", "tp"), crossed)


def call(body, outs, ins, scratch=(), token=None, aliases=(), after=()):
    spaces = {"vmem": pltpu.VMEM, "smem": pltpu.SMEM, "any": pl.ANY, "hbm": pl.ANY, "kept": pltpu.VMEM}
    ins, outs = list(ins), list(outs)
    n_ins, n_outs = len(ins), len(outs)
    ins += [(a, "any") for a in after]
    if token is not None:
        ins.append((token, "any"))
    outs.append(((8, 128), F32, "any"))

    def without_tokens(*refs):
        first = refs[:n_ins]
        rest = refs[len(ins) :]
        body(*first, *rest[:n_outs], *rest[n_outs + 1 :])

    arrays = [
        pltpu.with_memory_space_constraint(a, pltpu.HBM) if where == "hbm" else a for a, where in ins
    ]
    got = pl.pallas_call(
        without_tokens,
        out_shape=[
            (pltpu.VMEM if where == "kept" else jax.ShapeDtypeStruct)(shape, dtype)
            for shape, dtype, where in outs
        ],
        in_specs=[pl.BlockSpec(memory_space=spaces[where]) for unused, where in ins],
        out_specs=[pl.BlockSpec(memory_space=spaces[where]) for *unused, where in outs],
        scratch_shapes=list(scratch),
        input_output_aliases=dict(aliases),
        compiler_params=pltpu.CompilerParams(vmem_limit_bytes=LIMIT),
        cost_estimate=pl.CostEstimate(flops=1024, bytes_accessed=1024, transcendentals=0),
    )(*arrays)
    return got[:-1], got[-1]


def dot(left, right):
    return jnp.dot(left, right, preferred_element_type=F32)


def dot_t(left, right):
    return lax.dot_general(left, right, (((1,), (1,)), ((), ())), preferred_element_type=F32)


def t_dot(left, right):
    return lax.dot_general(left, right, (((0,), (0,)), ((), ())), preferred_element_type=F32)


def unit_norm(values):
    centre = values - jnp.mean(values, -1, keepdims=True)
    inv_std = lax.rsqrt(jnp.mean(centre * centre, -1, keepdims=True) + 1e-06)
    return centre * inv_std, inv_std


def norm_back(grad, gain, unit_vals, inv_std):
    scaled = grad * gain
    return inv_std * (
        scaled
        - jnp.mean(scaled, -1, keepdims=True)
        - unit_vals * jnp.mean(scaled * unit_vals, -1, keepdims=True)
    )


def rows_at(place, rows):
    return pl.ds(pl.multiple_of(place * rows, rows), rows)


def join(own_ref, got_ref, side, whole_ref):
    rows = own_ref.shape[0]
    whole_ref[rows_at(side, rows)] = own_ref[...].astype(F32)
    whole_ref[rows_at(1 - side, rows)] = got_ref[...].astype(F32)
    return whole_ref[...]


def split(whole_ref, side, send_ref, keep_ref):
    rows = send_ref.shape[0]
    send_ref[...] = whole_ref[rows_at(1 - side, rows)].astype(BF16)
    keep_ref[...] = whole_ref[rows_at(side, rows)]


def store_lefts(parts, keep_ref, message, place):
    width = parts[0].shape[1]
    if keep_ref is None:
        for number, part in enumerate(parts):
            message[:, number * width : (number + 1) * width] = part
        return 2 * width
    half = width // 2
    for number, part in enumerate(parts):
        at = slice(number * half, (number + 1) * half)

        @pl.when(place == 0)
        def first():
            keep_ref[:, at] = part[:, :half]
            message[:, at] = part[:, half:]

        @pl.when(place != 0)
        def second():
            keep_ref[:, at] = part[:, half:]
            message[:, at] = part[:, :half]

    return width


def start_all(copies):
    for copy in copies:
        copy.start()
    return copies


def row_chunks(whole, count):
    return [slice(i * whole // count, (i + 1) * whole // count) for i in range(count)]


def after_mlp_up(pre, hidden_ref, slope_ref, at):
    squared = pre * pre
    tanh = jnp.tanh(GELU_SCALE * pre * (1.0 + GELU_CUBE * squared))
    hidden_ref[:, at] = (0.5 * pre * (1.0 + tanh)).astype(BF16)
    slope_ref[:, at] = 0.5 * (1.0 + tanh) + 0.5 * pre * (1.0 - tanh * tanh) * (
        GELU_SCALE * (1.0 + 3.0 * GELU_CUBE * squared)
    )


def column_blocks(width, size):
    return [slice(at, min(at + size, width)) for at in range(0, width, size)]


def mlp_first_kernel(
    flags, gains, streams, w_up, w_down, normed_ref, hidden_ref, slope_ref, send, keep, unit_ref, inv_ref,
    upper, grad_lower, up_here, down_here, gains_here, sems, whole,
):
    up_cut, down_cut = row_chunks(up_here.shape[1], CHUNKS), row_chunks(down_here.shape[1], CHUNKS)
    firsts = start_all(
        [
            pltpu.make_async_copy(streams.at[0, 0], upper, sems.at[0]),
            pltpu.make_async_copy(gains, gains_here, sems.at[1]),
        ]
    )
    ups = start_all(
        [
            pltpu.make_async_copy(w_up.at[0, at], up_here.at[0, at], sems.at[3 + i])
            for i, at in enumerate(up_cut)
        ]
    )
    downs = start_all(
        [
            pltpu.make_async_copy(w_down.at[0, at], down_here.at[0, at], sems.at[3 + CHUNKS + i])
            for i, at in enumerate(down_cut)
        ]
    )
    last = pltpu.make_async_copy(streams.at[0, 3], grad_lower, sems.at[2])
    last.start()
    for copy in firsts:
        copy.wait()
    unit, inv_std = unit_norm(upper[...])
    normed_ref[...] = (unit * gains_here[1:2]).astype(BF16)
    unit_ref[...] = unit
    inv_ref[...] = jnp.broadcast_to(inv_std, inv_ref.shape)
    pre = None
    for i, at in enumerate(up_cut):
        ups[i].wait()
        part = dot(normed_ref[:, at], up_here[0, at])
        pre = part if pre is None else pre + part
    after_mlp_up(pre, hidden_ref, slope_ref, slice(None))
    for i, at in enumerate(down_cut):
        downs[i].wait()
        whole[:, at] = dot_t(hidden_ref[...], down_here[0, at])
    split(whole, flags[0], send, keep)
    last.wait()


def mlp_forward_kernel(
    flags, gains, own, got, head, w_up, w_down, normed_ref, hidden_ref, slope_ref, send, keep, unit_ref, inv_ref,
    upper_ref, whole,
):
    upper = jnp.where(flags[1] == 1, head[0], join(own, got, flags[0], whole))
    upper_ref[...] = upper
    unit, inv_std = unit_norm(upper)
    normed = (unit * gains[1:2]).astype(BF16)
    for at in column_blocks(hidden_ref.shape[1], BLOCK):
        after_mlp_up(dot(normed, w_up[0, :, at]), hidden_ref, slope_ref, at)
    whole[...] = dot_t(hidden_ref[...], w_down[0])
    split(whole, flags[0], send, keep)
    normed_ref[...] = normed
    unit_ref[...] = unit
    inv_ref[...] = jnp.broadcast_to(inv_std, inv_ref.shape)


def mlp_backward_kernel(later, flags, *refs):
    if later:
        own, got, head = refs[:3]
        refs = refs[3:]
    else:
        grad_lower_ref, refs = refs[0], refs[1:]
    slope, w_up, w_down, grad_pre_ref, send, keep = refs[:6]
    whole = refs[-1]
    if later:
        grad_lower_ref = refs[6]
        grad_lower = jnp.where(flags[1] == 1, head[3], join(own, got, flags[0], whole))
        grad_lower_ref[...] = grad_lower
    else:
        grad_lower = grad_lower_ref[...]
    grad_low = grad_lower.astype(BF16)
    for at in column_blocks(grad_pre_ref.shape[1], BLOCK):
        grad_pre_ref[:, at] = (dot(grad_low, w_down[0, :, at]) * slope[:, at]).astype(BF16)
    whole[...] = dot_t(grad_pre_ref[...], w_up[0])
    split(whole, flags[0], send, keep)


def pack_kernel(two, flags, first, second, *refs):
    if two:
        keep_left, message, rights = refs[-1], refs[-2], refs[:-2]
    else:
        keep_left, message, rights = None, refs[-1], refs[:-1]
    at = store_lefts([first[...], second[...].astype(BF16)], keep_left, message, flags[2])
    for ref in rights:
        message[:, at : at + ref.shape[1]] = ref[...]
        at += ref.shape[1]


def add_kernel(left, right, out):
    out[...] = (left[...].astype(F32) + right[...].astype(F32)).astype(BF16)


def add_pass_kernel(left, right, unused, out, unused_out):
    add_kernel(left, right, out)


def project_kernel(later, flags, gains, *refs):
    if later:
        before = refs[0]
        refs = refs[1:]
    source, own, got, w_qkv, lower_ref, att_low_ref, query_ref, kv_ref, unit_ref, inv_ref = refs[:10]
    lower_low, whole = refs[10:-1], refs[-1]
    if later:
        lower = jnp.where(flags[1] == 1, source[1], before[...].astype(F32))
    else:
        lower = source[0, 1]
    lower = lower - join(own, got, flags[0], whole)
    unit, inv_std = unit_norm(lower)
    att_low = (unit * gains[0:1]).astype(BF16)
    local = query_ref.shape[0]
    kv_ref[...] = dot_t(w_qkv[local:], att_low).astype(BF16)
    query_ref[...] = dot_t(w_qkv[:local], att_low).astype(BF16)
    lower_ref[...] = lower
    att_low_ref[...] = att_low
    unit_ref[...] = unit
    inv_ref[...] = jnp.broadcast_to(inv_std, inv_ref.shape)
    for ref in lower_low:
        ref[...] = lower.astype(BF16)


def attend_kernel(others, flags, *refs):
    query, kv = refs[0], refs[1 : 2 + others]
    w_out, probs_ref, mixed_ref, send, keep, whole = refs[2 + others :]
    local = query.shape[0]
    for head in range(local // HEAD_DIM):
        at = slice(head * HEAD_DIM, (head + 1) * HEAD_DIM)
        at_value = slice(local + head * HEAD_DIM, local + (head + 1) * HEAD_DIM)
        keys = jnp.concatenate([ref[at, :] for ref in kv], 1)
        values = jnp.concatenate([ref[at_value, :] for ref in kv], 1)
        scores = t_dot(keys, query[at, :]) * 0.125
        top = jnp.max(scores, 0, keepdims=True)
        weights = jnp.exp(scores - top)
        probs = weights * (1.0 / jnp.sum(weights, 0, keepdims=True))
        probs_ref[head] = probs
        mixed_ref[at, :] = dot(values, probs.astype(BF16)).astype(BF16)
    whole[...] = t_dot(mixed_ref[...], w_out[...])
    split(whole, flags[0], send, keep)


def attend_back_kernel(later, others, flags, gains, *refs):
    if later:
        before, refs = refs[0], refs[1:]
    source, unit, inv, own, got, query = refs[:6]
    kv = refs[6 : 7 + others]
    refs = refs[7 + others :]
    probs_ref, w_out, total_low_ref, grad_query, kv_own = refs[:5]
    kv_sent = refs[5 : 5 + others]
    totals, whole = refs[5 + others : -1], refs[-1]
    if later:
        total = jnp.where(flags[1] == 1, source[2], before[...].astype(F32))
    else:
        total = source[0, 2]
    grad_normed = join(own, got, flags[0], whole)
    total = total + norm_back(grad_normed, gains[1:2], unit[...], inv[:, 0:1])
    total_low = total.astype(BF16)
    grad_mixed = dot_t(w_out[...], total_low).astype(BF16)
    local, rows = query.shape
    for head in range(local // HEAD_DIM):
        at = slice(head * HEAD_DIM, (head + 1) * HEAD_DIM)
        at_value = slice(local + head * HEAD_DIM, local + (head + 1) * HEAD_DIM)
        keys = jnp.concatenate([ref[at, :] for ref in kv], 1)
        values = jnp.concatenate([ref[at_value, :] for ref in kv], 1)
        probs = probs_ref[head]
        grad_head = grad_mixed[at, :]
        grad_probs = t_dot(values, grad_head)
        delta = jnp.sum(probs * grad_probs, 0, keepdims=True)
        grad_scores = (probs * (grad_probs - delta)).astype(BF16)
        grad_query[at, :] = (0.125 * dot(keys, grad_scores)).astype(BF16)
        grad_keys = 0.125 * dot_t(query[at, :], grad_scores)
        grad_values = dot_t(grad_head, probs.astype(BF16))
        kv_own[at, :] = grad_keys[:, :rows]
        kv_own[at_value, :] = grad_values[:, :rows]
        for number, ref in enumerate(kv_sent):
            cols = slice((number + 1) * rows, (number + 2) * rows)
            ref[at, :] = grad_keys[:, cols].astype(BF16)
            ref[at_value, :] = grad_values[:, cols].astype(BF16)
    total_low_ref[...] = total_low
    for ref in totals:
        ref[...] = total


def project_back_kernel(others, passed, flags, *refs):
    grad_query, kv_own = refs[:2]
    kv_got = refs[2 : 2 + others]
    mixed, w_qkv = refs[2 + others : 4 + others]
    rights, send, keep = refs[4 + others + passed : 7 + others + passed]
    whole = refs[-1]
    local = mixed.shape[0]
    total = kv_own[...]
    for ref in kv_got:
        total = total + ref[...].astype(F32)
    rights[:local, :] = grad_query[...]
    rights[local : 3 * local, :] = total.astype(BF16)
    whole[...] = t_dot(rights[: 3 * local, :], w_qkv[...])
    split(whole, flags[0], send, keep)
    rights[3 * local :, :] = mixed[...]


def upper_boundary_kernel(flags, upper, own, got, out):
    total = (own[...].astype(F32) + got[...].astype(F32)).astype(BF16)
    out[...] = (upper[rows_at(flags[0], out.shape[0])] - total.astype(F32)).astype(BF16)


def lower_boundary_kernel(flags, gains, unit, inv, grad_lower, own, got, out):
    rows = rows_at(flags[0], out.shape[0])
    grad_att = (own[...].astype(F32) + got[...].astype(F32)).astype(BF16).astype(F32)
    back = norm_back(grad_att, gains[0:1], unit[rows], inv[rows][:, 0:1])
    out[...] = (grad_lower[rows] + back).astype(BF16)


def recon_middle_kernel(lower_in, total, out, sems):
    copies = start_all(
        [
            pltpu.make_async_copy(lower_in, out.at[0, 1], sems.at[0]),
            pltpu.make_async_copy(total, out.at[0, 2], sems.at[1]),
        ]
    )
    for copy in copies:
        copy.wait()


def recon_upper_kernel(flags, unused, upper, own, got, out, here, sem, whole):
    here[...] = upper[...] - join(own, got, flags[0], whole)
    copy = pltpu.make_async_copy(here, out.at[0, 0], sem)
    copy.start()
    copy.wait()


def recon_lower_kernel(flags, gains, unused, unit, inv, grad_lower, own, got, out, here, sem, whole):
    grad_att = join(own, got, flags[0], whole)
    here[...] = grad_lower[...] + norm_back(grad_att, gains[0:1], unit[...], inv[:, 0:1])
    copy = pltpu.make_async_copy(here, out.at[0, 3], sem)
    copy.start()
    copy.wait()


def mlp_grad_kernel(places, *refs):
    out = refs[-1]
    cut, width = out.shape
    left = jnp.concatenate([refs[i][:, at : at + cut] for i, at, unused, unused in places], 0)
    right = jnp.concatenate([refs[i][:, at : at + width] for unused, unused, i, at in places], 0)
    out[...] = t_dot(left, right).astype(BF16)


def att_grad_kernel(count, *refs):
    lefts, rights, qkv, out = refs[:count], refs[count : 2 * count], refs[2 * count], refs[2 * count + 1]
    cut, split_at = out.shape[1], qkv.shape[0]
    right = jnp.concatenate([ref[...] for ref in rights], 1)
    for number, (at, to) in enumerate([(slice(0, split_at), qkv), (slice(split_at, None), out)]):
        left = jnp.concatenate([ref[:, number * cut : (number + 1) * cut] for ref in lefts], 0)
        to[...] = dot(right[at], left).astype(BF16)


def send_message(keep, message, width):
    length = lax.axis_size("seq")
    if keep is not None:
        return [keep, shift(message, "seq", 1)]
    place = lax.axis_index("seq")
    cut = width // length

    def at(index):
        return jnp.concatenate(
            [
                lax.dynamic_slice_in_dim(message[:, :width], index * cut, cut, 1),
                lax.dynamic_slice_in_dim(message[:, width : 2 * width], index * cut, cut, 1),
                message[:, 2 * width :],
            ],
            1,
        )

    return [at(place)] + [
        shift(at((place + by) % length), "seq", by) for by in range(1, length)
    ]


def send_whole(part):
    return [part] + [shift(part, "seq", by) for by in range(1, lax.axis_size("seq"))]


def per_device(streams, head_streams, gains, w_qkv, w_out, w_up, w_down):
    width, local = w_qkv.shape[1], w_qkv.shape[3]
    rows = streams.shape[2]
    n_seq = lax.axis_size("seq")
    others = n_seq - 1
    hidden_width = w_up.shape[2]
    half = rows // 2
    gains = gains[0]
    w_qkv_t = jnp.transpose(w_qkv[0], (1, 2, 0)).reshape(3 * local, width)
    w_out_t = w_out[0].T
    is_last = lax.axis_index("section") == lax.axis_size("section") - 1
    flags = jnp.stack(
        [lax.axis_index("tp") % 2, is_last.astype(jnp.int32), lax.axis_index("seq")]
    ).astype(jnp.int32)
    flag, gain = (flags, "smem"), (gains, "vmem")
    whole, one_sem = pltpu.VMEM((rows, width), F32), pltpu.SemaphoreType.DMA
    full, low = ((rows, width), F32, "vmem"), ((rows, width), BF16, "vmem")
    halves = [((half, width), BF16, "vmem"), ((half, width), F32, "vmem")]
    half_low = halves[0]
    two = n_seq == 2

    def pack(first, second, *rights, **more):
        size = width * (1 if two else 2) + sum(right.shape[1] for right in rights)
        got = run(
            functools.partial(pack_kernel, two),
            [((rows, size), BF16, "vmem")] + [low] * two,
            [flag] + here(first, second, *rights),
            **more,
        )
        return (got[1] if two else None), got[0]

    hid_low = ((rows, hidden_width), BF16, "vmem")
    hid_full = ((rows, hidden_width), F32, "vmem")
    token = None

    def run(body, outs, ins, *rest, **more):
        nonlocal token
        got, token = call(body, outs, ins, *rest, token=token, **more)
        return got

    def here(*arrays):
        return [(a, "vmem") for a in arrays]

    def middle_adds(total):
        by = 2
        while by * 2 < lax.axis_size("tp"):
            (total,) = run(add_kernel, [half_low], here(total, swap(total, "tp", by)))
            by *= 2
        return total, (swap(total, "tp", by) if by < lax.axis_size("tp") else None)

    def add(left, right):
        if right is None:
            return left
        return run(add_kernel, [half_low], here(left, right))[0]

    def zero_if_none(got, like):
        return jnp.zeros_like(like) if got is None else got

    def add_pass(left, right, passed, **more):
        if right is None:
            return left, passed
        return run(
            add_pass_kernel,
            [half_low, (passed.shape, passed.dtype, "any")],
            here(left, right) + [(passed, "any")],
            aliases=[(2, 1)],
            **more,
        )

    norm_outs = [full, ((rows, 128), F32, "vmem")]
    cut = width // n_seq
    left_width = 2 * cut
    for tick in range(2):
        later = tick > 0
        mlp_outs = [low, hid_low, hid_full] + halves + norm_outs
        if later:
            normed, hidden, slope, send_f, keep_f, unit_up, inv_up, upper = run(
                mlp_forward_kernel,
                mlp_outs + [full],
                [flag, gain] + here(own_upper, got_upper, head_streams, up_here, down_here),
                [whole],
            )
            got_f = swap(send_f, "tp", 1)
            hidden_2 = send_whole(hidden)
            (next_grad,) = run(
                lower_boundary_kernel,
                [half_low],
                [flag, gain] + here(unit_att, inv_att, grad_lower, sum_b, zero_if_none(got_b, sum_b)),
            )
            own_grad, got_grad = back_to_pair(next_grad)
            sum_f, lower_low = add_pass(keep_f, got_f, lower_low)
            next_lower = back_a_block(lower_low)
            sum_f, got_f = middle_adds(sum_f)
            source = here(own_grad, got_grad, head_streams)
        else:
            got = run(
                mlp_first_kernel,
                mlp_outs + [full, full] + [(w.shape, BF16, "kept") for w in (w_up, w_down)],
                [flag] + [(a, "hbm") for a in (gains, streams, w_up, w_down)],
                [
                    pltpu.VMEM(gains.shape, F32),
                    pltpu.SemaphoreType.DMA((3 + 2 * CHUNKS,)),
                    whole,
                ],
            )
            normed, hidden, slope, send_f, keep_f, unit_up, inv_up, upper, grad_lower = got[:9]
            up_here, down_here = got[9:]
            got_f = swap(send_f, "tp", 1)
            hidden_1 = send_whole(hidden)
            source = here(grad_lower)
        got = run(
            functools.partial(mlp_backward_kernel, later),
            [hid_low] + halves + [full] * later,
            [flag] + source + here(slope, up_here, down_here),
            [whole],
        )
        grad_pre, send_b, keep_b = got[:3]
        if later:
            grad_lower = got[3]
        got_b = swap(send_b, "tp", 1)
        if later:
            own_out, total_low = add_pass(sum_f, got_f, total_low, after=rights_1[1:])
            got_out = swap(own_out, "tp", 1)
            next_total = back_a_block(total_low)
            factors_3 = send_message(*pack(normed, grad_lower), width)
            (sum_b,) = run(add_kernel, [half_low], here(keep_b, got_b))
            sum_b, got_b = middle_adds(sum_b)
        else:
            (sum_f,) = run(add_kernel, [half_low], here(keep_f, got_f))
            sum_f, got_f = middle_adds(sum_f)
            factors_0 = send_message(*pack(normed, grad_lower), width)
            own_out = add(sum_f, got_f)
            got_out = swap(own_out, "tp", 1)
            (sum_b,) = run(add_kernel, [half_low], here(keep_b, got_b), after=hidden_1[1:])
            sum_b, got_b = middle_adds(sum_b)
            grad_pre_1 = grad_pre

        source = here(next_lower, head_streams) if later else here(streams)
        got = run(
            functools.partial(project_kernel, later),
            [full, low, ((local, rows), BF16, "vmem"), ((2 * local, rows), BF16, "vmem")]
            + norm_outs
            + [low] * (not later),
            [flag, gain] + source + here(own_out, got_out, w_qkv_t),
            [whole],
            after=factors_1[1:] if later else factors_0[1:],
        )
        lower_in, att_low, query, kv, unit_att, inv_att = got[:6]
        if not later:
            lower_low = got[6]
        all_kv = [kv] + [shift(kv, "seq", -by) for by in range(1, n_seq)]
        own_normed = add(sum_b, got_b)
        got_normed = swap(own_normed, "tp", 1)
        probs, mixed, send_f, keep_f = run(
            functools.partial(attend_kernel, others),
            [((local // HEAD_DIM, n_seq * rows, rows), F32, "vmem"), ((local, rows), BF16, "vmem")]
            + halves,
            [flag] + here(query, *all_kv, w_out_t),
            [whole],
            after=hidden_2[1:] + factors_3[1:] if later else (),
        )
        got_f = swap(send_f, "tp", 1)

        got = run(
            functools.partial(attend_back_kernel, later, others),
            [low, ((local, rows), BF16, "vmem"), ((2 * local, rows), F32, "vmem")]
            + [((2 * local, rows), BF16, "vmem")] * others
            + [full] * later,
            [flag, gain]
            + (here(next_total, head_streams) if later else here(streams))
            + here(unit_up, inv_up, own_normed, got_normed, query, *all_kv, probs, w_out_t),
            [whole],
        )
        total_low, grad_query, kv_own = got[:3]
        kv_got = [shift(part, "seq", by + 1) for by, part in enumerate(got[3 : 3 + others])]
        (sum_f,) = run(add_kernel, [half_low], here(keep_f, got_f))
        sum_f, got_f = middle_adds(sum_f)
        if later:
            recon_out = [((1, 4, rows, width), F32, "any")]
            (recon,) = run(
                recon_middle_kernel, recon_out, here(lower_in, got[-1]), [pltpu.SemaphoreType.DMA((2,))]
            )
        got = run(
            functools.partial(project_back_kernel, others, int(later)),
            [((4 * local, rows), BF16, "vmem")] + halves + [(grad_pre.shape, BF16, "any")] * later,
            [flag] + here(grad_query, kv_own, *kv_got, mixed, w_qkv_t) + [(grad_pre, "any")] * later,
            [whole],
            aliases=[(5 + others, 3)] * later,
        )
        rights, send_b, keep_b = got[:3]
        got_b = swap(send_b, "tp", 1)
        rights_att = send_whole(rights)

        if later:
            rights_2 = rights_att
            grad_pre_2 = send_whole(got[3])
            factors_2 = send_message(*pack(att_low, total_low), width)
            own_f = add(sum_f, got_f)
            got_f = swap(own_f, "tp", 1)
            (sum_b,) = run(add_kernel, [half_low], here(keep_b, got_b))
            sum_b, got_b = middle_adds(sum_b)
        else:
            rights_1 = rights_att
            (next_half,) = run(
                upper_boundary_kernel,
                [half_low],
                [flag] + here(upper, sum_f, zero_if_none(got_f, sum_f)),
            )
            (sum_b,) = run(add_kernel, [half_low], here(keep_b, got_b))
            sum_b, got_b = middle_adds(sum_b)
            own_upper, got_upper = back_to_pair(next_half)
            factors_1 = send_message(*pack(att_low, total_low, grad_pre), width)

    ups = [(factors_0[0], 0, grad_pre_1, 0), (factors_3[0], 0, grad_pre_2[0], 0)]
    downs = [(factors_0[0], cut, hidden_1[0], 0), (factors_3[0], cut, hidden_2[0], 0)]
    for i in range(1, n_seq):
        ups += [(factors_0[i], 0, factors_1[i], left_width), (factors_3[i], 0, grad_pre_2[i], 0)]
        downs += [(factors_0[i], cut, hidden_1[i], 0), (factors_3[i], cut, hidden_2[i], 0)]

    def mlp_grad(terms):
        if not two:
            left = jnp.concatenate([a[:, at : at + cut] for a, at, unused, unused in terms], 0)
            right = jnp.concatenate([a[:, at : at + hidden_width] for unused, unused, a, at in terms], 0)
            return t_dot(left, right).astype(BF16)
        arrays, places = [], []
        for left, left_at, right, right_at in terms:
            for array in (left, right):
                if not any(array is known for known in arrays):
                    arrays.append(array)
            where = [next(i for i, known in enumerate(arrays) if known is a) for a in (left, right)]
            places.append((where[0], left_at, where[1], right_at))
        (grad,) = run(
            functools.partial(mlp_grad_kernel, places),
            [((cut, hidden_width), BF16, "vmem")],
            here(*arrays),
        )
        return grad

    grad_down = mlp_grad(downs)
    (recon,) = run(
        recon_upper_kernel,
        recon_out,
        [flag, (recon, "any")] + here(upper, own_f, got_f),
        [whole, one_sem, whole],
        aliases=[(1, 0)],
    )
    own_b = add(sum_b, got_b)
    got_b = swap(own_b, "tp", 1)
    grad_up = mlp_grad(ups)
    lefts_att, rights_att = factors_1 + factors_2, rights_1 + rights_2
    if two:
        grad_qkv, grad_out = run(
            functools.partial(att_grad_kernel, len(rights_att)),
            [((3 * local, cut), BF16, "vmem"), ((local, cut), BF16, "vmem")],
            here(*lefts_att, *rights_att),
        )
    else:
        right = jnp.concatenate(rights_att, 1)
        left = jnp.concatenate([a[:, :left_width] for a in lefts_att], 0)
        grad_qkv = dot(right[: 3 * local], left[:, :cut]).astype(BF16)
        grad_out = dot(right[3 * local :], left[:, cut:]).astype(BF16)
    (recon,) = run(
        recon_lower_kernel,
        recon_out,
        [flag, gain, (recon, "any")] + here(unit_att, inv_att, grad_lower, own_b, got_b),
        [whole, one_sem, whole],
        aliases=[(2, 0)],
    )
    return (
        recon,
        jnp.transpose(grad_qkv.reshape(3, local, cut), (2, 0, 1))[None],
        grad_out.T[None],
        grad_up[None],
        grad_down[None],
    )


def solution(mesh):
    placed = (
        P("section", None, "seq", None),
        P(None, "seq", None),
        P("section", None, None),
        P("section", None, None, "tp"),
        P("section", None, "tp"),
        P("section", None, "tp"),
        P("section", None, "tp"),
    )
    return jax.shard_map(
        per_device,
        mesh=mesh,
        in_specs=placed,
        out_specs=(
            P("section", None, "seq", None),
            P("section", "seq", None, "tp"),
            P("section", "seq", "tp"),
            P("section", "seq", "tp"),
            P("section", "seq", "tp"),
        ),
        check_vma=False,
    )
```

time: 492 us -> 152 us (0.31)
  waiting for transfers between devices: 344 us -> 48 us
  starting transfers between devices: 2.1 us -> 58.3 us
  matrix products: 54.7 us -> 0 us
  Pallas kernels: 0 us -> 44.5 us
  local copies, waits for them, and re-layouts: 35.8 us -> 0.03 us
  other arithmetic: 26.3 us -> 0.08 us
  between operations: 15 us -> 1.21 us
  blocking collectives: 13.3 us -> 0 us
    psum x4 -> x0, waiting for transfers between devices: 186 us -> none  [the longest x2 135 us: block_step(): mlp_out, grad_normed = lax.psum((mlp_part, normed_part), 'tp')]
    unnamed x15 -> x0, waiting for transfers between devices: 109 us -> none
    ppermute x1 -> x41, starting transfers between devices: 1.28 us -> 58.3 us  [the longest x22 33.4 us: swap(): return lax.ppermute(shard, axis, [(i, i ^ by) for i in range(length)])]
    dot_general x36 -> x0, matrix products: 54.7 us -> none  [the longest x2 5.43 us: block_step(): jnp.dot(grad_lower_low.T, hidden, preferred_element_type=jnp.float32)]
    reduce_scatter x1 -> x0, waiting for transfers between devices: 45.2 us -> none  [per_device(): lax.psum_scatter(as_sent(totals), 'seq', scatter_dimension=0, tiled=True)]
    pallas_call x0 -> x38, Pallas kernels: none -> 44.5 us  [call(): pl.pallas_call(without_tokens, out_shape=[(pltpu.VMEM if where == 'kept'...]
    ppermute x1 -> x41, waiting for transfers between devices: 3.95 us -> 48 us  [the longest x22 28.6 us: swap(): return lax.ppermute(shard, axis, [(i, i ^ by) for i in range(length)])]
    unnamed x107 -> x10, local copies, waits for them, and re-layouts: 34.8 us -> 0.03 us
  transfers between devices with their start and end apart: 11 -> 41, of which waited for: 11 -> 23; matrix products, arithmetic and copies ran while one was open for 12% -> 0% of each run, Pallas kernels for 0% -> 24%
where the time goes in v2:
time: 152 us
  starting transfers between devices  58.3 us (38%)
  waiting for transfers between devices  48 us (32%)
  Pallas kernels  44.5 us (29%)
    pallas_call x38, Pallas kernels, call(): pl.pallas_call(without_tokens, out_shape=[(pltpu.VMEM if where == 'kept'...  44.5 us
    ppermute x22, starting transfers between devices, swap(): return lax.ppermute(shard, axis, [(i, i ^ by) for i in range(length)])  33.4 us
    ppermute x22, waiting for transfers between devices, swap(): return lax.ppermute(shard, axis, [(i, i ^ by) for i in range(length)])  28.6 us
    ppermute x13, starting transfers between devices, shift(): lax.ppermute(shard, axis, [(i, (i + by) % length) for i in range(length)])  16.9 us
    ppermute x2, waiting for transfers between devices, back_to_pair(): lax.ppermute(shard, ('section', 'tp'), crossed)  9.14 us
    ppermute x13, waiting for transfers between devices, shift(): lax.ppermute(shard, axis, [(i, (i + by) % length) for i in range(length)])  8.67 us
    ppermute x4, starting transfers between devices, back_a_block(): lax.ppermute(shard, 'section', [(i, i - 1) for i in range(1, length)])  5.33 us
  transfers between devices with their start and end apart: 41, of which 23 were waited for; matrix products, arithmetic and copies ran while one was open for 0% of the time, Pallas kernels for 24%

profile of v2, /device:TPU:0, one launch (start us, length us, event | category | flops | bytes accessed | tf_op | source)
XLA Modules:
  0.0 152.1 jit_solution(18051247876878488237)
XLA Ops:
  0.7 5.9 %shard_map.110 = (bf16[128,1280]{1,0:T(8,128)(2,1)S(1)}, bf16[128,1280]{1,0:T(8,128)(2,1)S(1)}, f32[128,1280]{1,0:T(8,128)S(1)}, bf16[64,1280]{1,0:T(8,128)(2,1)...) custom-call(s32[3]{0:T(128)S(1)} %pad_add_fusion.refs_0_, ...), custom_call_target="tpu_custom_call" | custom-call | flops 1024 | bytes 1024 | tf_op jit(solution)/shard_map/pallas_call | solution.py:60
  6.6 3.1 %collective-permute-start = (bf16[64,1280]{1,0:T(8,128)(2,1)S(1)}, bf16[64,1280]{1,0:T(8,128)(2,1)S(1)}, u32[]{:S(2)}, u32[]{:S(2)}) collective-permute-start(bf16[64,1280]{1,0:T(8,128)(2,1)S(1)} %get-tuple-element.139), channel_id=1, source_target_pairs={{0,1},{1,0},{2,3},{3,2},{4,5},{5,4},{6,7},{7,6},{8,9},{9,8},{10,11... | collective-permute-start | bytes 491528 | tf_op jit(solution)/shard_map/ppermute | solution.py:22
  13.9 2.8 %collective-permute-start.1 = (bf16[64,1280]{1,0:T(8,128)(2,1)S(1)}, bf16[64,1280]{1,0:T(8,128)(2,1)S(1)}, u32[]{:S(2)}, u32[]{:S(2)}) collective-permute-start(bf16[64,1280]{1,0:T(8,128)(2,1)S(1)} %get-tuple-element.146.refs_0_), channel_id=1, source_target_pairs={{0,2},{1,3},{2,0},{3,1},{4,6},{5,7},{6,4},{7,5},{8,10},{9,11},{10,... | collective-permute-start | bytes 491528 | tf_op jit(solution)/shard_map/ppermute | solution.py:22
  20.6 3.3 %collective-permute-done.1.refs_1_ = bf16[64,1280]{1,0:T(8,128)(2,1)S(1)} collective-permute-done((bf16[64,1280]{1,0:T(8,128)(2,1)S(1)}, bf16[64,1280]{1,0:T(8,128)(2,1)S(1)}, u32[]{:S(2)}, u32[]{:S(2)}) %collective-permute-start.1) | collective-permute-done | bytes 163872 | tf_op jit(solution)/shard_map/ppermute | solution.py:22
  28.0 3.4 %collective-permute-done.2.refs_4_ = bf16[64,1280]{1,0:T(8,128)(2,1)S(1)} collective-permute-done((bf16[64,1280]{1,0:T(8,128)(2,1)S(1)}, bf16[64,1280]{1,0:T(8,128)(2,1)S(1)}, u32[]{:S(2)}, u32[]{:S(2)}) %collective-permute-start.2) | collective-permute-done | bytes 163872 | tf_op jit(solution)/shard_map/ppermute | solution.py:22
  33.1 2.2 %collective-permute-start.6 = (bf16[640,128]{1,0:T(8,128)(2,1)S(1)}, bf16[640,128]{1,0:T(8,128)(2,1)S(1)}, u32[]{:S(2)}, u32[]{:S(2)}) collective-permute-start(bf16[640,128]{1,0:T(8,128)(2,1)S(1)} %get-tuple-element.158.refs_2_.refs_8_), channel_id=1, source_target_pairs={{0,4},{4,0},{1,5},{5,1},{2,6},{6,2},{3,7},{7,3},{8,12},{12,8},{9,1... | collective-permute-start | bytes 491528 | tf_op jit(solution)/shard_map/ppermute | solution.py:27
  36.1 2.5 %collective-permute-done.6.refs_3_.refs_9_ = bf16[640,128]{1,0:T(8,128)(2,1)S(1)} collective-permute-done((bf16[640,128]{1,0:T(8,128)(2,1)S(1)}, bf16[640,128]{1,0:T(8,128)(2,1)S(1)}, u32[]{:S(2)}, u32[]{:S(2)}) %collective-permute-start.6) | collective-permute-done | bytes 163872 | tf_op jit(solution)/shard_map/ppermute | solution.py:27
  38.7 2.4 %shard_map.118 = (f32[5,256,128]{2,1,0:T(8,128)S(1)}, bf16[320,128]{1,0:T(8,128)(2,1)S(1)}, bf16[64,1280]{1,0:T(8,128)(2,1)S(1)}, f32[64,1280]{1,0:T(8,128)S(1)}, f32[8,128]{1,0:T(8,128)S(1)}) custom-call(s32[3]{0:T(128)S(1)} %pad_add_fusion.refs_0_, bf16[320,128]{1,0:T(8,128)(2,1)S(1)} %get-tuple-element.157.refs_1_.refs_7_, ...), custom_call_target="tpu_custom_call" | custom-call | flops 1024 | bytes 1024 | tf_op jit(solution)/shard_map/pallas_call | solution.py:60
  43.1 2.8 %shard_map.119 = (bf16[128,1280]{1,0:T(8,128)(2,1)S(1)}, bf16[320,128]{1,0:T(8,128)(2,1)S(1)}, f32[640,128]{1,0:T(8,128)S(1)}, bf16[640,128]{1,0:T(8,128)(2,1)S(1)}, f32[8,128]{1,0:T(8,128)S(1)}) custom-call(s32[3]{0:T(128)S(1)} %pad_add_fusion.refs_0_, f32[2,1280]{1,0:T(2,128)S(1)} %bitcast.32, f32[1,4,128,1280]{3,2,1,0:T(8,128)S(1)} %copy-done.2, ...), custom_call_target="tpu_custom_call" | custom-call | flops 1024 | bytes 1024 | tf_op jit(solution)/shard_map/pallas_call | solution.py:60
  46.5 2.8 %collective-permute-start.10 = (bf16[64,1280]{1,0:T(8,128)(2,1)S(1)}, bf16[64,1280]{1,0:T(8,128)(2,1)S(1)}, u32[]{:S(2)}, u32[]{:S(2)}) collective-permute-start(bf16[64,1280]{1,0:T(8,128)(2,1)S(1)} %get-tuple-element.170.refs_2_), channel_id=1, source_target_pairs={{0,2},{1,3},{2,0},{3,1},{4,6},{5,7},{6,4},{7,5},{8,10},{9,11},{10,... | collective-permute-start | bytes 491528 | tf_op jit(solution)/shard_map/ppermute | solution.py:22
  60.4 3.1 %collective-permute-done.13.refs_3_ = bf16[64,1280]{1,0:T(8,128)(2,1)S(1)} collective-permute-done((bf16[64,1280]{1,0:T(8,128)(2,1)S(1)}, bf16[64,1280]{1,0:T(8,128)(2,1)S(1)}, u32[]{:S(2)}, u32[]{:S(2)}) %collective-permute-start.13) | collective-permute-done | bytes 163872 | tf_op jit(solution)/shard_map/ppermute | solution.py:40
  63.5 2.6 %shard_map.125 = (bf16[128,1280]{1,0:T(8,128)(2,1)S(1)}, bf16[128,1280]{1,0:T(8,128)(2,1)S(1)}, f32[128,1280]{1,0:T(8,128)S(1)}, bf16[64,1280]{1,0:T(8,128)(2,1)...) custom-call(s32[3]{0:T(128)S(1)} %pad_add_fusion.refs_0_, ...), custom_call_target="tpu_custom_call" | custom-call | flops 1024 | bytes 1024 | tf_op jit(solution)/shard_map/pallas_call | solution.py:60
  67.5 2.7 %collective-permute-start.19 = (bf16[1280,128]{1,0:T(8,128)(2,1)S(1)}, bf16[1280,128]{1,0:T(8,128)(2,1)S(1)}, u32[]{:S(2)}, u32[]{:S(2)}) collective-permute-start(bf16[1280,128]{1,0:T(8,128)(2,1)S(1)} %get-tuple-element.196.refs_4_), channel_id=1, source_target_pairs={{0,4},{4,0},{1,5},{5,1},{2,6},{6,2},{3,7},{7,3},{8,12},{12,8},{9,1... | collective-permute-start | bytes 983048 | tf_op jit(solution)/shard_map/ppermute | solution.py:27
  78.7 6.0 %collective-permute-done.21.refs_2_ = bf16[64,1280]{1,0:T(8,128)(2,1)S(1)} collective-permute-done((bf16[64,1280]{1,0:T(8,128)(2,1)S(1)}, bf16[64,1280]{1,0:T(8,128)(2,1)S(1)}, u32[]{:S(2)}, u32[]{:S(2)}) %collective-permute-start.21) | collective-permute-done | bytes 163872 | tf_op jit(solution)/shard_map/ppermute | solution.py:40
  94.1 3.3 %collective-permute-start.26 = (bf16[64,1280]{1,0:T(8,128)(2,1)S(1)}, bf16[64,1280]{1,0:T(8,128)(2,1)S(1)}, u32[]{:S(2)}, u32[]{:S(2)}) collective-permute-start(bf16[64,1280]{1,0:T(8,128)(2,1)S(1)} %get-tuple-element.214.refs_0_), channel_id=1, source_target_pairs={{0,2},{1,3},{2,0},{3,1},{4,6},{5,7},{6,4},{7,5},{8,10},{9,11},{10,... | collective-permute-start | bytes 491528 | tf_op jit(solution)/shard_map/ppermute | solution.py:22
  101.1 3.8 %collective-permute-done.26.refs_1_ = bf16[64,1280]{1,0:T(8,128)(2,1)S(1)} collective-permute-done((bf16[64,1280]{1,0:T(8,128)(2,1)S(1)}, bf16[64,1280]{1,0:T(8,128)(2,1)S(1)}, u32[]{:S(2)}, u32[]{:S(2)}) %collective-permute-start.26) | collective-permute-done | bytes 163872 | tf_op jit(solution)/shard_map/ppermute | solution.py:22
  107.8 2.4 %shard_map.134 = (f32[5,256,128]{2,1,0:T(8,128)S(1)}, bf16[320,128]{1,0:T(8,128)(2,1)S(1)}, bf16[64,1280]{1,0:T(8,128)(2,1)S(1)}, f32[64,1280]{1,0:T(8,128)S(1)}, f32[8,128]{1,0:T(8,128)S(1)}) custom-call(s32[3]{0:T(128)S(1)} %pad_add_fusion.refs_0_, bf16[320,128]{1,0:T(8,128)(2,1)S(1)} %get-tuple-element.217.refs_1_.refs_8_, ...), custom_call_target="tpu_custom_call" | custom-call | flops 1024 | bytes 1024 | tf_op jit(solution)/shard_map/pallas_call | solution.py:60
  112.0 2.9 %shard_map.135 = (bf16[128,1280]{1,0:T(8,128)(2,1)S(1)}, bf16[320,128]{1,0:T(8,128)(2,1)S(1)}, f32[640,128]{1,0:T(8,128)S(1)}, bf16[640,128]{1,0:T(8,128)(2,1)S(...) custom-call(s32[3]{0:T(128)S(1)} %pad_add_fusion.refs_0_, f32[2,1280]{1,0:T(2,128)S(1)} %bitcast.36, ...), custom_call_target="tpu_custom_call" | custom-call | flops 1024 | bytes 1024 | tf_op jit(solution)/shard_map/pallas_call | solution.py:60
  116.5 4.5 %collective-permute-start.32 = (bf16[64,1280]{1,0:T(8,128)(2,1)S(1)}, bf16[64,1280]{1,0:T(8,128)(2,1)S(1)}, u32[]{:S(2)}, u32[]{:S(2)}) collective-permute-start(bf16[64,1280]{1,0:T(8,128)(2,1)S(1)} %get-tuple-element.231.refs_0_), channel_id=1, source_target_pairs={{0,2},{1,3},{2,0},{3,1},{4,6},{5,7},{6,4},{7,5},{8,10},{9,11},{10,... | collective-permute-start | bytes 491528 | tf_op jit(solution)/shard_map/ppermute | solution.py:22
  129.4 3.1 %collective-permute-done.35.refs_1_ = bf16[64,1280]{1,0:T(8,128)(2,1)S(1)} collective-permute-done((bf16[64,1280]{1,0:T(8,128)(2,1)S(1)}, bf16[64,1280]{1,0:T(8,128)(2,1)S(1)}, u32[]{:S(2)}, u32[]{:S(2)}) %collective-permute-start.35) | collective-permute-done | bytes 163872 | tf_op jit(solution)/shard_map/ppermute | solution.py:22
  137.4 4.7 %collective-permute-done.36.refs_1_ = bf16[64,1280]{1,0:T(8,128)(2,1)S(1)} collective-permute-done((bf16[64,1280]{1,0:T(8,128)(2,1)S(1)}, bf16[64,1280]{1,0:T(8,128)(2,1)S(1)}, u32[]{:S(2)}, u32[]{:S(2)}) %collective-permute-start.36) | collective-permute-done | bytes 163872 | tf_op jit(solution)/shard_map/ppermute | solution.py:22
  142.3 2.2 %shard_map.145 = (bf16[640,1280]{1,0:T(8,128)(2,1)}, f32[8,128]{1,0:T(8,128)S(1)}) custom-call(bf16[128,1280]{1,0:T(8,128)(2,1)S(1)} %get-tuple-element.243.refs_0_, bf16[128,1280]{1,0:T(8,128)(2,1)S(1)} %get-tuple-element.180.refs_3_.refs_1_, bf16[128,1280]{1,0:T(8,128)(2,1)S(1)} %get-tuple-element.244.refs_2_, ...), custom_call_target="tpu_custom_call" | custom-call | flops 1024 | bytes 1024 | tf_op jit(solution)/shard_map/pallas_call | solution.py:60
  144.5 3.3 %collective-permute-done.39.refs_7_ = bf16[1280,128]{1,0:T(8,128)(2,1)S(1)} collective-permute-done((bf16[1280,128]{1,0:T(8,128)(2,1)S(1)}, bf16[1280,128]{1,0:T(8,128)(2,1)S(1)}, u32[]{:S(2)}, u32[]{:S(2)}) %collective-permute-start.39) | collective-permute-done | bytes 327712 | tf_op jit(solution)/shard_map/ppermute | solution.py:27
  147.8 2.3 %shard_map.146 = (bf16[960,640]{1,0:T(8,128)(2,1)}, bf16[320,640]{1,0:T(8,128)(2,1)}, f32[8,128]{1,0:T(8,128)S(1)}) custom-call(bf16[128,1280]{1,0:T(8,128)(2,1)S(1)} %get-tuple-element.256.refs_0_, bf16[128,2560]{1,0:T(8,128)(2,1)S(1)} %collective-permute-done.23.refs_7_.refs_5_.refs_1_, bf16[128,1280]{1,0:T(8,128)(2,1)S(1)} %get-tuple-element.257.refs_2_, ...), custom_call_target="tpu_custom_call" | custom-call | flops 1024 | bytes 1024 | tf_op jit(solution)/shard_map/pallas_call | solution.py:60
  (107 shorter events, 72.6 us)
Async XLA Ops:
  9.7 16.5 %collective-permute-start.5 = (bf16[128,1280]{1,0:T(8,128)(2,1)S(1)}, bf16[128,1280]{1,0:T(8,128)(2,1)S(1)}, u32[]{:S(2)}, u32[]{:S(2)}) collective-permute-start(bf16[128,1280]{1,0:T(8,128)(2,1)S(1)} %get-tuple-element.154.refs_1_), channel_id=1, source_target_pairs={{0,4},{4,0},{1,5},{5,1},{2,6},{6,2},{3,7},{7,3},{8,12},{12,8},{9,1... | collective-permute-start | bytes 983048 | tf_op jit(solution)/shard_map/ppermute | solution.py:27
  13.9 10.0 %collective-permute-start.1 = (bf16[64,1280]{1,0:T(8,128)(2,1)S(1)}, bf16[64,1280]{1,0:T(8,128)(2,1)S(1)}, u32[]{:S(2)}, u32[]{:S(2)}) collective-permute-start(bf16[64,1280]{1,0:T(8,128)(2,1)S(1)} %get-tuple-element.146.refs_0_), channel_id=1, source_target_pairs={{0,2},{1,3},{2,0},{3,1},{4,6},{5,7},{6,4},{7,5},{8,10},{9,11},{10,... | collective-permute-start | bytes 491528 | tf_op jit(solution)/shard_map/ppermute | solution.py:22
  17.4 14.0 %collective-permute-start.3 = (bf16[128,1280]{1,0:T(8,128)(2,1)S(1)}, bf16[128,1280]{1,0:T(8,128)(2,1)S(1)}, u32[]{:S(2)}, u32[]{:S(2)}) collective-permute-start(bf16[128,1280]{1,0:T(8,128)(2,1)S(1)} %get-tuple-element.151), channel_id=1, source_target_pairs={{0,4},{4,0},{1,5},{5,1},{2,6},{6,2},{3,7},{7,3},{8,12},{12,8},{9,1... | collective-permute-start | bytes 983048 | tf_op jit(solution)/shard_map/ppermute | solution.py:27
  26.2 9.7 %collective-permute-start.7 = (bf16[64,1280]{1,0:T(8,128)(2,1)S(1)}, bf16[64,1280]{1,0:T(8,128)(2,1)S(1)}, u32[]{:S(2)}, u32[]{:S(2)}) collective-permute-start(bf16[64,1280]{1,0:T(8,128)(2,1)S(1)} %get-tuple-element.159.refs_0_), channel_id=1, source_target_pairs={{0,2},{1,3},{2,0},{3,1},{4,6},{5,7},{6,4},{7,5},{8,10},{9,11},{10,... | collective-permute-start | bytes 491528 | tf_op jit(solution)/shard_map/ppermute | solution.py:22
  46.5 7.6 %collective-permute-start.10 = (bf16[64,1280]{1,0:T(8,128)(2,1)S(1)}, bf16[64,1280]{1,0:T(8,128)(2,1)S(1)}, u32[]{:S(2)}, u32[]{:S(2)}) collective-permute-start(bf16[64,1280]{1,0:T(8,128)(2,1)S(1)} %get-tuple-element.170.refs_2_), channel_id=1, source_target_pairs={{0,2},{1,3},{2,0},{3,1},{4,6},{5,7},{6,4},{7,5},{8,10},{9,11},{10,... | collective-permute-start | bytes 491528 | tf_op jit(solution)/shard_map/ppermute | solution.py:22
  57.9 12.4 %collective-permute-start.16 = (bf16[64,1280]{1,0:T(8,128)(2,1)S(1)}, bf16[64,1280]{1,0:T(8,128)(2,1)S(1)}, u32[]{:S(2)}, u32[]{:S(2)}) collective-permute-start(bf16[64,1280]{1,0:T(8,128)(2,1)S(1)} %get-tuple-element.191.refs_5_), channel_id=1, source_target_pairs={{0,2},{1,3},{2,0},{3,1},{4,6},{5,7},{6,4},{7,5},{8,10},{9,11},{10,... | collective-permute-start | bytes 491528 | tf_op jit(solution)/shard_map/ppermute | solution.py:22
  66.1 7.6 %collective-permute-start.15 = (bf16[64,1280]{1,0:T(8,128)(2,1)S(1)}, bf16[64,1280]{1,0:T(8,128)(2,1)S(1)}, u32[]{:S(2)}, u32[]{:S(2)}) collective-permute-start(bf16[64,1280]{1,0:T(8,128)(2,1)S(1)} %get-tuple-element.187), channel_id=1, source_target_pairs={{0,1},{1,0},{2,3},{3,2},{4,5},{5,4},{6,7},{7,6},{8,9},{9,8},{10,11... | collective-permute-start | bytes 491528 | tf_op jit(solution)/shard_map/ppermute | solution.py:22
  67.5 19.5 %collective-permute-start.19 = (bf16[1280,128]{1,0:T(8,128)(2,1)S(1)}, bf16[1280,128]{1,0:T(8,128)(2,1)S(1)}, u32[]{:S(2)}, u32[]{:S(2)}) collective-permute-start(bf16[1280,128]{1,0:T(8,128)(2,1)S(1)} %get-tuple-element.196.refs_4_), channel_id=1, source_target_pairs={{0,4},{4,0},{1,5},{5,1},{2,6},{6,2},{3,7},{7,3},{8,12},{12,8},{9,1... | collective-permute-start | bytes 983048 | tf_op jit(solution)/shard_map/ppermute | solution.py:27
  70.2 28.5 %collective-permute-start.23 = (bf16[128,2560]{1,0:T(8,128)(2,1)S(1)}, bf16[128,2560]{1,0:T(8,128)(2,1)S(1)}, u32[]{:S(2)}, u32[]{:S(2)}) collective-permute-start(bf16[128,2560]{1,0:T(8,128)(2,1)S(1)} %get-tuple-element.202), channel_id=1, source_target_pairs={{0,4},{4,0},{1,5},{5,1},{2,6},{6,2},{3,7},{7,3},{8,12},{12,8},{9,1... | collective-permute-start | bytes 1966088 | tf_op jit(solution)/shard_map/ppermute | solution.py:27
  72.4 12.4 %collective-permute-start.21 = (bf16[64,1280]{1,0:T(8,128)(2,1)S(1)}, bf16[64,1280]{1,0:T(8,128)(2,1)S(1)}, u32[]{:S(2)}, u32[]{:S(2)}) collective-permute-start(bf16[64,1280]{1,0:T(8,128)(2,1)S(1)} %get-tuple-element.197), channel_id=1, source_target_pairs={{8,1},{9,0},{10,3},{11,2},{16,9},{17,8},{18,11},{19,10},{24,17},{2... | collective-permute-start | bytes 491528 | tf_op jit(solution)/shard_map/ppermute | solution.py:40
  73.7 13.3 %collective-permute-start.18 = (bf16[64,1280]{1,0:T(8,128)(2,1)S(1)}, bf16[64,1280]{1,0:T(8,128)(2,1)S(1)}, u32[]{:S(2)}, u32[]{:S(2)}) collective-permute-start(bf16[64,1280]{1,0:T(8,128)(2,1)S(1)} %get-tuple-element.195.refs_0_), channel_id=1, source_target_pairs={{0,2},{1,3},{2,0},{3,1},{4,6},{5,7},{6,4},{7,5},{8,10},{9,11},{10,... | collective-permute-start | bytes 491528 | tf_op jit(solution)/shard_map/ppermute | solution.py:22
  77.3 20.1 %collective-permute-start.17 = (bf16[128,1280]{1,0:T(8,128)(2,1)S(1)}, bf16[128,1280]{1,0:T(8,128)(2,1)S(1)}, u32[]{:S(2)}, u32[]{:S(2)}) collective-permute-start(bf16[128,1280]{1,0:T(8,128)(2,1)S(1)} %get-tuple-element.194), channel_id=1, source_target_pairs={{8,0},{16,8},{24,16},{9,1},{17,9},{25,17},{10,2},{18,10},{26,18},{... | collective-permute-start | bytes 983048 | tf_op jit(solution)/shard_map/ppermute | solution.py:32
  89.2 17.8 %collective-permute-start.29 = (bf16[128,1280]{1,0:T(8,128)(2,1)S(1)}, bf16[128,1280]{1,0:T(8,128)(2,1)S(1)}, u32[]{:S(2)}, u32[]{:S(2)}) collective-permute-start(bf16[128,1280]{1,0:T(8,128)(2,1)S(1)} %get-tuple-element.219.refs_3_), channel_id=1, source_target_pairs={{0,4},{4,0},{1,5},{5,1},{2,6},{6,2},{3,7},{7,3},{8,12},{12,8},{9,1... | collective-permute-start | bytes 983048 | tf_op jit(solution)/shard_map/ppermute | solution.py:27
  92.3 14.6 %collective-permute-start.30 = (bf16[128,1280]{1,0:T(8,128)(2,1)S(1)}, bf16[128,1280]{1,0:T(8,128)(2,1)S(1)}, u32[]{:S(2)}, u32[]{:S(2)}) collective-permute-start(bf16[128,1280]{1,0:T(8,128)(2,1)S(1)} %get-tuple-element.220), channel_id=1, source_target_pairs={{0,4},{4,0},{1,5},{5,1},{2,6},{6,2},{3,7},{7,3},{8,12},{12,8},{9,1... | collective-permute-start | bytes 983048 | tf_op jit(solution)/shard_map/ppermute | solution.py:27
  94.1 10.8 %collective-permute-start.26 = (bf16[64,1280]{1,0:T(8,128)(2,1)S(1)}, bf16[64,1280]{1,0:T(8,128)(2,1)S(1)}, u32[]{:S(2)}, u32[]{:S(2)}) collective-permute-start(bf16[64,1280]{1,0:T(8,128)(2,1)S(1)} %get-tuple-element.214.refs_0_), channel_id=1, source_target_pairs={{0,2},{1,3},{2,0},{3,1},{4,6},{5,7},{6,4},{7,5},{8,10},{9,11},{10,... | collective-permute-start | bytes 491528 | tf_op jit(solution)/shard_map/ppermute | solution.py:22
  97.4 14.1 %collective-permute-start.25 = (bf16[128,1280]{1,0:T(8,128)(2,1)S(1)}, bf16[128,1280]{1,0:T(8,128)(2,1)S(1)}, u32[]{:S(2)}, u32[]{:S(2)}) collective-permute-start(bf16[128,1280]{1,0:T(8,128)(2,1)S(1)} %get-tuple-element.211), channel_id=1, source_target_pairs={{8,0},{16,8},{24,16},{9,1},{17,9},{25,17},{10,2},{18,10},{26,18},{... | collective-permute-start | bytes 983048 | tf_op jit(solution)/shard_map/ppermute | solution.py:32
  100.3 7.5 %collective-permute-start.28 = (bf16[640,128]{1,0:T(8,128)(2,1)S(1)}, bf16[640,128]{1,0:T(8,128)(2,1)S(1)}, u32[]{:S(2)}, u32[]{:S(2)}) collective-permute-start(bf16[640,128]{1,0:T(8,128)(2,1)S(1)} %get-tuple-element.218.refs_2_.refs_9_), channel_id=1, source_target_pairs={{0,4},{4,0},{1,5},{5,1},{2,6},{6,2},{3,7},{7,3},{8,12},{12,8},{9,1... | collective-permute-start | bytes 491528 | tf_op jit(solution)/shard_map/ppermute | solution.py:27
  116.5 12.6 %collective-permute-start.32 = (bf16[64,1280]{1,0:T(8,128)(2,1)S(1)}, bf16[64,1280]{1,0:T(8,128)(2,1)S(1)}, u32[]{:S(2)}, u32[]{:S(2)}) collective-permute-start(bf16[64,1280]{1,0:T(8,128)(2,1)S(1)} %get-tuple-element.231.refs_0_), channel_id=1, source_target_pairs={{0,2},{1,3},{2,0},{3,1},{4,6},{5,7},{6,4},{7,5},{8,10},{9,11},{10,... | collective-permute-start | bytes 491528 | tf_op jit(solution)/shard_map/ppermute | solution.py:22
  123.2 9.4 %collective-permute-start.35 = (bf16[64,1280]{1,0:T(8,128)(2,1)S(1)}, bf16[64,1280]{1,0:T(8,128)(2,1)S(1)}, u32[]{:S(2)}, u32[]{:S(2)}) collective-permute-start(bf16[64,1280]{1,0:T(8,128)(2,1)S(1)} %get-tuple-element.246), channel_id=1, source_target_pairs={{0,1},{1,0},{2,3},{3,2},{4,5},{5,4},{6,7},{7,6},{8,9},{9,8},{10,11... | collective-permute-start | bytes 491528 | tf_op jit(solution)/shard_map/ppermute | solution.py:22
  124.4 17.9 %collective-permute-start.40 = (bf16[128,1280]{1,0:T(8,128)(2,1)S(1)}, bf16[128,1280]{1,0:T(8,128)(2,1)S(1)}, u32[]{:S(2)}, u32[]{:S(2)}) collective-permute-start(bf16[128,1280]{1,0:T(8,128)(2,1)S(1)} %get-tuple-element.260.refs_3_), channel_id=1, source_target_pairs={{0,4},{4,0},{1,5},{5,1},{2,6},{6,2},{3,7},{7,3},{8,12},{12,8},{9,1... | collective-permute-start | bytes 983048 | tf_op jit(solution)/shard_map/ppermute | solution.py:27
  125.7 18.8 %collective-permute-start.38 = (bf16[128,1280]{1,0:T(8,128)(2,1)S(1)}, bf16[128,1280]{1,0:T(8,128)(2,1)S(1)}, u32[]{:S(2)}, u32[]{:S(2)}) collective-permute-start(bf16[128,1280]{1,0:T(8,128)(2,1)S(1)} %get-tuple-element.258), channel_id=1, source_target_pairs={{0,4},{4,0},{1,5},{5,1},{2,6},{6,2},{3,7},{7,3},{8,12},{12,8},{9,1... | collective-permute-start | bytes 983048 | tf_op jit(solution)/shard_map/ppermute | solution.py:27
  127.1 20.7 %collective-permute-start.39 = (bf16[1280,128]{1,0:T(8,128)(2,1)S(1)}, bf16[1280,128]{1,0:T(8,128)(2,1)S(1)}, u32[]{:S(2)}, u32[]{:S(2)}) collective-permute-start(bf16[1280,128]{1,0:T(8,128)(2,1)S(1)} %get-tuple-element.259.refs_6_), channel_id=1, source_target_pairs={{0,4},{4,0},{1,5},{5,1},{2,6},{6,2},{3,7},{7,3},{8,12},{12,8},{9,1... | collective-permute-start | bytes 983048 | tf_op jit(solution)/shard_map/ppermute | solution.py:27
  132.6 9.5 %collective-permute-start.36 = (bf16[64,1280]{1,0:T(8,128)(2,1)S(1)}, bf16[64,1280]{1,0:T(8,128)(2,1)S(1)}, u32[]{:S(2)}, u32[]{:S(2)}) collective-permute-start(bf16[64,1280]{1,0:T(8,128)(2,1)S(1)} %get-tuple-element.253.refs_0_), channel_id=1, source_target_pairs={{0,2},{1,3},{2,0},{3,1},{4,6},{5,7},{6,4},{7,5},{8,10},{9,11},{10,... | collective-permute-start | bytes 491528 | tf_op jit(solution)/shard_map/ppermute | solution.py:22
  142.2 8.0 %collective-permute-start.37 = (bf16[64,1280]{1,0:T(8,128)(2,1)S(1)}, bf16[64,1280]{1,0:T(8,128)(2,1)S(1)}, u32[]{:S(2)}, u32[]{:S(2)}) collective-permute-start(bf16[64,1280]{1,0:T(8,128)(2,1)S(1)} %get-tuple-element.255.refs_6_), channel_id=1, source_target_pairs={{0,1},{1,0},{2,3},{3,2},{4,5},{5,4},{6,7},{7,6},{8,9},{9,8},{10,11... | collective-permute-start | bytes 491528 | tf_op jit(solution)/shard_map/ppermute | solution.py:22
  (22 other events, 185.5 us)

commit v3 on v2

--- a/solution.py
+++ b/solution.py
@@ -40,10 +40,13 @@
     return back_a_block(shard), lax.ppermute(shard, ("section", "tp"), crossed)
 
 
-def call(body, outs, ins, scratch=(), token=None, aliases=(), after=()):
+def call(body, outs, ins, scratch=(), token=None, aliases=(), after=(), passed=()):
     spaces = {"vmem": pltpu.VMEM, "smem": pltpu.SMEM, "any": pl.ANY, "hbm": pl.ANY, "kept": pltpu.VMEM}
     ins, outs = list(ins), list(outs)
     n_ins, n_outs = len(ins), len(outs)
+    aliases = list(aliases) + [(n_ins + i, n_outs + i) for i in range(len(passed))]
+    ins += [(a, "any") for a in passed]
+    outs += [(a.shape, a.dtype, "any") for a in passed]
     ins += [(a, "any") for a in after]
     if token is not None:
         ins.append((token, "any"))
@@ -52,7 +55,7 @@
     def without_tokens(*refs):
         first = refs[:n_ins]
         rest = refs[len(ins) :]
-        body(*first, *rest[:n_outs], *rest[n_outs + 1 :])
+        body(*first, *rest[:n_outs], *rest[len(outs) :])
 
     arrays = [
         pltpu.with_memory_space_constraint(a, pltpu.HBM) if where == "hbm" else a for a, where in ins
@@ -122,7 +125,7 @@
     if keep_ref is None:
         for number, part in enumerate(parts):
             message[:, number * width : (number + 1) * width] = part
-        return 2 * width
+        return len(parts) * width
     half = width // 2
     for number, part in enumerate(parts):
         at = slice(number * half, (number + 1) * half)
@@ -137,12 +140,12 @@
             keep_ref[:, at] = part[:, half:]
             message[:, at] = part[:, :half]
 
-    return width
+    return len(parts) * half
 
 
 def start_all(copies):
-    for copy in copies:
-        copy.start()
+    for number, copy in enumerate(copies):
+        copy.start(priority=number % 2)
     return copies
 
 
@@ -163,10 +166,16 @@
     return [slice(at, min(at + size, width)) for at in range(0, width, size)]
 
 
+def after_left(message, hidden_width):
+    return message.at[:, message.shape[1] - hidden_width :]
+
+
 def mlp_first_kernel(
-    flags, gains, streams, w_up, w_down, normed_ref, hidden_ref, slope_ref, send, keep, unit_ref, inv_ref,
-    upper, grad_lower, up_here, down_here, gains_here, sems, whole,
+    flags, gains, streams, w_up, w_down, message, slope_ref, send, keep, unit_ref, inv_ref, upper, grad_lower,
+    up_here, down_here, *refs,
 ):
+    keep_left = refs[0] if len(refs) == 5 else None
+    gains_here, normed_ref, sems, whole = refs[-4:]
     up_cut, down_cut = row_chunks(up_here.shape[1], CHUNKS), row_chunks(down_here.shape[1], CHUNKS)
     firsts = start_all(
         [
@@ -194,34 +203,38 @@
     normed_ref[...] = (unit * gains_here[1:2]).astype(BF16)
     unit_ref[...] = unit
     inv_ref[...] = jnp.broadcast_to(inv_std, inv_ref.shape)
+    store_lefts([normed_ref[...]], keep_left, message, flags[2])
     pre = None
     for i, at in enumerate(up_cut):
         ups[i].wait()
         part = dot(normed_ref[:, at], up_here[0, at])
         pre = part if pre is None else pre + part
-    after_mlp_up(pre, hidden_ref, slope_ref, slice(None))
+    hidden = after_left(message, slope_ref.shape[1])
+    after_mlp_up(pre, hidden, slope_ref, slice(None))
     for i, at in enumerate(down_cut):
         downs[i].wait()
-        whole[:, at] = dot_t(hidden_ref[...], down_here[0, at])
+        whole[:, at] = dot_t(hidden[...], down_here[0, at])
     split(whole, flags[0], send, keep)
     last.wait()
 
 
 def mlp_forward_kernel(
-    flags, gains, own, got, head, w_up, w_down, normed_ref, hidden_ref, slope_ref, send, keep, unit_ref, inv_ref,
-    upper_ref, whole,
+    flags, gains, own, got, head, w_up, w_down, message, slope_ref, send, keep, unit_ref, inv_ref, upper_ref, *refs
 ):
+    keep_left = refs[0] if len(refs) == 2 else None
+    whole = refs[-1]
     upper = jnp.where(flags[1] == 1, head[0], join(own, got, flags[0], whole))
     upper_ref[...] = upper
     unit, inv_std = unit_norm(upper)
     normed = (unit * gains[1:2]).astype(BF16)
-    for at in column_blocks(hidden_ref.shape[1], BLOCK):
-        after_mlp_up(dot(normed, w_up[0, :, at]), hidden_ref, slope_ref, at)
-    whole[...] = dot_t(hidden_ref[...], w_down[0])
+    hidden = after_left(message, slope_ref.shape[1])
+    for at in column_blocks(slope_ref.shape[1], BLOCK):
+        after_mlp_up(dot(normed, w_up[0, :, at]), hidden, slope_ref, at)
+    whole[...] = dot_t(hidden[...], w_down[0])
     split(whole, flags[0], send, keep)
-    normed_ref[...] = normed
     unit_ref[...] = unit
     inv_ref[...] = jnp.broadcast_to(inv_std, inv_ref.shape)
+    store_lefts([normed], keep_left, message, flags[2])
 
 
 def mlp_backward_kernel(later, flags, *refs):
@@ -230,38 +243,30 @@
         refs = refs[3:]
     else:
         grad_lower_ref, refs = refs[0], refs[1:]
-    slope, w_up, w_down, grad_pre_ref, send, keep = refs[:6]
+    slope, w_up, w_down, message, send, keep = refs[:6]
     whole = refs[-1]
+    refs = refs[6:-1]
     if later:
-        grad_lower_ref = refs[6]
+        grad_lower_ref, refs = refs[0], refs[1:]
         grad_lower = jnp.where(flags[1] == 1, head[3], join(own, got, flags[0], whole))
         grad_lower_ref[...] = grad_lower
     else:
         grad_lower = grad_lower_ref[...]
     grad_low = grad_lower.astype(BF16)
-    for at in column_blocks(grad_pre_ref.shape[1], BLOCK):
-        grad_pre_ref[:, at] = (dot(grad_low, w_down[0, :, at]) * slope[:, at]).astype(BF16)
-    whole[...] = dot_t(grad_pre_ref[...], w_up[0])
+    grad_pre = after_left(message, slope.shape[1])
+    for at in column_blocks(slope.shape[1], BLOCK):
+        grad_pre[:, at] = (dot(grad_low, w_down[0, :, at]) * slope[:, at]).astype(BF16)
+    whole[...] = dot_t(grad_pre[...], w_up[0])
     split(whole, flags[0], send, keep)
+    store_lefts([grad_low], refs[0] if refs else None, message, flags[2])
 
 
 def pack_kernel(two, flags, first, second, *refs):
-    if two:
-        keep_left, message, rights = refs[-1], refs[-2], refs[:-2]
-    else:
-        keep_left, message, rights = None, refs[-1], refs[:-1]
-    at = store_lefts([first[...], second[...].astype(BF16)], keep_left, message, flags[2])
-    for ref in rights:
-        message[:, at : at + ref.shape[1]] = ref[...]
-        at += ref.shape[1]
+    store_lefts([first[...], second[...]], refs[1] if two else None, refs[0], flags[2])
 
 
 def add_kernel(left, right, out):
     out[...] = (left[...].astype(F32) + right[...].astype(F32)).astype(BF16)
-
-
-def add_pass_kernel(left, right, unused, out, unused_out):
-    add_kernel(left, right, out)
 
 
 def project_kernel(later, flags, gains, *refs):
@@ -292,17 +297,16 @@
     query, kv = refs[0], refs[1 : 2 + others]
     w_out, probs_ref, mixed_ref, send, keep, whole = refs[2 + others :]
     local = query.shape[0]
-    for head in range(local // HEAD_DIM):
-        at = slice(head * HEAD_DIM, (head + 1) * HEAD_DIM)
-        at_value = slice(local + head * HEAD_DIM, local + (head + 1) * HEAD_DIM)
-        keys = jnp.concatenate([ref[at, :] for ref in kv], 1)
-        values = jnp.concatenate([ref[at_value, :] for ref in kv], 1)
-        scores = t_dot(keys, query[at, :]) * 0.125
-        top = jnp.max(scores, 0, keepdims=True)
-        weights = jnp.exp(scores - top)
-        probs = weights * (1.0 / jnp.sum(weights, 0, keepdims=True))
-        probs_ref[head] = probs
-        mixed_ref[at, :] = dot(values, probs.astype(BF16)).astype(BF16)
+    heads = [slice(at, at + HEAD_DIM) for at in range(0, local, HEAD_DIM)]
+    keys = jnp.concatenate([ref[:local, :] for ref in kv], 1)
+    values = jnp.concatenate([ref[local:, :] for ref in kv], 1)
+    scores = [t_dot(keys[at], query[at, :]) * 0.125 for at in heads]
+    weights = [jnp.exp(part - jnp.max(part, 0, keepdims=True)) for part in scores]
+    probs = [part * (1.0 / jnp.sum(part, 0, keepdims=True)) for part in weights]
+    mixed = [dot(values[at], part.astype(BF16)).astype(BF16) for at, part in zip(heads, probs)]
+    for head, at in enumerate(heads):
+        probs_ref[head] = probs[head]
+        mixed_ref[at, :] = mixed[head]
     whole[...] = t_dot(mixed_ref[...], w_out[...])
     split(whole, flags[0], send, keep)
 
@@ -325,36 +329,34 @@
     total_low = total.astype(BF16)
     grad_mixed = dot_t(w_out[...], total_low).astype(BF16)
     local, rows = query.shape
-    for head in range(local // HEAD_DIM):
-        at = slice(head * HEAD_DIM, (head + 1) * HEAD_DIM)
-        at_value = slice(local + head * HEAD_DIM, local + (head + 1) * HEAD_DIM)
-        keys = jnp.concatenate([ref[at, :] for ref in kv], 1)
-        values = jnp.concatenate([ref[at_value, :] for ref in kv], 1)
-        probs = probs_ref[head]
-        grad_head = grad_mixed[at, :]
-        grad_probs = t_dot(values, grad_head)
-        delta = jnp.sum(probs * grad_probs, 0, keepdims=True)
-        grad_scores = (probs * (grad_probs - delta)).astype(BF16)
-        grad_query[at, :] = (0.125 * dot(keys, grad_scores)).astype(BF16)
-        grad_keys = 0.125 * dot_t(query[at, :], grad_scores)
-        grad_values = dot_t(grad_head, probs.astype(BF16))
-        kv_own[at, :] = grad_keys[:, :rows]
-        kv_own[at_value, :] = grad_values[:, :rows]
+    heads = [slice(at, at + HEAD_DIM) for at in range(0, local, HEAD_DIM)]
+    keys = jnp.concatenate([ref[:local, :] for ref in kv], 1)
+    values = jnp.concatenate([ref[local:, :] for ref in kv], 1)
+    probs = [probs_ref[head] for head in range(len(heads))]
+    grad_probs = [t_dot(values[at], grad_mixed[at]) for at in heads]
+    grad_scores = [
+        (p * (g - jnp.sum(p * g, 0, keepdims=True))).astype(BF16) for p, g in zip(probs, grad_probs)
+    ]
+    grad_values = [dot_t(grad_mixed[at], p.astype(BF16)) for at, p in zip(heads, probs)]
+    grad_keys = [0.125 * dot_t(query[at, :], g) for at, g in zip(heads, grad_scores)]
+    for head, at in enumerate(heads):
+        at_value = slice(local + at.start, local + at.stop)
+        kv_own[at, :] = grad_keys[head][:, :rows]
+        kv_own[at_value, :] = grad_values[head][:, :rows]
         for number, ref in enumerate(kv_sent):
             cols = slice((number + 1) * rows, (number + 2) * rows)
-            ref[at, :] = grad_keys[:, cols].astype(BF16)
-            ref[at_value, :] = grad_values[:, cols].astype(BF16)
+            ref[at, :] = grad_keys[head][:, cols].astype(BF16)
+            ref[at_value, :] = grad_values[head][:, cols].astype(BF16)
+        grad_query[at, :] = (0.125 * dot(keys[at], grad_scores[head])).astype(BF16)
     total_low_ref[...] = total_low
     for ref in totals:
         ref[...] = total
 
 
-def project_back_kernel(others, passed, flags, *refs):
+def project_back_kernel(others, flags, *refs):
     grad_query, kv_own = refs[:2]
     kv_got = refs[2 : 2 + others]
-    mixed, w_qkv = refs[2 + others : 4 + others]
-    rights, send, keep = refs[4 + others + passed : 7 + others + passed]
-    whole = refs[-1]
+    mixed, w_qkv, rights, send, keep, whole = refs[2 + others :]
     local = mixed.shape[0]
     total = kv_own[...]
     for ref in kv_got:
@@ -421,7 +423,7 @@
         to[...] = dot(right[at], left).astype(BF16)
 
 
-def send_message(keep, message, width):
+def send_message(keep, message, width, count):
     length = lax.axis_size("seq")
     if keep is not None:
         return [keep, shift(message, "seq", 1)]
@@ -429,14 +431,11 @@
     cut = width // length
 
     def at(index):
-        return jnp.concatenate(
-            [
-                lax.dynamic_slice_in_dim(message[:, :width], index * cut, cut, 1),
-                lax.dynamic_slice_in_dim(message[:, width : 2 * width], index * cut, cut, 1),
-                message[:, 2 * width :],
-            ],
-            1,
-        )
+        lefts = [
+            lax.dynamic_slice_in_dim(message[:, i * width : (i + 1) * width], index * cut, cut, 1)
+            for i in range(count)
+        ]
+        return jnp.concatenate(lefts + [message[:, count * width :]], 1)
 
     return [at(place)] + [
         shift(at((place + by) % length), "seq", by) for by in range(1, length)
@@ -468,17 +467,19 @@
     half_low = halves[0]
     two = n_seq == 2
 
-    def pack(first, second, *rights, **more):
-        size = width * (1 if two else 2) + sum(right.shape[1] for right in rights)
+    left_size = width // 2 if two else width
+
+    def pack(first, second, **more):
         got = run(
             functools.partial(pack_kernel, two),
-            [((rows, size), BF16, "vmem")] + [low] * two,
-            [flag] + here(first, second, *rights),
+            [((rows, 2 * left_size), BF16, "vmem")] + [low] * two,
+            [flag] + here(first, second),
             **more,
         )
         return (got[1] if two else None), got[0]
 
-    hid_low = ((rows, hidden_width), BF16, "vmem")
+    message_outs = [((rows, left_size + hidden_width), BF16, "vmem")]
+    keep_outs = [((rows, left_size), BF16, "vmem")] * two
     hid_full = ((rows, hidden_width), F32, "vmem")
     token = None
 
@@ -497,92 +498,85 @@
             by *= 2
         return total, (swap(total, "tp", by) if by < lax.axis_size("tp") else None)
 
-    def add(left, right):
+    def add(left, right, **more):
         if right is None:
             return left
-        return run(add_kernel, [half_low], here(left, right))[0]
+        return run(add_kernel, [half_low], here(left, right), **more)[0]
 
     def zero_if_none(got, like):
         return jnp.zeros_like(like) if got is None else got
-
-    def add_pass(left, right, passed, **more):
-        if right is None:
-            return left, passed
-        return run(
-            add_pass_kernel,
-            [half_low, (passed.shape, passed.dtype, "any")],
-            here(left, right) + [(passed, "any")],
-            aliases=[(2, 1)],
-            **more,
-        )
 
     norm_outs = [full, ((rows, 128), F32, "vmem")]
     cut = width // n_seq
     left_width = 2 * cut
     for tick in range(2):
         later = tick > 0
-        mlp_outs = [low, hid_low, hid_full] + halves + norm_outs
+        mlp_outs = message_outs + [hid_full] + halves + norm_outs
         if later:
-            normed, hidden, slope, send_f, keep_f, unit_up, inv_up, upper = run(
+            got = run(
                 mlp_forward_kernel,
-                mlp_outs + [full],
+                mlp_outs + [full] + keep_outs,
                 [flag, gain] + here(own_upper, got_upper, head_streams, up_here, down_here),
                 [whole],
             )
+            message, slope, send_f, keep_f, unit_up, inv_up, upper = got[:7]
             got_f = swap(send_f, "tp", 1)
-            hidden_2 = send_whole(hidden)
+            message_2, factors_2 = message, send_message(got[7] if two else None, message, width, 1)
             (next_grad,) = run(
                 lower_boundary_kernel,
                 [half_low],
                 [flag, gain] + here(unit_att, inv_att, grad_lower, sum_b, zero_if_none(got_b, sum_b)),
             )
             own_grad, got_grad = back_to_pair(next_grad)
-            sum_f, lower_low = add_pass(keep_f, got_f, lower_low)
-            next_lower = back_a_block(lower_low)
+            sum_f, lower_low, total_low = run(
+                add_kernel, [half_low], here(keep_f, got_f), passed=[lower_low, total_low]
+            )
+            next_lower, next_total = back_a_block(lower_low), back_a_block(total_low)
             sum_f, got_f = middle_adds(sum_f)
             source = here(own_grad, got_grad, head_streams)
         else:
             got = run(
                 mlp_first_kernel,
-                mlp_outs + [full, full] + [(w.shape, BF16, "kept") for w in (w_up, w_down)],
+                mlp_outs + [full, full] + [(w.shape, BF16, "kept") for w in (w_up, w_down)] + keep_outs,
                 [flag] + [(a, "hbm") for a in (gains, streams, w_up, w_down)],
                 [
                     pltpu.VMEM(gains.shape, F32),
+                    pltpu.VMEM((rows, width), BF16),
                     pltpu.SemaphoreType.DMA((3 + 2 * CHUNKS,)),
                     whole,
                 ],
             )
-            normed, hidden, slope, send_f, keep_f, unit_up, inv_up, upper, grad_lower = got[:9]
-            up_here, down_here = got[9:]
+            message, slope, send_f, keep_f, unit_up, inv_up, upper, grad_lower = got[:8]
+            up_here, down_here = got[8:10]
             got_f = swap(send_f, "tp", 1)
-            hidden_1 = send_whole(hidden)
+            message_0, factors_0 = message, send_message(got[10] if two else None, message, width, 1)
             source = here(grad_lower)
         got = run(
             functools.partial(mlp_backward_kernel, later),
-            [hid_low] + halves + [full] * later,
+            message_outs + halves + [full] * later + keep_outs,
             [flag] + source + here(slope, up_here, down_here),
             [whole],
+            after=rights_1[1:] + lefts_1[1:] if later else (),
         )
-        grad_pre, send_b, keep_b = got[:3]
+        message, send_b, keep_b = got[:3]
+        keep_left = got[-1] if two else None
         if later:
             grad_lower = got[3]
         got_b = swap(send_b, "tp", 1)
         if later:
-            own_out, total_low = add_pass(sum_f, got_f, total_low, after=rights_1[1:])
+            message_3, factors_3 = message, send_message(keep_left, message, width, 1)
+            own_out = add(sum_f, got_f)
             got_out = swap(own_out, "tp", 1)
-            next_total = back_a_block(total_low)
-            factors_3 = send_message(*pack(normed, grad_lower), width)
             (sum_b,) = run(add_kernel, [half_low], here(keep_b, got_b))
             sum_b, got_b = middle_adds(sum_b)
         else:
             (sum_f,) = run(add_kernel, [half_low], here(keep_f, got_f))
             sum_f, got_f = middle_adds(sum_f)
-            factors_0 = send_message(*pack(normed, grad_lower), width)
+            message_1, factors_1 = message, send_message(keep_left, message, width, 1)
             own_out = add(sum_f, got_f)
             got_out = swap(own_out, "tp", 1)
-            (sum_b,) = run(add_kernel, [half_low], here(keep_b, got_b), after=hidden_1[1:])
+            (sum_b,) = run(add_kernel, [half_low], here(keep_b, got_b), after=())
             sum_b, got_b = middle_adds(sum_b)
-            grad_pre_1 = grad_pre
 
         source = here(next_lower, head_streams) if later else here(streams)
         got = run(
@@ -592,13 +586,13 @@
             + [low] * (not later),
             [flag, gain] + source + here(own_out, got_out, w_qkv_t),
             [whole],
-            after=factors_1[1:] if later else factors_0[1:],
+            after=() if later else factors_0[1:],
         )
         lower_in, att_low, query, kv, unit_att, inv_att = got[:6]
         if not later:
             lower_low = got[6]
         all_kv = [kv] + [shift(kv, "seq", -by) for by in range(1, n_seq)]
-        own_normed = add(sum_b, got_b)
+        own_normed = add(sum_b, got_b, after=() if later else ())
         got_normed = swap(own_normed, "tp", 1)
         probs, mixed, send_f, keep_f = run(
             functools.partial(attend_kernel, others),
@@ -606,7 +600,7 @@
             + halves,
             [flag] + here(query, *all_kv, w_out_t),
             [whole],
-            after=hidden_2[1:] + factors_3[1:] if later else (),
+            after=factors_2[1:] if later else factors_1[1:],
         )
         got_f = swap(send_f, "tp", 1)
 
@@ -622,28 +616,25 @@
         )
         total_low, grad_query, kv_own = got[:3]
         kv_got = [shift(part, "seq", by + 1) for by, part in enumerate(got[3 : 3 + others])]
-        (sum_f,) = run(add_kernel, [half_low], here(keep_f, got_f))
+        (sum_f,) = run(add_kernel, [half_low], here(keep_f, got_f), after=factors_3[1:] if later else ())
         sum_f, got_f = middle_adds(sum_f)
         if later:
             recon_out = [((1, 4, rows, width), F32, "any")]
             (recon,) = run(
                 recon_middle_kernel, recon_out, here(lower_in, got[-1]), [pltpu.SemaphoreType.DMA((2,))]
             )
-        got = run(
-            functools.partial(project_back_kernel, others, int(later)),
-            [((4 * local, rows), BF16, "vmem")] + halves + [(grad_pre.shape, BF16, "any")] * later,
-            [flag] + here(grad_query, kv_own, *kv_got, mixed, w_qkv_t) + [(grad_pre, "any")] * later,
+        rights, send_b, keep_b = run(
+            functools.partial(project_back_kernel, others),
+            [((4 * local, rows), BF16, "vmem")] + halves,
+            [flag] + here(grad_query, kv_own, *kv_got, mixed, w_qkv_t),
             [whole],
-            aliases=[(5 + others, 3)] * later,
         )
-        rights, send_b, keep_b = got[:3]
         got_b = swap(send_b, "tp", 1)
         rights_att = send_whole(rights)
 
         if later:
             rights_2 = rights_att
-            grad_pre_2 = send_whole(got[3])
-            factors_2 = send_message(*pack(att_low, total_low), width)
+            lefts_2 = send_message(*pack(att_low, total_low), width, 2)
             own_f = add(sum_f, got_f)
             got_f = swap(own_f, "tp", 1)
             (sum_b,) = run(add_kernel, [half_low], here(keep_b, got_b))
@@ -658,13 +649,18 @@
             (sum_b,) = run(add_kernel, [half_low], here(keep_b, got_b))
             sum_b, got_b = middle_adds(sum_b)
             own_upper, got_upper = back_to_pair(next_half)
-            factors_1 = send_message(*pack(att_low, total_low, grad_pre), width)
-
-    ups = [(factors_0[0], 0, grad_pre_1, 0), (factors_3[0], 0, grad_pre_2[0], 0)]
-    downs = [(factors_0[0], cut, hidden_1[0], 0), (factors_3[0], cut, hidden_2[0], 0)]
-    for i in range(1, n_seq):
-        ups += [(factors_0[i], 0, factors_1[i], left_width), (factors_3[i], 0, grad_pre_2[i], 0)]
-        downs += [(factors_0[i], cut, hidden_1[i], 0), (factors_3[i], cut, hidden_2[i], 0)]
+            lefts_1 = send_message(*pack(att_low, total_low, after=[own_upper]), width, 2)
+
+    ups, downs = [], []
+    for up, down, mine_up, mine_down in (
+        (factors_0, factors_1, message_1, message_0),
+        (factors_2, factors_3, message_3, message_2),
+    ):
+        ups.append((up[0], 0, mine_up, left_size))
+        downs.append((down[0], 0, mine_down, left_size))
+        for i in range(1, n_seq):
+            ups.append((up[i], 0, down[i], cut))
+            downs.append((down[i], 0, up[i], cut))
 
     def mlp_grad(terms):
         if not two:
@@ -693,10 +689,10 @@
         [whole, one_sem, whole],
         aliases=[(1, 0)],
     )
+    grad_up = mlp_grad(ups)
     own_b = add(sum_b, got_b)
     got_b = swap(own_b, "tp", 1)
-    grad_up = mlp_grad(ups)
-    lefts_att, rights_att = factors_1 + factors_2, rights_1 + rights_2
+    lefts_att, rights_att = lefts_1 + lefts_2, rights_1 + rights_2
     if two:
         grad_qkv, grad_out = run(
             functools.partial(att_grad_kernel, len(rights_att)),

time: 152 us -> 145 us (0.954); the launches traced: 152 us -> 143 us
  Pallas kernels: 44.5 us -> 41 us
  waiting for transfers between devices: 48 us -> 44.9 us
  starting transfers between devices: 58.3 us -> 56.2 us
    ppermute x22, starting transfers between devices: 33.4 us -> 28.7 us  [swap(): return lax.ppermute(shard, axis, [(i, i ^ by) for i in range(length)])]
    ppermute x2, waiting for transfers between devices: 9.14 us -> 4.82 us  [back_to_pair(): lax.ppermute(shard, ('section', 'tp'), crossed)]
    ppermute x13 -> x12, waiting for transfers between devices: 8.67 us -> 12.2 us  [shift(): lax.ppermute(shard, axis, [(i, (i + by) % length) for i in range(length)])]
    pallas_call x38 -> x36, Pallas kernels: 44.5 us -> 41 us  [call(): pl.pallas_call(without_tokens, out_shape=[(pltpu.VMEM if where == 'kept'...]
    ppermute x13 -> x12, starting transfers between devices: 16.9 us -> 19.6 us  [shift(): lax.ppermute(shard, axis, [(i, (i + by) % length) for i in range(length)])]
    ppermute x4, waiting for transfers between devices: 1.55 us -> 0.01 us  [back_a_block(): lax.ppermute(shard, 'section', [(i, i - 1) for i in range(1, length)])]
  transfers between devices with their start and end apart: 41 -> 40, of which waited for: 23 -> 22; matrix products, arithmetic and copies ran while one was open for 0% -> 0% of each run, Pallas kernels for 24% -> 23%
where the time goes in v3:
time: 145 us; the launch traced here: 143 us
  starting transfers between devices  56.2 us (39%)
  waiting for transfers between devices  44.9 us (31%)
  Pallas kernels  41 us (28%)
    pallas_call x36, Pallas kernels, call(): pl.pallas_call(without_tokens, out_shape=[(pltpu.VMEM if where == 'kept'...  41 us
    ppermute x22, starting transfers between devices, swap(): return lax.ppermute(shard, axis, [(i, i ^ by) for i in range(length)])  28.7 us
    ppermute x22, waiting for transfers between devices, swap(): return lax.ppermute(shard, axis, [(i, i ^ by) for i in range(length)])  27.9 us
    ppermute x12, starting transfers between devices, shift(): lax.ppermute(shard, axis, [(i, (i + by) % length) for i in range(length)])  19.6 us
    ppermute x12, waiting for transfers between devices, shift(): lax.ppermute(shard, axis, [(i, (i + by) % length) for i in range(length)])  12.2 us
    ppermute x4, starting transfers between devices, back_a_block(): lax.ppermute(shard, 'section', [(i, i - 1) for i in range(1, length)])  5.33 us
    ppermute x2, waiting for transfers between devices, back_to_pair(): lax.ppermute(shard, ('section', 'tp'), crossed)  4.82 us
  transfers between devices with their start and end apart: 40, of which 22 were waited for; matrix products, arithmetic and copies ran while one was open for 0% of the time, Pallas kernels for 23%

profile of v3, /device:TPU:0, one launch (start us, length us, event | category | flops | bytes accessed | tf_op | source)
XLA Modules:
  0.0 143.4 jit_solution(13228436351155465693)
XLA Ops:
  0.7 6.8 %shard_map.110 = (bf16[128,1920]{1,0:T(8,128)(2,1)S(1)}, f32[128,1280]{1,0:T(8,128)S(1)}, bf16[64,1280]{1,0:T(8,128)(2,1)S(1)}, f32[64,1280]{1,0:T(8,128)S(1)}, ...) custom-call(s32[3]{0:T(128)S(1)} %pad_add_fusion.refs_0_, ...), custom_call_target="tpu_custom_call" | custom-call | flops 1024 | bytes 1024 | tf_op jit(solution)/shard_map/pallas_call | solution.py:63
  7.6 3.1 %collective-permute-start = (bf16[64,1280]{1,0:T(8,128)(2,1)S(1)}, bf16[64,1280]{1,0:T(8,128)(2,1)S(1)}, u32[]{:S(2)}, u32[]{:S(2)}) collective-permute-start(bf16[64,1280]{1,0:T(8,128)(2,1)S(1)} %get-tuple-element.134), channel_id=1, source_target_pairs={{0,1},{1,0},{2,3},{3,2},{4,5},{5,4},{6,7},{7,6},{8,9},{9,8},{10,11... | collective-permute-start | bytes 491528 | tf_op jit(solution)/shard_map/ppermute | solution.py:22
  14.9 2.8 %collective-permute-start.1 = (bf16[64,1280]{1,0:T(8,128)(2,1)S(1)}, bf16[64,1280]{1,0:T(8,128)(2,1)S(1)}, u32[]{:S(2)}, u32[]{:S(2)}) collective-permute-start(bf16[64,1280]{1,0:T(8,128)(2,1)S(1)} %get-tuple-element.141.refs_0_), channel_id=1, source_target_pairs={{0,2},{1,3},{2,0},{3,1},{4,6},{5,7},{6,4},{7,5},{8,10},{9,11},{10,... | collective-permute-start | bytes 491528 | tf_op jit(solution)/shard_map/ppermute | solution.py:22
  20.8 4.0 %collective-permute-done.1.refs_1_ = bf16[64,1280]{1,0:T(8,128)(2,1)S(1)} collective-permute-done((bf16[64,1280]{1,0:T(8,128)(2,1)S(1)}, bf16[64,1280]{1,0:T(8,128)(2,1)S(1)}, u32[]{:S(2)}, u32[]{:S(2)}) %collective-permute-start.1) | collective-permute-done | bytes 163872 | tf_op jit(solution)/shard_map/ppermute | solution.py:22
  26.4 2.5 %collective-permute-start.7 = (bf16[64,1280]{1,0:T(8,128)(2,1)S(1)}, bf16[64,1280]{1,0:T(8,128)(2,1)S(1)}, u32[]{:S(2)}, u32[]{:S(2)}) collective-permute-start(bf16[64,1280]{1,0:T(8,128)(2,1)S(1)} %get-tuple-element.152.refs_0_), channel_id=1, source_target_pairs={{0,2},{1,3},{2,0},{3,1},{4,6},{5,7},{6,4},{7,5},{8,10},{9,11},{10,... | collective-permute-start | bytes 491528 | tf_op jit(solution)/shard_map/ppermute | solution.py:22
  28.9 4.5 %collective-permute-done.2.refs_4_ = bf16[64,1280]{1,0:T(8,128)(2,1)S(1)} collective-permute-done((bf16[64,1280]{1,0:T(8,128)(2,1)S(1)}, bf16[64,1280]{1,0:T(8,128)(2,1)S(1)}, u32[]{:S(2)}, u32[]{:S(2)}) %collective-permute-start.2) | collective-permute-done | bytes 163872 | tf_op jit(solution)/shard_map/ppermute | solution.py:22
  36.7 3.8 %collective-permute-done.5.refs_3_.refs_9_ = bf16[640,128]{1,0:T(8,128)(2,1)S(1)} collective-permute-done((bf16[640,128]{1,0:T(8,128)(2,1)S(1)}, bf16[640,128]{1,0:T(8,128)(2,1)S(1)}, u32[]{:S(2)}, u32[]{:S(2)}) %collective-permute-start.5) | collective-permute-done | bytes 163872 | tf_op jit(solution)/shard_map/ppermute | solution.py:27
  48.6 2.3 %collective-permute-done.11.refs_3_ = bf16[640,128]{1,0:T(8,128)(2,1)S(1)} collective-permute-done((bf16[640,128]{1,0:T(8,128)(2,1)S(1)}, bf16[640,128]{1,0:T(8,128)(2,1)S(1)}, u32[]{:S(2)}, u32[]{:S(2)}) %collective-permute-start.11) | collective-permute-done | bytes 163872 | tf_op jit(solution)/shard_map/ppermute | solution.py:27
  52.8 2.6 %collective-permute-done.10.refs_3_ = bf16[64,1280]{1,0:T(8,128)(2,1)S(1)} collective-permute-done((bf16[64,1280]{1,0:T(8,128)(2,1)S(1)}, bf16[64,1280]{1,0:T(8,128)(2,1)S(1)}, u32[]{:S(2)}, u32[]{:S(2)}) %collective-permute-start.10) | collective-permute-done | bytes 163872 | tf_op jit(solution)/shard_map/ppermute | solution.py:22
  61.5 2.4 %collective-permute-done.13.refs_3_ = bf16[64,1280]{1,0:T(8,128)(2,1)S(1)} collective-permute-done((bf16[64,1280]{1,0:T(8,128)(2,1)S(1)}, bf16[64,1280]{1,0:T(8,128)(2,1)S(1)}, u32[]{:S(2)}, u32[]{:S(2)}) %collective-permute-start.13) | collective-permute-done | bytes 163872 | tf_op jit(solution)/shard_map/ppermute | solution.py:40
  63.9 2.6 %shard_map.124 = (bf16[128,1920]{1,0:T(8,128)(2,1)S(1)}, f32[128,1280]{1,0:T(8,128)S(1)}, bf16[64,1280]{1,0:T(8,128)(2,1)S(1)}, f32[64,1280]{1,0:T(8,128)S(1)}, ...) custom-call(s32[3]{0:T(128)S(1)} %pad_add_fusion.refs_0_, ...), custom_call_target="tpu_custom_call" | custom-call | flops 1024 | bytes 1024 | tf_op jit(solution)/shard_map/pallas_call | solution.py:63
  66.6 2.6 %collective-permute-start.15 = (bf16[64,1280]{1,0:T(8,128)(2,1)S(1)}, bf16[64,1280]{1,0:T(8,128)(2,1)S(1)}, u32[]{:S(2)}, u32[]{:S(2)}) collective-permute-start(bf16[64,1280]{1,0:T(8,128)(2,1)S(1)} %get-tuple-element.179), channel_id=1, source_target_pairs={{0,1},{1,0},{2,3},{3,2},{4,5},{5,4},{6,7},{7,6},{8,9},{9,8},{10,11... | collective-permute-start | bytes 491528 | tf_op jit(solution)/shard_map/ppermute | solution.py:22
  78.3 2.4 %collective-permute-done.20.refs_2_ = bf16[64,1280]{1,0:T(8,128)(2,1)S(1)} collective-permute-done((bf16[64,1280]{1,0:T(8,128)(2,1)S(1)}, bf16[64,1280]{1,0:T(8,128)(2,1)S(1)}, u32[]{:S(2)}, u32[]{:S(2)}) %collective-permute-start.20) | collective-permute-done | bytes 163872 | tf_op jit(solution)/shard_map/ppermute | solution.py:40
  80.8 2.2 %shard_map.127 = (bf16[128,1920]{1,0:T(8,128)(2,1)S(1)}, bf16[64,1280]{1,0:T(8,128)(2,1)S(1)}, f32[64,1280]{1,0:T(8,128)S(1)}, f32[128,1280]{1,0:T(8,128)S(1)}, ...) custom-call(s32[3]{0:T(128)S(1)} %pad_add_fusion.refs_0_, bf16[64,1280]{1,0:T(8,128)(2,1)S(1)} %collective-permute-done.19.refs_1_, ...), custom_call_target="tpu_custom_call" | custom-call | flops 1024 | bytes 1024 | tf_op jit(solution)/shard_map/pallas_call | solution.py:63
  85.7 2.4 %collective-permute-start.31 = (bf16[128,1920]{1,0:T(8,128)(2,1)S(1)}, bf16[128,1920]{1,0:T(8,128)(2,1)S(1)}, u32[]{:S(2)}, u32[]{:S(2)}) collective-permute-start(bf16[128,1920]{1,0:T(8,128)(2,1)S(1)} %get-tuple-element.215.refs_5_), channel_id=1, source_target_pairs={{0,4},{4,0},{1,5},{5,1},{2,6},{6,2},{3,7},{7,3},{8,12},{12,8},{9,1... | collective-permute-start | bytes 1474568 | tf_op jit(solution)/shard_map/ppermute | solution.py:27
  88.4 2.5 %collective-permute-start.26 = (bf16[64,1280]{1,0:T(8,128)(2,1)S(1)}, bf16[64,1280]{1,0:T(8,128)(2,1)S(1)}, u32[]{:S(2)}, u32[]{:S(2)}) collective-permute-start(bf16[64,1280]{1,0:T(8,128)(2,1)S(1)} %get-tuple-element.203.refs_0_), channel_id=1, source_target_pairs={{0,2},{1,3},{2,0},{3,1},{4,6},{5,7},{6,4},{7,5},{8,10},{9,11},{10,... | collective-permute-start | bytes 491528 | tf_op jit(solution)/shard_map/ppermute | solution.py:22
  96.1 3.5 %collective-permute-start.27 = (bf16[64,1280]{1,0:T(8,128)(2,1)S(1)}, bf16[64,1280]{1,0:T(8,128)(2,1)S(1)}, u32[]{:S(2)}, u32[]{:S(2)}) collective-permute-start(bf16[64,1280]{1,0:T(8,128)(2,1)S(1)} %get-tuple-element.205.refs_6_), channel_id=1, source_target_pairs={{0,1},{1,0},{2,3},{3,2},{4,5},{5,4},{6,7},{7,6},{8,9},{9,8},{10,11... | collective-permute-start | bytes 491528 | tf_op jit(solution)/shard_map/ppermute | solution.py:22
  106.8 3.5 %collective-permute-start.33 = (bf16[640,128]{1,0:T(8,128)(2,1)S(1)}, bf16[640,128]{1,0:T(8,128)(2,1)S(1)}, u32[]{:S(2)}, u32[]{:S(2)}) collective-permute-start(bf16[640,128]{1,0:T(8,128)(2,1)S(1)} %get-tuple-element.225), channel_id=1, source_target_pairs={{0,4},{4,0},{1,5},{5,1},{2,6},{6,2},{3,7},{7,3},{8,12},{12,8},{9,1... | collective-permute-start | bytes 491528 | tf_op jit(solution)/shard_map/ppermute | solution.py:27
  112.7 2.5 %collective-permute-done.33.refs_3_ = bf16[640,128]{1,0:T(8,128)(2,1)S(1)} collective-permute-done((bf16[640,128]{1,0:T(8,128)(2,1)S(1)}, bf16[640,128]{1,0:T(8,128)(2,1)S(1)}, u32[]{:S(2)}, u32[]{:S(2)}) %collective-permute-start.33) | collective-permute-done | bytes 163872 | tf_op jit(solution)/shard_map/ppermute | solution.py:27
  117.1 4.2 %collective-permute-done.32.refs_1_ = bf16[64,1280]{1,0:T(8,128)(2,1)S(1)} collective-permute-done((bf16[64,1280]{1,0:T(8,128)(2,1)S(1)}, bf16[64,1280]{1,0:T(8,128)(2,1)S(1)}, u32[]{:S(2)}, u32[]{:S(2)}) %collective-permute-start.32) | collective-permute-done | bytes 163872 | tf_op jit(solution)/shard_map/ppermute | solution.py:22
  126.7 2.2 %shard_map.140 = (bf16[640,1280]{1,0:T(8,128)(2,1)}, f32[8,128]{1,0:T(8,128)S(1)}) custom-call(bf16[128,640]{1,0:T(8,128)(2,1)S(1)} %get-tuple-element.231.refs_0_, bf16[128,1920]{1,0:T(8,128)(2,1)S(1)} %get-tuple-element.144.refs_1_, bf16[128,1920]{1,0:T(8,128)(2,1)S(1)} %collective-permute-done.6.refs_5_.refs_2_.refs_3_, ...), custom_call_target="tpu_custom_call" | custom-call | flops 1024 | bytes 1024 | tf_op jit(solution)/shard_map/pallas_call | solution.py:63
  130.4 2.2 %shard_map.142 = (bf16[640,1280]{1,0:T(8,128)(2,1)}, f32[8,128]{1,0:T(8,128)S(1)}) custom-call(bf16[128,640]{1,0:T(8,128)(2,1)S(1)} %get-tuple-element.243.refs_0_, bf16[128,1920]{1,0:T(8,128)(2,1)S(1)} %get-tuple-element.151.refs_1_, bf16[128,1920]{1,0:T(8,128)(2,1)S(1)} %collective-permute-done.3.refs_6_.refs_3_.refs_2_, ...), custom_call_target="tpu_custom_call" | custom-call | flops 1024 | bytes 1024 | tf_op jit(solution)/shard_map/pallas_call | solution.py:63
  132.7 2.6 %collective-permute-done.36.refs_1_ = bf16[64,1280]{1,0:T(8,128)(2,1)S(1)} collective-permute-done((bf16[64,1280]{1,0:T(8,128)(2,1)S(1)}, bf16[64,1280]{1,0:T(8,128)(2,1)S(1)}, u32[]{:S(2)}, u32[]{:S(2)}) %collective-permute-start.36) | collective-permute-done | bytes 163872 | tf_op jit(solution)/shard_map/ppermute | solution.py:22
  137.5 2.4 %shard_map.144 = (bf16[960,640]{1,0:T(8,128)(2,1)}, bf16[320,640]{1,0:T(8,128)(2,1)}, f32[8,128]{1,0:T(8,128)S(1)}) custom-call(bf16[128,1280]{1,0:T(8,128)(2,1)S(1)} %get-tuple-element.248.refs_0_, bf16[128,1280]{1,0:T(8,128)(2,1)S(1)} %collective-permute-done.22.refs_8_.refs_1_, bf16[128,1280]{1,0:T(8,128)(2,1)S(1)} %get-tuple-element.249.refs_2_, ...), custom_call_target="tpu_custom_call" | custom-call | flops 1024 | bytes 1024 | tf_op jit(solution)/shard_map/pallas_call | solution.py:63
  (103 shorter events, 69.6 us)
Async XLA Ops:
  10.6 22.8 %collective-permute-start.3 = (bf16[128,1920]{1,0:T(8,128)(2,1)S(1)}, bf16[128,1920]{1,0:T(8,128)(2,1)S(1)}, u32[]{:S(2)}, u32[]{:S(2)}) collective-permute-start(bf16[128,1920]{1,0:T(8,128)(2,1)S(1)} %get-tuple-element.144.refs_1_), channel_id=1, source_target_pairs={{0,4},{4,0},{1,5},{5,1},{2,6},{6,2},{3,7},{7,3},{8,12},{12,8},{9,1... | collective-permute-start | bytes 1474568 | tf_op jit(solution)/shard_map/ppermute | solution.py:27
  14.9 9.9 %collective-permute-start.1 = (bf16[64,1280]{1,0:T(8,128)(2,1)S(1)}, bf16[64,1280]{1,0:T(8,128)(2,1)S(1)}, u32[]{:S(2)}, u32[]{:S(2)}) collective-permute-start(bf16[64,1280]{1,0:T(8,128)(2,1)S(1)} %get-tuple-element.141.refs_0_), channel_id=1, source_target_pairs={{0,2},{1,3},{2,0},{3,1},{4,6},{5,7},{6,4},{7,5},{8,10},{9,11},{10,... | collective-permute-start | bytes 491528 | tf_op jit(solution)/shard_map/ppermute | solution.py:22
  17.7 19.0 %collective-permute-start.6 = (bf16[128,1920]{1,0:T(8,128)(2,1)S(1)}, bf16[128,1920]{1,0:T(8,128)(2,1)S(1)}, u32[]{:S(2)}, u32[]{:S(2)}) collective-permute-start(bf16[128,1920]{1,0:T(8,128)(2,1)S(1)} %get-tuple-element.151.refs_1_), channel_id=1, source_target_pairs={{0,4},{4,0},{1,5},{5,1},{2,6},{6,2},{3,7},{7,3},{8,12},{12,8},{9,1... | collective-permute-start | bytes 1474568 | tf_op jit(solution)/shard_map/ppermute | solution.py:27
  24.9 8.6 %collective-permute-start.2 = (bf16[64,1280]{1,0:T(8,128)(2,1)S(1)}, bf16[64,1280]{1,0:T(8,128)(2,1)S(1)}, u32[]{:S(2)}, u32[]{:S(2)}) collective-permute-start(bf16[64,1280]{1,0:T(8,128)(2,1)S(1)} %get-tuple-element.143.refs_3_), channel_id=1, source_target_pairs={{0,1},{1,0},{2,3},{3,2},{4,5},{5,4},{6,7},{7,6},{8,9},{9,8},{10,11... | collective-permute-start | bytes 491528 | tf_op jit(solution)/shard_map/ppermute | solution.py:22
  26.4 9.9 %collective-permute-start.7 = (bf16[64,1280]{1,0:T(8,128)(2,1)S(1)}, bf16[64,1280]{1,0:T(8,128)(2,1)S(1)}, u32[]{:S(2)}, u32[]{:S(2)}) collective-permute-start(bf16[64,1280]{1,0:T(8,128)(2,1)S(1)} %get-tuple-element.152.refs_0_), channel_id=1, source_target_pairs={{0,2},{1,3},{2,0},{3,1},{4,6},{5,7},{6,4},{7,5},{8,10},{9,11},{10,... | collective-permute-start | bytes 491528 | tf_op jit(solution)/shard_map/ppermute | solution.py:22
  58.6 16.6 %collective-permute-start.21 = (bf16[1280,128]{1,0:T(8,128)(2,1)S(1)}, bf16[1280,128]{1,0:T(8,128)(2,1)S(1)}, u32[]{:S(2)}, u32[]{:S(2)}) collective-permute-start(bf16[1280,128]{1,0:T(8,128)(2,1)S(1)} %get-tuple-element.190.refs_4_), channel_id=1, source_target_pairs={{0,4},{4,0},{1,5},{5,1},{2,6},{6,2},{3,7},{7,3},{8,12},{12,8},{9,1... | collective-permute-start | bytes 983048 | tf_op jit(solution)/shard_map/ppermute | solution.py:27
  59.6 11.3 %collective-permute-start.16 = (bf16[64,1280]{1,0:T(8,128)(2,1)S(1)}, bf16[64,1280]{1,0:T(8,128)(2,1)S(1)}, u32[]{:S(2)}, u32[]{:S(2)}) collective-permute-start(bf16[64,1280]{1,0:T(8,128)(2,1)S(1)} %get-tuple-element.183.refs_5_), channel_id=1, source_target_pairs={{0,2},{1,3},{2,0},{3,1},{4,6},{5,7},{6,4},{7,5},{8,10},{9,11},{10,... | collective-permute-start | bytes 491528 | tf_op jit(solution)/shard_map/ppermute | solution.py:22
  60.5 20.2 %collective-permute-start.22 = (bf16[128,1280]{1,0:T(8,128)(2,1)S(1)}, bf16[128,1280]{1,0:T(8,128)(2,1)S(1)}, u32[]{:S(2)}, u32[]{:S(2)}) collective-permute-start(bf16[128,1280]{1,0:T(8,128)(2,1)S(1)} %get-tuple-element.191), channel_id=1, source_target_pairs={{0,4},{4,0},{1,5},{5,1},{2,6},{6,2},{3,7},{7,3},{8,12},{12,8},{9,1... | collective-permute-start | bytes 983048 | tf_op jit(solution)/shard_map/ppermute | solution.py:27
  66.6 7.7 %collective-permute-start.15 = (bf16[64,1280]{1,0:T(8,128)(2,1)S(1)}, bf16[64,1280]{1,0:T(8,128)(2,1)S(1)}, u32[]{:S(2)}, u32[]{:S(2)}) collective-permute-start(bf16[64,1280]{1,0:T(8,128)(2,1)S(1)} %get-tuple-element.179), channel_id=1, source_target_pairs={{0,1},{1,0},{2,3},{3,2},{4,5},{5,4},{6,7},{7,6},{8,9},{9,8},{10,11... | collective-permute-start | bytes 491528 | tf_op jit(solution)/shard_map/ppermute | solution.py:22
  73.0 7.8 %collective-permute-start.20 = (bf16[64,1280]{1,0:T(8,128)(2,1)S(1)}, bf16[64,1280]{1,0:T(8,128)(2,1)S(1)}, u32[]{:S(2)}, u32[]{:S(2)}) collective-permute-start(bf16[64,1280]{1,0:T(8,128)(2,1)S(1)} %get-tuple-element.188), channel_id=1, source_target_pairs={{8,1},{9,0},{10,3},{11,2},{16,9},{17,8},{18,11},{19,10},{24,17},{2... | collective-permute-start | bytes 491528 | tf_op jit(solution)/shard_map/ppermute | solution.py:40
  74.3 11.3 %collective-permute-start.18 = (bf16[64,1280]{1,0:T(8,128)(2,1)S(1)}, bf16[64,1280]{1,0:T(8,128)(2,1)S(1)}, u32[]{:S(2)}, u32[]{:S(2)}) collective-permute-start(bf16[64,1280]{1,0:T(8,128)(2,1)S(1)} %get-tuple-element.187.refs_0_), channel_id=1, source_target_pairs={{0,2},{1,3},{2,0},{3,1},{4,6},{5,7},{6,4},{7,5},{8,10},{9,11},{10,... | collective-permute-start | bytes 491528 | tf_op jit(solution)/shard_map/ppermute | solution.py:22
  75.2 24.5 %collective-permute-start.29 = (bf16[128,1920]{1,0:T(8,128)(2,1)S(1)}, bf16[128,1920]{1,0:T(8,128)(2,1)S(1)}, u32[]{:S(2)}, u32[]{:S(2)}) collective-permute-start(bf16[128,1920]{1,0:T(8,128)(2,1)S(1)} %get-tuple-element.208.refs_5_), channel_id=1, source_target_pairs={{0,4},{4,0},{1,5},{5,1},{2,6},{6,2},{3,7},{7,3},{8,12},{12,8},{9,1... | collective-permute-start | bytes 1474568 | tf_op jit(solution)/shard_map/ppermute | solution.py:27
  76.9 15.5 %collective-permute-start.17 = (bf16[128,1280]{1,0:T(8,128)(2,1)S(1)}, bf16[128,1280]{1,0:T(8,128)(2,1)S(1)}, u32[]{:S(2)}, u32[]{:S(2)}) collective-permute-start(bf16[128,1280]{1,0:T(8,128)(2,1)S(1)} %get-tuple-element.186), channel_id=1, source_target_pairs={{8,0},{16,8},{24,16},{9,1},{17,9},{25,17},{10,2},{18,10},{26,18},{... | collective-permute-start | bytes 983048 | tf_op jit(solution)/shard_map/ppermute | solution.py:32
  85.7 24.6 %collective-permute-start.31 = (bf16[128,1920]{1,0:T(8,128)(2,1)S(1)}, bf16[128,1920]{1,0:T(8,128)(2,1)S(1)}, u32[]{:S(2)}, u32[]{:S(2)}) collective-permute-start(bf16[128,1920]{1,0:T(8,128)(2,1)S(1)} %get-tuple-element.215.refs_5_), channel_id=1, source_target_pairs={{0,4},{4,0},{1,5},{5,1},{2,6},{6,2},{3,7},{7,3},{8,12},{12,8},{9,1... | collective-permute-start | bytes 1474568 | tf_op jit(solution)/shard_map/ppermute | solution.py:27
  88.4 7.7 %collective-permute-start.26 = (bf16[64,1280]{1,0:T(8,128)(2,1)S(1)}, bf16[64,1280]{1,0:T(8,128)(2,1)S(1)}, u32[]{:S(2)}, u32[]{:S(2)}) collective-permute-start(bf16[64,1280]{1,0:T(8,128)(2,1)S(1)} %get-tuple-element.203.refs_0_), channel_id=1, source_target_pairs={{0,2},{1,3},{2,0},{3,1},{4,6},{5,7},{6,4},{7,5},{8,10},{9,11},{10,... | collective-permute-start | bytes 491528 | tf_op jit(solution)/shard_map/ppermute | solution.py:22
  91.0 13.6 %collective-permute-start.25 = (bf16[128,1280]{1,0:T(8,128)(2,1)S(1)}, bf16[128,1280]{1,0:T(8,128)(2,1)S(1)}, u32[]{:S(2)}, u32[]{:S(2)}) collective-permute-start(bf16[128,1280]{1,0:T(8,128)(2,1)S(1)} %get-tuple-element.200), channel_id=1, source_target_pairs={{8,0},{16,8},{24,16},{9,1},{17,9},{25,17},{10,2},{18,10},{26,18},{... | collective-permute-start | bytes 983048 | tf_op jit(solution)/shard_map/ppermute | solution.py:32
  96.1 8.6 %collective-permute-start.27 = (bf16[64,1280]{1,0:T(8,128)(2,1)S(1)}, bf16[64,1280]{1,0:T(8,128)(2,1)S(1)}, u32[]{:S(2)}, u32[]{:S(2)}) collective-permute-start(bf16[64,1280]{1,0:T(8,128)(2,1)S(1)} %get-tuple-element.205.refs_6_), channel_id=1, source_target_pairs={{0,1},{1,0},{2,3},{3,2},{4,5},{5,4},{6,7},{7,6},{8,9},{9,8},{10,11... | collective-permute-start | bytes 491528 | tf_op jit(solution)/shard_map/ppermute | solution.py:22
  106.8 8.4 %collective-permute-start.33 = (bf16[640,128]{1,0:T(8,128)(2,1)S(1)}, bf16[640,128]{1,0:T(8,128)(2,1)S(1)}, u32[]{:S(2)}, u32[]{:S(2)}) collective-permute-start(bf16[640,128]{1,0:T(8,128)(2,1)S(1)} %get-tuple-element.225), channel_id=1, source_target_pairs={{0,4},{4,0},{1,5},{5,1},{2,6},{6,2},{3,7},{7,3},{8,12},{12,8},{9,1... | collective-permute-start | bytes 491528 | tf_op jit(solution)/shard_map/ppermute | solution.py:27
  110.4 10.9 %collective-permute-start.32 = (bf16[64,1280]{1,0:T(8,128)(2,1)S(1)}, bf16[64,1280]{1,0:T(8,128)(2,1)S(1)}, u32[]{:S(2)}, u32[]{:S(2)}) collective-permute-start(bf16[64,1280]{1,0:T(8,128)(2,1)S(1)} %get-tuple-element.220.refs_0_), channel_id=1, source_target_pairs={{0,2},{1,3},{2,0},{3,1},{4,6},{5,7},{6,4},{7,5},{8,10},{9,11},{10,... | collective-permute-start | bytes 491528 | tf_op jit(solution)/shard_map/ppermute | solution.py:22
  116.3 8.4 %collective-permute-start.35 = (bf16[64,1280]{1,0:T(8,128)(2,1)S(1)}, bf16[64,1280]{1,0:T(8,128)(2,1)S(1)}, u32[]{:S(2)}, u32[]{:S(2)}) collective-permute-start(bf16[64,1280]{1,0:T(8,128)(2,1)S(1)} %get-tuple-element.234), channel_id=1, source_target_pairs={{0,1},{1,0},{2,3},{3,2},{4,5},{5,4},{6,7},{7,6},{8,9},{9,8},{10,11... | collective-permute-start | bytes 491528 | tf_op jit(solution)/shard_map/ppermute | solution.py:22
  121.3 7.6 %collective-permute-start.34 = (bf16[64,1280]{1,0:T(8,128)(2,1)S(1)}, bf16[64,1280]{1,0:T(8,128)(2,1)S(1)}, u32[]{:S(2)}, u32[]{:S(2)}) collective-permute-start(bf16[64,1280]{1,0:T(8,128)(2,1)S(1)} %get-tuple-element.230.refs_3_), channel_id=1, source_target_pairs={{0,1},{1,0},{2,3},{3,2},{4,5},{5,4},{6,7},{7,6},{8,9},{9,8},{10,11... | collective-permute-start | bytes 491528 | tf_op jit(solution)/shard_map/ppermute | solution.py:22
  121.4 14.0 %collective-permute-start.38 = (bf16[128,1280]{1,0:T(8,128)(2,1)S(1)}, bf16[128,1280]{1,0:T(8,128)(2,1)S(1)}, u32[]{:S(2)}, u32[]{:S(2)}) collective-permute-start(bf16[128,1280]{1,0:T(8,128)(2,1)S(1)} %get-tuple-element.250), channel_id=1, source_target_pairs={{0,4},{4,0},{1,5},{5,1},{2,6},{6,2},{3,7},{7,3},{8,12},{12,8},{9,1... | collective-permute-start | bytes 983048 | tf_op jit(solution)/shard_map/ppermute | solution.py:27
  121.8 15.7 %collective-permute-start.39 = (bf16[1280,128]{1,0:T(8,128)(2,1)S(1)}, bf16[1280,128]{1,0:T(8,128)(2,1)S(1)}, u32[]{:S(2)}, u32[]{:S(2)}) collective-permute-start(bf16[1280,128]{1,0:T(8,128)(2,1)S(1)} %get-tuple-element.251.refs_6_), channel_id=1, source_target_pairs={{0,4},{4,0},{1,5},{5,1},{2,6},{6,2},{3,7},{7,3},{8,12},{12,8},{9,1... | collective-permute-start | bytes 983048 | tf_op jit(solution)/shard_map/ppermute | solution.py:27
  124.8 10.5 %collective-permute-start.36 = (bf16[64,1280]{1,0:T(8,128)(2,1)S(1)}, bf16[64,1280]{1,0:T(8,128)(2,1)S(1)}, u32[]{:S(2)}, u32[]{:S(2)}) collective-permute-start(bf16[64,1280]{1,0:T(8,128)(2,1)S(1)} %get-tuple-element.242.refs_0_), channel_id=1, source_target_pairs={{0,2},{1,3},{2,0},{3,1},{4,6},{5,7},{6,4},{7,5},{8,10},{9,11},{10,... | collective-permute-start | bytes 491528 | tf_op jit(solution)/shard_map/ppermute | solution.py:22
  (21 other events, 184.3 us)

commit v4 on v3

--- a/solution.py
+++ b/solution.py
@@ -37,7 +37,8 @@
     crossed = [
         (i * pairs + j, (i - 1) * pairs + (j ^ 1)) for i in range(1, length) for j in range(pairs)
     ]
-    return back_a_block(shard), lax.ppermute(shard, ("section", "tp"), crossed)
+    other = lax.ppermute(shard, ("section", "tp"), crossed)
+    return back_a_block(shard), other
 
 
 def call(body, outs, ins, scratch=(), token=None, aliases=(), after=(), passed=()):
@@ -144,8 +145,8 @@
 
 
 def start_all(copies):
-    for number, copy in enumerate(copies):
-        copy.start(priority=number % 2)
+    for copy in copies:
+        copy.start()
     return copies
 
 
@@ -171,12 +172,11 @@
 
 
 def mlp_first_kernel(
-    flags, gains, streams, w_up, w_down, message, slope_ref, send, keep, unit_ref, inv_ref, upper, grad_lower,
-    up_here, down_here, *refs,
+    flags, gains, streams, w_up, message, slope_ref, unit_ref, inv_ref, upper, grad_lower, up_here, *refs
 ):
-    keep_left = refs[0] if len(refs) == 5 else None
-    gains_here, normed_ref, sems, whole = refs[-4:]
-    up_cut, down_cut = row_chunks(up_here.shape[1], CHUNKS), row_chunks(down_here.shape[1], CHUNKS)
+    keep_left = refs[0] if len(refs) == 4 else None
+    gains_here, normed_ref, sems = refs[-3:]
+    up_cut = row_chunks(up_here.shape[1], CHUNKS)
     firsts = start_all(
         [
             pltpu.make_async_copy(streams.at[0, 0], upper, sems.at[0]),
@@ -187,12 +187,6 @@
         [
             pltpu.make_async_copy(w_up.at[0, at], up_here.at[0, at], sems.at[3 + i])
             for i, at in enumerate(up_cut)
-        ]
-    )
-    downs = start_all(
-        [
-            pltpu.make_async_copy(w_down.at[0, at], down_here.at[0, at], sems.at[3 + CHUNKS + i])
-            for i, at in enumerate(down_cut)
         ]
     )
     last = pltpu.make_async_copy(streams.at[0, 3], grad_lower, sems.at[2])
@@ -203,19 +197,19 @@
     normed_ref[...] = (unit * gains_here[1:2]).astype(BF16)
     unit_ref[...] = unit
     inv_ref[...] = jnp.broadcast_to(inv_std, inv_ref.shape)
-    store_lefts([normed_ref[...]], keep_left, message, flags[2])
     pre = None
     for i, at in enumerate(up_cut):
         ups[i].wait()
         part = dot(normed_ref[:, at], up_here[0, at])
         pre = part if pre is None else pre + part
-    hidden = after_left(message, slope_ref.shape[1])
-    after_mlp_up(pre, hidden, slope_ref, slice(None))
-    for i, at in enumerate(down_cut):
-        downs[i].wait()
-        whole[:, at] = dot_t(hidden[...], down_here[0, at])
+    after_mlp_up(pre, after_left(message, slope_ref.shape[1]), slope_ref, slice(None))
+    store_lefts([normed_ref[...]], keep_left, message, flags[2])
+    last.wait()
+
+
+def mlp_first_down_kernel(flags, message, w_down, send, keep, whole):
+    whole[...] = dot_t(after_left(message, w_down.shape[2])[...], w_down[0])
     split(whole, flags[0], send, keep)
-    last.wait()
 
 
 def mlp_forward_kernel(
@@ -516,7 +510,7 @@
             got = run(
                 mlp_forward_kernel,
                 mlp_outs + [full] + keep_outs,
-                [flag, gain] + here(own_upper, got_upper, head_streams, up_here, down_here),
+                [flag, gain] + here(own_upper, got_upper, head_streams, up_here, w_down),
                 [whole],
             )
             message, slope, send_f, keep_f, unit_up, inv_up, upper = got[:7]
@@ -537,24 +531,27 @@
         else:
             got = run(
                 mlp_first_kernel,
-                mlp_outs + [full, full] + [(w.shape, BF16, "kept") for w in (w_up, w_down)] + keep_outs,
-                [flag] + [(a, "hbm") for a in (gains, streams, w_up, w_down)],
+                message_outs
+                + [hid_full]
+                + norm_outs
+                + [full, full, (w_up.shape, BF16, "kept")]
+                + keep_outs,
+                [flag] + [(a, "hbm") for a in (gains, streams, w_up)],
                 [
                     pltpu.VMEM(gains.shape, F32),
                     pltpu.VMEM((rows, width), BF16),
-                    pltpu.SemaphoreType.DMA((3 + 2 * CHUNKS,)),
-                    whole,
+                    pltpu.SemaphoreType.DMA((3 + CHUNKS,)),
                 ],
             )
-            message, slope, send_f, keep_f, unit_up, inv_up, upper, grad_lower = got[:8]
-            up_here, down_here = got[8:10]
+            message, slope, unit_up, inv_up, upper, grad_lower, up_here = got[:7]
+            send_f, keep_f = run(mlp_first_down_kernel, halves, [flag] + here(message, w_down), [whole])
             got_f = swap(send_f, "tp", 1)
-            message_0, factors_0 = message, send_message(got[10] if two else None, message, width, 1)
+            message_0, factors_0 = message, send_message(got[7] if two else None, message, width, 1)
             source = here(grad_lower)
         got = run(
             functools.partial(mlp_backward_kernel, later),
             message_outs + halves + [full] * later + keep_outs,
-            [flag] + source + here(slope, up_here, down_here),
+            [flag] + source + here(slope, up_here, w_down),
             [whole],
             after=rights_1[1:] + lefts_1[1:] if later else (),
         )

time: 145 us -> 145 us (level)
  waiting for transfers between devices: 44.9 us -> 50 us
  starting transfers between devices: 56.2 us -> 51.4 us
    ppermute x22, starting transfers between devices: 28.7 us -> 24.7 us  [swap(): return lax.ppermute(shard, axis, [(i, i ^ by) for i in range(length)])]
    ppermute x22, waiting for transfers between devices: 27.9 us -> 31.8 us  [swap(): return lax.ppermute(shard, axis, [(i, i ^ by) for i in range(length)])]
    pallas_call x36 -> x37, Pallas kernels: 41 us -> 39.9 us  [call(): pl.pallas_call(without_tokens, out_shape=[(pltpu.VMEM if where == 'kept'...]
where the time goes in v4:
time: 145 us; the launch traced here: 142 us
  starting transfers between devices  51.4 us (35%)
  waiting for transfers between devices  50 us (34%)
  Pallas kernels  39.9 us (28%)
    pallas_call x37, Pallas kernels, call(): pl.pallas_call(without_tokens, out_shape=[(pltpu.VMEM if where == 'kept'...  39.9 us
    ppermute x22, waiting for transfers between devices, swap(): return lax.ppermute(shard, axis, [(i, i ^ by) for i in range(length)])  31.8 us
    ppermute x22, starting transfers between devices, swap(): return lax.ppermute(shard, axis, [(i, i ^ by) for i in range(length)])  24.7 us
    ppermute x12, starting transfers between devices, shift(): lax.ppermute(shard, axis, [(i, (i + by) % length) for i in range(length)])  18.7 us
    ppermute x12, waiting for transfers between devices, shift(): lax.ppermute(shard, axis, [(i, (i + by) % length) for i in range(length)])  12.2 us
    ppermute x2, waiting for transfers between devices, back_to_pair(): other = lax.ppermute(shard, ('section', 'tp'), crossed)  5.93 us
    ppermute x4, starting transfers between devices, back_a_block(): lax.ppermute(shard, 'section', [(i, i - 1) for i in range(1, length)])  5.33 us
  transfers between devices with their start and end apart: 40, of which 22 were waited for; matrix products, arithmetic and copies ran while one was open for 0% of the time, Pallas kernels for 23%

profile of v4, /device:TPU:0, one launch (start us, length us, event | category | flops | bytes accessed | tf_op | source)
XLA Modules:
  0.0 142.4 jit_solution(3849269272146402877)
XLA Ops:
  0.7 4.0 %shard_map.110 = (bf16[128,1920]{1,0:T(8,128)(2,1)S(1)}, f32[128,1280]{1,0:T(8,128)S(1)}, f32[128,1280]{1,0:T(8,128)S(1)}, f32[128,128]{1,0:T(8,128)S(1)}, f32[1...) custom-call(s32[3]{0:T(128)S(1)} %pad_add_fusion.refs_0_, ...), custom_call_target="tpu_custom_call" | custom-call | flops 1024 | bytes 1024 | tf_op jit(solution)/shard_map/pallas_call | solution.py:64
  6.5 3.1 %collective-permute-start = (bf16[64,1280]{1,0:T(8,128)(2,1)S(1)}, bf16[64,1280]{1,0:T(8,128)(2,1)S(1)}, u32[]{:S(2)}, u32[]{:S(2)}) collective-permute-start(bf16[64,1280]{1,0:T(8,128)(2,1)S(1)} %get-tuple-element.136), channel_id=1, source_target_pairs={{0,1},{1,0},{2,3},{3,2},{4,5},{5,4},{6,7},{7,6},{8,9},{9,8},{10,11... | collective-permute-start | bytes 491528 | tf_op jit(solution)/shard_map/ppermute | solution.py:22
  13.8 2.8 %collective-permute-start.1 = (bf16[64,1280]{1,0:T(8,128)(2,1)S(1)}, bf16[64,1280]{1,0:T(8,128)(2,1)S(1)}, u32[]{:S(2)}, u32[]{:S(2)}) collective-permute-start(bf16[64,1280]{1,0:T(8,128)(2,1)S(1)} %get-tuple-element.142.refs_0_), channel_id=1, source_target_pairs={{0,2},{1,3},{2,0},{3,1},{4,6},{5,7},{6,4},{7,5},{8,10},{9,11},{10,... | collective-permute-start | bytes 491528 | tf_op jit(solution)/shard_map/ppermute | solution.py:22
  19.7 4.0 %collective-permute-done.1.refs_1_ = bf16[64,1280]{1,0:T(8,128)(2,1)S(1)} collective-permute-done((bf16[64,1280]{1,0:T(8,128)(2,1)S(1)}, bf16[64,1280]{1,0:T(8,128)(2,1)S(1)}, u32[]{:S(2)}, u32[]{:S(2)}) %collective-permute-start.1) | collective-permute-done | bytes 163872 | tf_op jit(solution)/shard_map/ppermute | solution.py:22
  25.4 2.5 %collective-permute-start.7 = (bf16[64,1280]{1,0:T(8,128)(2,1)S(1)}, bf16[64,1280]{1,0:T(8,128)(2,1)S(1)}, u32[]{:S(2)}, u32[]{:S(2)}) collective-permute-start(bf16[64,1280]{1,0:T(8,128)(2,1)S(1)} %get-tuple-element.152.refs_0_), channel_id=1, source_target_pairs={{0,2},{1,3},{2,0},{3,1},{4,6},{5,7},{6,4},{7,5},{8,10},{9,11},{10,... | collective-permute-start | bytes 491528 | tf_op jit(solution)/shard_map/ppermute | solution.py:22
  27.8 4.5 %collective-permute-done.2.refs_4_ = bf16[64,1280]{1,0:T(8,128)(2,1)S(1)} collective-permute-done((bf16[64,1280]{1,0:T(8,128)(2,1)S(1)}, bf16[64,1280]{1,0:T(8,128)(2,1)S(1)}, u32[]{:S(2)}, u32[]{:S(2)}) %collective-permute-start.2) | collective-permute-done | bytes 163872 | tf_op jit(solution)/shard_map/ppermute | solution.py:22
  35.6 3.8 %collective-permute-done.5.refs_3_.refs_9_ = bf16[640,128]{1,0:T(8,128)(2,1)S(1)} collective-permute-done((bf16[640,128]{1,0:T(8,128)(2,1)S(1)}, bf16[640,128]{1,0:T(8,128)(2,1)S(1)}, u32[]{:S(2)}, u32[]{:S(2)}) %collective-permute-start.5) | collective-permute-done | bytes 163872 | tf_op jit(solution)/shard_map/ppermute | solution.py:27
  47.5 2.3 %collective-permute-done.11.refs_3_ = bf16[640,128]{1,0:T(8,128)(2,1)S(1)} collective-permute-done((bf16[640,128]{1,0:T(8,128)(2,1)S(1)}, bf16[640,128]{1,0:T(8,128)(2,1)S(1)}, u32[]{:S(2)}, u32[]{:S(2)}) %collective-permute-start.11) | collective-permute-done | bytes 163872 | tf_op jit(solution)/shard_map/ppermute | solution.py:27
  51.7 2.7 %collective-permute-done.10.refs_3_ = bf16[64,1280]{1,0:T(8,128)(2,1)S(1)} collective-permute-done((bf16[64,1280]{1,0:T(8,128)(2,1)S(1)}, bf16[64,1280]{1,0:T(8,128)(2,1)S(1)}, u32[]{:S(2)}, u32[]{:S(2)}) %collective-permute-start.10) | collective-permute-done | bytes 163872 | tf_op jit(solution)/shard_map/ppermute | solution.py:22
  60.6 2.4 %collective-permute-done.13.refs_3_ = bf16[64,1280]{1,0:T(8,128)(2,1)S(1)} collective-permute-done((bf16[64,1280]{1,0:T(8,128)(2,1)S(1)}, bf16[64,1280]{1,0:T(8,128)(2,1)S(1)}, u32[]{:S(2)}, u32[]{:S(2)}) %collective-permute-start.13) | collective-permute-done | bytes 163872 | tf_op jit(solution)/shard_map/ppermute | solution.py:40
  63.0 2.6 %shard_map.125 = (bf16[128,1920]{1,0:T(8,128)(2,1)S(1)}, f32[128,1280]{1,0:T(8,128)S(1)}, bf16[64,1280]{1,0:T(8,128)(2,1)S(1)}, f32[64,1280]{1,0:T(8,128)S(1)}, ...) custom-call(s32[3]{0:T(128)S(1)} %pad_add_fusion.refs_0_, ...), custom_call_target="tpu_custom_call" | custom-call | flops 1024 | bytes 1024 | tf_op jit(solution)/shard_map/pallas_call | solution.py:64
  65.6 2.7 %collective-permute-start.15 = (bf16[64,1280]{1,0:T(8,128)(2,1)S(1)}, bf16[64,1280]{1,0:T(8,128)(2,1)S(1)}, u32[]{:S(2)}, u32[]{:S(2)}) collective-permute-start(bf16[64,1280]{1,0:T(8,128)(2,1)S(1)} %get-tuple-element.179), channel_id=1, source_target_pairs={{0,1},{1,0},{2,3},{3,2},{4,5},{5,4},{6,7},{7,6},{8,9},{9,8},{10,11... | collective-permute-start | bytes 491528 | tf_op jit(solution)/shard_map/ppermute | solution.py:22
  77.3 3.5 %collective-permute-done.20.refs_2_ = bf16[64,1280]{1,0:T(8,128)(2,1)S(1)} collective-permute-done((bf16[64,1280]{1,0:T(8,128)(2,1)S(1)}, bf16[64,1280]{1,0:T(8,128)(2,1)S(1)}, u32[]{:S(2)}, u32[]{:S(2)}) %collective-permute-start.20) | collective-permute-done | bytes 163872 | tf_op jit(solution)/shard_map/ppermute | solution.py:40
  80.8 2.2 %shard_map.128 = (bf16[128,1920]{1,0:T(8,128)(2,1)S(1)}, bf16[64,1280]{1,0:T(8,128)(2,1)S(1)}, f32[64,1280]{1,0:T(8,128)S(1)}, f32[128,1280]{1,0:T(8,128)S(1)}, ...) custom-call(s32[3]{0:T(128)S(1)} %pad_add_fusion.refs_0_, bf16[64,1280]{1,0:T(8,128)(2,1)S(1)} %collective-permute-done.19.refs_1_, ...), custom_call_target="tpu_custom_call" | custom-call | flops 1024 | bytes 1024 | tf_op jit(solution)/shard_map/pallas_call | solution.py:64
  85.2 2.3 %collective-permute-start.31 = (bf16[128,1920]{1,0:T(8,128)(2,1)S(1)}, bf16[128,1920]{1,0:T(8,128)(2,1)S(1)}, u32[]{:S(2)}, u32[]{:S(2)}) collective-permute-start(bf16[128,1920]{1,0:T(8,128)(2,1)S(1)} %get-tuple-element.215.refs_5_), channel_id=1, source_target_pairs={{0,4},{4,0},{1,5},{5,1},{2,6},{6,2},{3,7},{7,3},{8,12},{12,8},{9,1... | collective-permute-start | bytes 1474568 | tf_op jit(solution)/shard_map/ppermute | solution.py:27
  93.2 2.3 %collective-permute-start.28 = (bf16[640,128]{1,0:T(8,128)(2,1)S(1)}, bf16[640,128]{1,0:T(8,128)(2,1)S(1)}, u32[]{:S(2)}, u32[]{:S(2)}) collective-permute-start(bf16[640,128]{1,0:T(8,128)(2,1)S(1)} %get-tuple-element.207.refs_2_.refs_9_), channel_id=1, source_target_pairs={{0,4},{4,0},{1,5},{5,1},{2,6},{6,2},{3,7},{7,3},{8,12},{12,8},{9,1... | collective-permute-start | bytes 491528 | tf_op jit(solution)/shard_map/ppermute | solution.py:27
  95.5 3.0 %collective-permute-done.26.refs_1_ = bf16[64,1280]{1,0:T(8,128)(2,1)S(1)} collective-permute-done((bf16[64,1280]{1,0:T(8,128)(2,1)S(1)}, bf16[64,1280]{1,0:T(8,128)(2,1)S(1)}, u32[]{:S(2)}, u32[]{:S(2)}) %collective-permute-start.26) | collective-permute-done | bytes 163872 | tf_op jit(solution)/shard_map/ppermute | solution.py:22
  107.2 2.5 %collective-permute-start.33 = (bf16[640,128]{1,0:T(8,128)(2,1)S(1)}, bf16[640,128]{1,0:T(8,128)(2,1)S(1)}, u32[]{:S(2)}, u32[]{:S(2)}) collective-permute-start(bf16[640,128]{1,0:T(8,128)(2,1)S(1)} %get-tuple-element.225), channel_id=1, source_target_pairs={{0,4},{4,0},{1,5},{5,1},{2,6},{6,2},{3,7},{7,3},{8,12},{12,8},{9,1... | collective-permute-start | bytes 491528 | tf_op jit(solution)/shard_map/ppermute | solution.py:27
  111.7 2.5 %collective-permute-done.33.refs_3_ = bf16[640,128]{1,0:T(8,128)(2,1)S(1)} collective-permute-done((bf16[640,128]{1,0:T(8,128)(2,1)S(1)}, bf16[640,128]{1,0:T(8,128)(2,1)S(1)}, u32[]{:S(2)}, u32[]{:S(2)}) %collective-permute-start.33) | collective-permute-done | bytes 163872 | tf_op jit(solution)/shard_map/ppermute | solution.py:27
  116.1 4.2 %collective-permute-done.32.refs_1_ = bf16[64,1280]{1,0:T(8,128)(2,1)S(1)} collective-permute-done((bf16[64,1280]{1,0:T(8,128)(2,1)S(1)}, bf16[64,1280]{1,0:T(8,128)(2,1)S(1)}, u32[]{:S(2)}, u32[]{:S(2)}) %collective-permute-start.32) | collective-permute-done | bytes 163872 | tf_op jit(solution)/shard_map/ppermute | solution.py:22
  125.7 2.2 %shard_map.141 = (bf16[640,1280]{1,0:T(8,128)(2,1)}, f32[8,128]{1,0:T(8,128)S(1)}) custom-call(bf16[128,640]{1,0:T(8,128)(2,1)S(1)} %get-tuple-element.231.refs_0_, bf16[128,1920]{1,0:T(8,128)(2,1)S(1)} %get-tuple-element.133.refs_1_, bf16[128,1920]{1,0:T(8,128)(2,1)S(1)} %collective-permute-done.6.refs_5_.refs_2_.refs_3_, ...), custom_call_target="tpu_custom_call" | custom-call | flops 1024 | bytes 1024 | tf_op jit(solution)/shard_map/pallas_call | solution.py:64
  129.5 2.2 %shard_map.143 = (bf16[640,1280]{1,0:T(8,128)(2,1)}, f32[8,128]{1,0:T(8,128)S(1)}) custom-call(bf16[128,640]{1,0:T(8,128)(2,1)S(1)} %get-tuple-element.243.refs_0_, bf16[128,1920]{1,0:T(8,128)(2,1)S(1)} %get-tuple-element.151.refs_1_, bf16[128,1920]{1,0:T(8,128)(2,1)S(1)} %collective-permute-done.3.refs_6_.refs_3_.refs_2_, ...), custom_call_target="tpu_custom_call" | custom-call | flops 1024 | bytes 1024 | tf_op jit(solution)/shard_map/pallas_call | solution.py:64
  131.7 2.6 %collective-permute-done.36.refs_1_ = bf16[64,1280]{1,0:T(8,128)(2,1)S(1)} collective-permute-done((bf16[64,1280]{1,0:T(8,128)(2,1)S(1)}, bf16[64,1280]{1,0:T(8,128)(2,1)S(1)}, u32[]{:S(2)}, u32[]{:S(2)}) %collective-permute-start.36) | collective-permute-done | bytes 163872 | tf_op jit(solution)/shard_map/ppermute | solution.py:22
  136.6 2.3 %shard_map.145 = (bf16[960,640]{1,0:T(8,128)(2,1)}, bf16[320,640]{1,0:T(8,128)(2,1)}, f32[8,128]{1,0:T(8,128)S(1)}) custom-call(bf16[128,1280]{1,0:T(8,128)(2,1)S(1)} %get-tuple-element.248.refs_0_, bf16[128,1280]{1,0:T(8,128)(2,1)S(1)} %collective-permute-done.22.refs_8_.refs_1_, bf16[128,1280]{1,0:T(8,128)(2,1)S(1)} %get-tuple-element.249.refs_2_, ...), custom_call_target="tpu_custom_call" | custom-call | flops 1024 | bytes 1024 | tf_op jit(solution)/shard_map/pallas_call | solution.py:64
  (106 shorter events, 72.0 us)
Async XLA Ops:
  9.6 22.8 %collective-permute-start.3 = (bf16[128,1920]{1,0:T(8,128)(2,1)S(1)}, bf16[128,1920]{1,0:T(8,128)(2,1)S(1)}, u32[]{:S(2)}, u32[]{:S(2)}) collective-permute-start(bf16[128,1920]{1,0:T(8,128)(2,1)S(1)} %get-tuple-element.133.refs_1_), channel_id=1, source_target_pairs={{0,4},{4,0},{1,5},{5,1},{2,6},{6,2},{3,7},{7,3},{8,12},{12,8},{9,1... | collective-permute-start | bytes 1474568 | tf_op jit(solution)/shard_map/ppermute | solution.py:27
  13.8 9.9 %collective-permute-start.1 = (bf16[64,1280]{1,0:T(8,128)(2,1)S(1)}, bf16[64,1280]{1,0:T(8,128)(2,1)S(1)}, u32[]{:S(2)}, u32[]{:S(2)}) collective-permute-start(bf16[64,1280]{1,0:T(8,128)(2,1)S(1)} %get-tuple-element.142.refs_0_), channel_id=1, source_target_pairs={{0,2},{1,3},{2,0},{3,1},{4,6},{5,7},{6,4},{7,5},{8,10},{9,11},{10,... | collective-permute-start | bytes 491528 | tf_op jit(solution)/shard_map/ppermute | solution.py:22
  16.6 19.0 %collective-permute-start.6 = (bf16[128,1920]{1,0:T(8,128)(2,1)S(1)}, bf16[128,1920]{1,0:T(8,128)(2,1)S(1)}, u32[]{:S(2)}, u32[]{:S(2)}) collective-permute-start(bf16[128,1920]{1,0:T(8,128)(2,1)S(1)} %get-tuple-element.151.refs_1_), channel_id=1, source_target_pairs={{0,4},{4,0},{1,5},{5,1},{2,6},{6,2},{3,7},{7,3},{8,12},{12,8},{9,1... | collective-permute-start | bytes 1474568 | tf_op jit(solution)/shard_map/ppermute | solution.py:27
  23.8 8.6 %collective-permute-start.2 = (bf16[64,1280]{1,0:T(8,128)(2,1)S(1)}, bf16[64,1280]{1,0:T(8,128)(2,1)S(1)}, u32[]{:S(2)}, u32[]{:S(2)}) collective-permute-start(bf16[64,1280]{1,0:T(8,128)(2,1)S(1)} %get-tuple-element.144.refs_3_), channel_id=1, source_target_pairs={{0,1},{1,0},{2,3},{3,2},{4,5},{5,4},{6,7},{7,6},{8,9},{9,8},{10,11... | collective-permute-start | bytes 491528 | tf_op jit(solution)/shard_map/ppermute | solution.py:22
  25.4 10.0 %collective-permute-start.7 = (bf16[64,1280]{1,0:T(8,128)(2,1)S(1)}, bf16[64,1280]{1,0:T(8,128)(2,1)S(1)}, u32[]{:S(2)}, u32[]{:S(2)}) collective-permute-start(bf16[64,1280]{1,0:T(8,128)(2,1)S(1)} %get-tuple-element.152.refs_0_), channel_id=1, source_target_pairs={{0,2},{1,3},{2,0},{3,1},{4,6},{5,7},{6,4},{7,5},{8,10},{9,11},{10,... | collective-permute-start | bytes 491528 | tf_op jit(solution)/shard_map/ppermute | solution.py:22
  51.0 7.5 %collective-permute-start.14 = (bf16[64,1280]{1,0:T(8,128)(2,1)S(1)}, bf16[64,1280]{1,0:T(8,128)(2,1)S(1)}, u32[]{:S(2)}, u32[]{:S(2)}) collective-permute-start(bf16[64,1280]{1,0:T(8,128)(2,1)S(1)} %get-tuple-element.174), channel_id=1, source_target_pairs={{0,1},{1,0},{2,3},{3,2},{4,5},{5,4},{6,7},{7,6},{8,9},{9,8},{10,11... | collective-permute-start | bytes 491528 | tf_op jit(solution)/shard_map/ppermute | solution.py:22
  57.7 16.5 %collective-permute-start.21 = (bf16[1280,128]{1,0:T(8,128)(2,1)S(1)}, bf16[1280,128]{1,0:T(8,128)(2,1)S(1)}, u32[]{:S(2)}, u32[]{:S(2)}) collective-permute-start(bf16[1280,128]{1,0:T(8,128)(2,1)S(1)} %get-tuple-element.190.refs_4_), channel_id=1, source_target_pairs={{0,4},{4,0},{1,5},{5,1},{2,6},{6,2},{3,7},{7,3},{8,12},{12,8},{9,1... | collective-permute-start | bytes 983048 | tf_op jit(solution)/shard_map/ppermute | solution.py:27
  58.5 11.3 %collective-permute-start.16 = (bf16[64,1280]{1,0:T(8,128)(2,1)S(1)}, bf16[64,1280]{1,0:T(8,128)(2,1)S(1)}, u32[]{:S(2)}, u32[]{:S(2)}) collective-permute-start(bf16[64,1280]{1,0:T(8,128)(2,1)S(1)} %get-tuple-element.183.refs_5_), channel_id=1, source_target_pairs={{0,2},{1,3},{2,0},{3,1},{4,6},{5,7},{6,4},{7,5},{8,10},{9,11},{10,... | collective-permute-start | bytes 491528 | tf_op jit(solution)/shard_map/ppermute | solution.py:22
  59.5 21.3 %collective-permute-start.22 = (bf16[128,1280]{1,0:T(8,128)(2,1)S(1)}, bf16[128,1280]{1,0:T(8,128)(2,1)S(1)}, u32[]{:S(2)}, u32[]{:S(2)}) collective-permute-start(bf16[128,1280]{1,0:T(8,128)(2,1)S(1)} %get-tuple-element.191), channel_id=1, source_target_pairs={{0,4},{4,0},{1,5},{5,1},{2,6},{6,2},{3,7},{7,3},{8,12},{12,8},{9,1... | collective-permute-start | bytes 983048 | tf_op jit(solution)/shard_map/ppermute | solution.py:27
  65.6 7.6 %collective-permute-start.15 = (bf16[64,1280]{1,0:T(8,128)(2,1)S(1)}, bf16[64,1280]{1,0:T(8,128)(2,1)S(1)}, u32[]{:S(2)}, u32[]{:S(2)}) collective-permute-start(bf16[64,1280]{1,0:T(8,128)(2,1)S(1)} %get-tuple-element.179), channel_id=1, source_target_pairs={{0,1},{1,0},{2,3},{3,2},{4,5},{5,4},{6,7},{7,6},{8,9},{9,8},{10,11... | collective-permute-start | bytes 491528 | tf_op jit(solution)/shard_map/ppermute | solution.py:22
  71.9 8.9 %collective-permute-start.20 = (bf16[64,1280]{1,0:T(8,128)(2,1)S(1)}, bf16[64,1280]{1,0:T(8,128)(2,1)S(1)}, u32[]{:S(2)}, u32[]{:S(2)}) collective-permute-start(bf16[64,1280]{1,0:T(8,128)(2,1)S(1)} %get-tuple-element.188), channel_id=1, source_target_pairs={{8,1},{9,0},{10,3},{11,2},{16,9},{17,8},{18,11},{19,10},{24,17},{2... | collective-permute-start | bytes 491528 | tf_op jit(solution)/shard_map/ppermute | solution.py:40
  73.3 10.2 %collective-permute-start.18 = (bf16[64,1280]{1,0:T(8,128)(2,1)S(1)}, bf16[64,1280]{1,0:T(8,128)(2,1)S(1)}, u32[]{:S(2)}, u32[]{:S(2)}) collective-permute-start(bf16[64,1280]{1,0:T(8,128)(2,1)S(1)} %get-tuple-element.187.refs_0_), channel_id=1, source_target_pairs={{0,2},{1,3},{2,0},{3,1},{4,6},{5,7},{6,4},{7,5},{8,10},{9,11},{10,... | collective-permute-start | bytes 491528 | tf_op jit(solution)/shard_map/ppermute | solution.py:22
  74.1 24.9 %collective-permute-start.29 = (bf16[128,1920]{1,0:T(8,128)(2,1)S(1)}, bf16[128,1920]{1,0:T(8,128)(2,1)S(1)}, u32[]{:S(2)}, u32[]{:S(2)}) collective-permute-start(bf16[128,1920]{1,0:T(8,128)(2,1)S(1)} %get-tuple-element.208.refs_5_), channel_id=1, source_target_pairs={{0,4},{4,0},{1,5},{5,1},{2,6},{6,2},{3,7},{7,3},{8,12},{12,8},{9,1... | collective-permute-start | bytes 1474568 | tf_op jit(solution)/shard_map/ppermute | solution.py:27
  75.8 15.7 %collective-permute-start.17 = (bf16[128,1280]{1,0:T(8,128)(2,1)S(1)}, bf16[128,1280]{1,0:T(8,128)(2,1)S(1)}, u32[]{:S(2)}, u32[]{:S(2)}) collective-permute-start(bf16[128,1280]{1,0:T(8,128)(2,1)S(1)} %get-tuple-element.186), channel_id=1, source_target_pairs={{8,0},{16,8},{24,16},{9,1},{17,9},{25,17},{10,2},{18,10},{26,18},{... | collective-permute-start | bytes 983048 | tf_op jit(solution)/shard_map/ppermute | solution.py:32
  85.2 24.5 %collective-permute-start.31 = (bf16[128,1920]{1,0:T(8,128)(2,1)S(1)}, bf16[128,1920]{1,0:T(8,128)(2,1)S(1)}, u32[]{:S(2)}, u32[]{:S(2)}) collective-permute-start(bf16[128,1920]{1,0:T(8,128)(2,1)S(1)} %get-tuple-element.215.refs_5_), channel_id=1, source_target_pairs={{0,4},{4,0},{1,5},{5,1},{2,6},{6,2},{3,7},{7,3},{8,12},{12,8},{9,1... | collective-permute-start | bytes 1474568 | tf_op jit(solution)/shard_map/ppermute | solution.py:27
  88.4 10.1 %collective-permute-start.26 = (bf16[64,1280]{1,0:T(8,128)(2,1)S(1)}, bf16[64,1280]{1,0:T(8,128)(2,1)S(1)}, u32[]{:S(2)}, u32[]{:S(2)}) collective-permute-start(bf16[64,1280]{1,0:T(8,128)(2,1)S(1)} %get-tuple-element.203.refs_0_), channel_id=1, source_target_pairs={{0,2},{1,3},{2,0},{3,1},{4,6},{5,7},{6,4},{7,5},{8,10},{9,11},{10,... | collective-permute-start | bytes 491528 | tf_op jit(solution)/shard_map/ppermute | solution.py:22
  90.3 13.3 %collective-permute-start.25 = (bf16[128,1280]{1,0:T(8,128)(2,1)S(1)}, bf16[128,1280]{1,0:T(8,128)(2,1)S(1)}, u32[]{:S(2)}, u32[]{:S(2)}) collective-permute-start(bf16[128,1280]{1,0:T(8,128)(2,1)S(1)} %get-tuple-element.200), channel_id=1, source_target_pairs={{8,0},{16,8},{24,16},{9,1},{17,9},{25,17},{10,2},{18,10},{26,18},{... | collective-permute-start | bytes 983048 | tf_op jit(solution)/shard_map/ppermute | solution.py:32
  102.1 7.6 %collective-permute-start.30 = (bf16[64,1280]{1,0:T(8,128)(2,1)S(1)}, bf16[64,1280]{1,0:T(8,128)(2,1)S(1)}, u32[]{:S(2)}, u32[]{:S(2)}) collective-permute-start(bf16[64,1280]{1,0:T(8,128)(2,1)S(1)} %get-tuple-element.214), channel_id=1, source_target_pairs={{0,1},{1,0},{2,3},{3,2},{4,5},{5,4},{6,7},{7,6},{8,9},{9,8},{10,11... | collective-permute-start | bytes 491528 | tf_op jit(solution)/shard_map/ppermute | solution.py:22
  109.8 10.5 %collective-permute-start.32 = (bf16[64,1280]{1,0:T(8,128)(2,1)S(1)}, bf16[64,1280]{1,0:T(8,128)(2,1)S(1)}, u32[]{:S(2)}, u32[]{:S(2)}) collective-permute-start(bf16[64,1280]{1,0:T(8,128)(2,1)S(1)} %get-tuple-element.220.refs_0_), channel_id=1, source_target_pairs={{0,2},{1,3},{2,0},{3,1},{4,6},{5,7},{6,4},{7,5},{8,10},{9,11},{10,... | collective-permute-start | bytes 491528 | tf_op jit(solution)/shard_map/ppermute | solution.py:22
  115.4 8.4 %collective-permute-start.35 = (bf16[64,1280]{1,0:T(8,128)(2,1)S(1)}, bf16[64,1280]{1,0:T(8,128)(2,1)S(1)}, u32[]{:S(2)}, u32[]{:S(2)}) collective-permute-start(bf16[64,1280]{1,0:T(8,128)(2,1)S(1)} %get-tuple-element.234), channel_id=1, source_target_pairs={{0,1},{1,0},{2,3},{3,2},{4,5},{5,4},{6,7},{7,6},{8,9},{9,8},{10,11... | collective-permute-start | bytes 491528 | tf_op jit(solution)/shard_map/ppermute | solution.py:22
  120.3 7.6 %collective-permute-start.34 = (bf16[64,1280]{1,0:T(8,128)(2,1)S(1)}, bf16[64,1280]{1,0:T(8,128)(2,1)S(1)}, u32[]{:S(2)}, u32[]{:S(2)}) collective-permute-start(bf16[64,1280]{1,0:T(8,128)(2,1)S(1)} %get-tuple-element.230.refs_3_), channel_id=1, source_target_pairs={{0,1},{1,0},{2,3},{3,2},{4,5},{5,4},{6,7},{7,6},{8,9},{9,8},{10,11... | collective-permute-start | bytes 491528 | tf_op jit(solution)/shard_map/ppermute | solution.py:22
  120.4 14.0 %collective-permute-start.38 = (bf16[128,1280]{1,0:T(8,128)(2,1)S(1)}, bf16[128,1280]{1,0:T(8,128)(2,1)S(1)}, u32[]{:S(2)}, u32[]{:S(2)}) collective-permute-start(bf16[128,1280]{1,0:T(8,128)(2,1)S(1)} %get-tuple-element.250), channel_id=1, source_target_pairs={{0,4},{4,0},{1,5},{5,1},{2,6},{6,2},{3,7},{7,3},{8,12},{12,8},{9,1... | collective-permute-start | bytes 983048 | tf_op jit(solution)/shard_map/ppermute | solution.py:27
  121.3 15.2 %collective-permute-start.39 = (bf16[1280,128]{1,0:T(8,128)(2,1)S(1)}, bf16[1280,128]{1,0:T(8,128)(2,1)S(1)}, u32[]{:S(2)}, u32[]{:S(2)}) collective-permute-start(bf16[1280,128]{1,0:T(8,128)(2,1)S(1)} %get-tuple-element.251.refs_6_), channel_id=1, source_target_pairs={{0,4},{4,0},{1,5},{5,1},{2,6},{6,2},{3,7},{7,3},{8,12},{12,8},{9,1... | collective-permute-start | bytes 983048 | tf_op jit(solution)/shard_map/ppermute | solution.py:27
  123.8 10.5 %collective-permute-start.36 = (bf16[64,1280]{1,0:T(8,128)(2,1)S(1)}, bf16[64,1280]{1,0:T(8,128)(2,1)S(1)}, u32[]{:S(2)}, u32[]{:S(2)}) collective-permute-start(bf16[64,1280]{1,0:T(8,128)(2,1)S(1)} %get-tuple-element.242.refs_0_), channel_id=1, source_target_pairs={{0,2},{1,3},{2,0},{3,1},{4,6},{5,7},{6,4},{7,5},{8,10},{9,11},{10,... | collective-permute-start | bytes 491528 | tf_op jit(solution)/shard_map/ppermute | solution.py:22
  (22 other events, 188.3 us)

commit v5 on v4

--- a/solution.py
+++ b/solution.py
@@ -213,7 +213,7 @@
 
 
 def mlp_forward_kernel(
-    flags, gains, own, got, head, w_up, w_down, message, slope_ref, send, keep, unit_ref, inv_ref, upper_ref, *refs
+    flags, gains, got, own, head, w_up, w_down, message, slope_ref, send, keep, unit_ref, inv_ref, upper_ref, *refs
 ):
     keep_left = refs[0] if len(refs) == 2 else None
     whole = refs[-1]
@@ -392,12 +392,16 @@
     copy.wait()
 
 
-def recon_lower_kernel(flags, gains, unused, unit, inv, grad_lower, own, got, out, here, sem, whole):
-    grad_att = join(own, got, flags[0], whole)
-    here[...] = grad_lower[...] + norm_back(grad_att, gains[0:1], unit[...], inv[:, 0:1])
-    copy = pltpu.make_async_copy(here, out.at[0, 3], sem)
-    copy.start()
-    copy.wait()
+def recon_lower_kernel(flags, gains, unused, unit, inv, grad_lower, own, got, out, here, sems, whole):
+    join(own, got, flags[0], whole)
+    copies = []
+    for number, rows in enumerate(row_chunks(here.shape[0], 2)):
+        back = norm_back(whole[rows], gains[0:1], unit[rows], inv[rows, 0:1])
+        here[rows] = grad_lower[rows] + back
+        copies.append(pltpu.make_async_copy(here.at[rows], out.at[0, 3, rows], sems.at[number]))
+        copies[-1].start()
+    for copy in copies:
+        copy.wait()
 
 
 def mlp_grad_kernel(places, *refs):
@@ -510,7 +514,7 @@
             got = run(
                 mlp_forward_kernel,
                 mlp_outs + [full] + keep_outs,
-                [flag, gain] + here(own_upper, got_upper, head_streams, up_here, w_down),
+                [flag, gain] + here(got_upper, own_upper, head_streams, up_here, w_down),
                 [whole],
             )
             message, slope, send_f, keep_f, unit_up, inv_up, upper = got[:7]
@@ -562,7 +566,7 @@
         got_b = swap(send_b, "tp", 1)
         if later:
             message_3, factors_3 = message, send_message(keep_left, message, width, 1)
-            own_out = add(sum_f, got_f)
+            own_out = add(sum_f, got_f, after=())
             got_out = swap(own_out, "tp", 1)
             (sum_b,) = run(add_kernel, [half_low], here(keep_b, got_b))
             sum_b, got_b = middle_adds(sum_b)
@@ -589,7 +593,7 @@
         if not later:
             lower_low = got[6]
         all_kv = [kv] + [shift(kv, "seq", -by) for by in range(1, n_seq)]
-        own_normed = add(sum_b, got_b, after=() if later else ())
+        own_normed = add(sum_b, got_b, after=factors_2[1:] if later else ())
         got_normed = swap(own_normed, "tp", 1)
         probs, mixed, send_f, keep_f = run(
             functools.partial(attend_kernel, others),
@@ -597,7 +601,7 @@
             + halves,
             [flag] + here(query, *all_kv, w_out_t),
             [whole],
-            after=factors_2[1:] if later else factors_1[1:],
+            after=() if later else factors_1[1:],
         )
         got_f = swap(send_f, "tp", 1)
 
@@ -610,12 +614,14 @@
             + (here(next_total, head_streams) if later else here(streams))
             + here(unit_up, inv_up, own_normed, got_normed, query, *all_kv, probs, w_out_t),
             [whole],
+            after=factors_3[1:] if later else (),
         )
         total_low, grad_query, kv_own = got[:3]
         kv_got = [shift(part, "seq", by + 1) for by, part in enumerate(got[3 : 3 + others])]
-        (sum_f,) = run(add_kernel, [half_low], here(keep_f, got_f), after=factors_3[1:] if later else ())
-        sum_f, got_f = middle_adds(sum_f)
-        if later:
+        if not later:
+            (sum_f,) = run(add_kernel, [half_low], here(keep_f, got_f))
+            sum_f, got_f = middle_adds(sum_f)
+        else:
             recon_out = [((1, 4, rows, width), F32, "any")]
             (recon,) = run(
                 recon_middle_kernel, recon_out, here(lower_in, got[-1]), [pltpu.SemaphoreType.DMA((2,))]
@@ -625,17 +631,20 @@
             [((4 * local, rows), BF16, "vmem")] + halves,
             [flag] + here(grad_query, kv_own, *kv_got, mixed, w_qkv_t),
             [whole],
+            after=() if later else (),
         )
         got_b = swap(send_b, "tp", 1)
         rights_att = send_whole(rights)
 
         if later:
             rights_2 = rights_att
+            (sum_f,) = run(add_kernel, [half_low], here(keep_f, got_f))
+            sum_f, got_f = middle_adds(sum_f)
             lefts_2 = send_message(*pack(att_low, total_low), width, 2)
+            (sum_b,) = run(add_kernel, [half_low], here(keep_b, got_b))
+            sum_b, got_b = middle_adds(sum_b)
             own_f = add(sum_f, got_f)
             got_f = swap(own_f, "tp", 1)
-            (sum_b,) = run(add_kernel, [half_low], here(keep_b, got_b))
-            sum_b, got_b = middle_adds(sum_b)
         else:
             rights_1 = rights_att
             (next_half,) = run(
@@ -646,7 +655,7 @@
             (sum_b,) = run(add_kernel, [half_low], here(keep_b, got_b))
             sum_b, got_b = middle_adds(sum_b)
             own_upper, got_upper = back_to_pair(next_half)
-            lefts_1 = send_message(*pack(att_low, total_low, after=[own_upper]), width, 2)
+            lefts_1 = send_message(*pack(att_low, total_low), width, 2)
 
     ups, downs = [], []
     for up, down, mine_up, mine_down in (
@@ -679,6 +688,9 @@
         return grad
 
     grad_down = mlp_grad(downs)
+    grad_up = mlp_grad(ups)
+    own_b = add(sum_b, got_b)
+    got_b = swap(own_b, "tp", 1)
     (recon,) = run(
         recon_upper_kernel,
         recon_out,
@@ -686,9 +698,6 @@
         [whole, one_sem, whole],
         aliases=[(1, 0)],
     )
-    grad_up = mlp_grad(ups)
-    own_b = add(sum_b, got_b)
-    got_b = swap(own_b, "tp", 1)
     lefts_att, rights_att = lefts_1 + lefts_2, rights_1 + rights_2
     if two:
         grad_qkv, grad_out = run(
@@ -705,7 +714,7 @@
         recon_lower_kernel,
         recon_out,
         [flag, gain, (recon, "any")] + here(unit_att, inv_att, grad_lower, own_b, got_b),
-        [whole, one_sem, whole],
+        [whole, pltpu.SemaphoreType.DMA((2,)), whole],
         aliases=[(2, 0)],
     )
     return (

time: 145 us -> 143 us (0.986)
  waiting for transfers between devices: 50 us -> 42.7 us
  starting transfers between devices: 51.4 us -> 56.8 us
    ppermute x22, starting transfers between devices: 24.7 us -> 36.5 us  [swap(): return lax.ppermute(shard, axis, [(i, i ^ by) for i in range(length)])]
    ppermute x12, starting transfers between devices: 18.7 us -> 12.3 us  [shift(): lax.ppermute(shard, axis, [(i, (i + by) % length) for i in range(length)])]
    ppermute x22, waiting for transfers between devices: 31.8 us -> 26.5 us  [swap(): return lax.ppermute(shard, axis, [(i, i ^ by) for i in range(length)])]
  transfers between devices with their start and end apart: 40 -> 40, of which waited for: 22 -> 20; matrix products, arithmetic and copies ran while one was open for 0% -> 0% of each run, Pallas kernels for 23% -> 21%
where the time goes in v5:
time: 143 us; the launch traced here: 141 us
  starting transfers between devices  56.8 us (40%)
  waiting for transfers between devices  42.7 us (30%)
  Pallas kernels  39.8 us (28%)
    pallas_call x37, Pallas kernels, call(): pl.pallas_call(without_tokens, out_shape=[(pltpu.VMEM if where == 'kept'...  39.8 us
    ppermute x22, starting transfers between devices, swap(): return lax.ppermute(shard, axis, [(i, i ^ by) for i in range(length)])  36.5 us
    ppermute x22, waiting for transfers between devices, swap(): return lax.ppermute(shard, axis, [(i, i ^ by) for i in range(length)])  26.5 us
    ppermute x12, starting transfers between devices, shift(): lax.ppermute(shard, axis, [(i, (i + by) % length) for i in range(length)])  12.3 us
    ppermute x12, waiting for transfers between devices, shift(): lax.ppermute(shard, axis, [(i, (i + by) % length) for i in range(length)])  11.4 us
    ppermute x4, starting transfers between devices, back_a_block(): lax.ppermute(shard, 'section', [(i, i - 1) for i in range(1, length)])  5.33 us
    ppermute x2, waiting for transfers between devices, back_to_pair(): other = lax.ppermute(shard, ('section', 'tp'), crossed)  4.83 us
  transfers between devices with their start and end apart: 40, of which 20 were waited for; matrix products, arithmetic and copies ran while one was open for 0% of the time, Pallas kernels for 21%

profile of v5, /device:TPU:0, one launch (start us, length us, event | category | flops | bytes accessed | tf_op | source)
XLA Modules:
  0.0 140.6 jit_solution(13191900611901968408)
XLA Ops:
  0.7 4.0 %shard_map.110 = (bf16[128,1920]{1,0:T(8,128)(2,1)S(1)}, f32[128,1280]{1,0:T(8,128)S(1)}, f32[128,1280]{1,0:T(8,128)S(1)}, f32[128,128]{1,0:T(8,128)S(1)}, f32[1...) custom-call(s32[3]{0:T(128)S(1)} %pad_add_fusion.refs_0_, ...), custom_call_target="tpu_custom_call" | custom-call | flops 1024 | bytes 1024 | tf_op jit(solution)/shard_map/pallas_call | solution.py:64
  6.5 3.1 %collective-permute-start = (bf16[64,1280]{1,0:T(8,128)(2,1)S(1)}, bf16[64,1280]{1,0:T(8,128)(2,1)S(1)}, u32[]{:S(2)}, u32[]{:S(2)}) collective-permute-start(bf16[64,1280]{1,0:T(8,128)(2,1)S(1)} %get-tuple-element.136), channel_id=1, source_target_pairs={{0,1},{1,0},{2,3},{3,2},{4,5},{5,4},{6,7},{7,6},{8,9},{9,8},{10,11... | collective-permute-start | bytes 491528 | tf_op jit(solution)/shard_map/ppermute | solution.py:22
  11.1 2.1 %shard_map.112 = (bf16[128,1920]{1,0:T(8,128)(2,1)S(1)}, bf16[64,1280]{1,0:T(8,128)(2,1)S(1)}, f32[64,1280]{1,0:T(8,128)S(1)}, bf16[128,640]{1,0:T(8,128)(2,1)S(1)}, f32[8,128]{1,0:T(8,128)S(1)}) custom-call(s32[3]{0:T(128)S(1)} %pad_add_fusion.refs_0_, f32[128,1280]{1,0:T(8,128)S(1)} %get-tuple-element.137.refs_1_.refs_4_, ...), custom_call_target="tpu_custom_call" | custom-call | flops 1024 | bytes 1024 | tf_op jit(solution)/shard_map/pallas_call | solution.py:64
  13.8 2.8 %collective-permute-start.1 = (bf16[64,1280]{1,0:T(8,128)(2,1)S(1)}, bf16[64,1280]{1,0:T(8,128)(2,1)S(1)}, u32[]{:S(2)}, u32[]{:S(2)}) collective-permute-start(bf16[64,1280]{1,0:T(8,128)(2,1)S(1)} %get-tuple-element.142.refs_0_), channel_id=1, source_target_pairs={{0,2},{1,3},{2,0},{3,1},{4,6},{5,7},{6,4},{7,5},{8,10},{9,11},{10,... | collective-permute-start | bytes 491528 | tf_op jit(solution)/shard_map/ppermute | solution.py:22
  19.7 4.0 %collective-permute-done.1.refs_1_ = bf16[64,1280]{1,0:T(8,128)(2,1)S(1)} collective-permute-done((bf16[64,1280]{1,0:T(8,128)(2,1)S(1)}, bf16[64,1280]{1,0:T(8,128)(2,1)S(1)}, u32[]{:S(2)}, u32[]{:S(2)}) %collective-permute-start.1) | collective-permute-done | bytes 163872 | tf_op jit(solution)/shard_map/ppermute | solution.py:22
  25.4 2.5 %collective-permute-start.7 = (bf16[64,1280]{1,0:T(8,128)(2,1)S(1)}, bf16[64,1280]{1,0:T(8,128)(2,1)S(1)}, u32[]{:S(2)}, u32[]{:S(2)}) collective-permute-start(bf16[64,1280]{1,0:T(8,128)(2,1)S(1)} %get-tuple-element.152.refs_0_), channel_id=1, source_target_pairs={{0,2},{1,3},{2,0},{3,1},{4,6},{5,7},{6,4},{7,5},{8,10},{9,11},{10,... | collective-permute-start | bytes 491528 | tf_op jit(solution)/shard_map/ppermute | solution.py:22
  27.8 4.5 %collective-permute-done.2.refs_4_ = bf16[64,1280]{1,0:T(8,128)(2,1)S(1)} collective-permute-done((bf16[64,1280]{1,0:T(8,128)(2,1)S(1)}, bf16[64,1280]{1,0:T(8,128)(2,1)S(1)}, u32[]{:S(2)}, u32[]{:S(2)}) %collective-permute-start.2) | collective-permute-done | bytes 163872 | tf_op jit(solution)/shard_map/ppermute | solution.py:22
  35.6 3.8 %collective-permute-done.5.refs_3_.refs_9_ = bf16[640,128]{1,0:T(8,128)(2,1)S(1)} collective-permute-done((bf16[640,128]{1,0:T(8,128)(2,1)S(1)}, bf16[640,128]{1,0:T(8,128)(2,1)S(1)}, u32[]{:S(2)}, u32[]{:S(2)}) %collective-permute-start.5) | collective-permute-done | bytes 163872 | tf_op jit(solution)/shard_map/ppermute | solution.py:27
  47.5 2.3 %collective-permute-done.11.refs_3_ = bf16[640,128]{1,0:T(8,128)(2,1)S(1)} collective-permute-done((bf16[640,128]{1,0:T(8,128)(2,1)S(1)}, bf16[640,128]{1,0:T(8,128)(2,1)S(1)}, u32[]{:S(2)}, u32[]{:S(2)}) %collective-permute-start.11) | collective-permute-done | bytes 163872 | tf_op jit(solution)/shard_map/ppermute | solution.py:27
  51.7 2.7 %collective-permute-done.10.refs_3_ = bf16[64,1280]{1,0:T(8,128)(2,1)S(1)} collective-permute-done((bf16[64,1280]{1,0:T(8,128)(2,1)S(1)}, bf16[64,1280]{1,0:T(8,128)(2,1)S(1)}, u32[]{:S(2)}, u32[]{:S(2)}) %collective-permute-start.10) | collective-permute-done | bytes 163872 | tf_op jit(solution)/shard_map/ppermute | solution.py:22
  61.7 2.6 %shard_map.125 = (bf16[128,1920]{1,0:T(8,128)(2,1)S(1)}, f32[128,1280]{1,0:T(8,128)S(1)}, bf16[64,1280]{1,0:T(8,128)(2,1)S(1)}, f32[64,1280]{1,0:T(8,128)S(1)}, ...) custom-call(s32[3]{0:T(128)S(1)} %pad_add_fusion.refs_0_, ...), custom_call_target="tpu_custom_call" | custom-call | flops 1024 | bytes 1024 | tf_op jit(solution)/shard_map/pallas_call | solution.py:64
  66.0 4.0 %collective-permute-done.16.refs_6_ = bf16[64,1280]{1,0:T(8,128)(2,1)S(1)} collective-permute-done((bf16[64,1280]{1,0:T(8,128)(2,1)S(1)}, bf16[64,1280]{1,0:T(8,128)(2,1)S(1)}, u32[]{:S(2)}, u32[]{:S(2)}) %collective-permute-start.16) | collective-permute-done | bytes 163872 | tf_op jit(solution)/shard_map/ppermute | solution.py:22
  75.8 3.7 %collective-permute-done.20.refs_2_ = bf16[64,1280]{1,0:T(8,128)(2,1)S(1)} collective-permute-done((bf16[64,1280]{1,0:T(8,128)(2,1)S(1)}, bf16[64,1280]{1,0:T(8,128)(2,1)S(1)}, u32[]{:S(2)}, u32[]{:S(2)}) %collective-permute-start.20) | collective-permute-done | bytes 163872 | tf_op jit(solution)/shard_map/ppermute | solution.py:40
  79.5 2.2 %shard_map.128 = (bf16[128,1920]{1,0:T(8,128)(2,1)S(1)}, bf16[64,1280]{1,0:T(8,128)(2,1)S(1)}, f32[64,1280]{1,0:T(8,128)S(1)}, f32[128,1280]{1,0:T(8,128)S(1)}, ...) custom-call(s32[3]{0:T(128)S(1)} %pad_add_fusion.refs_0_, bf16[64,1280]{1,0:T(8,128)(2,1)S(1)} %collective-permute-done.19.refs_1_, ...), custom_call_target="tpu_custom_call" | custom-call | flops 1024 | bytes 1024 | tf_op jit(solution)/shard_map/pallas_call | solution.py:64
  84.7 2.4 %collective-permute-done.24.refs_1_ = bf16[64,1280]{1,0:T(8,128)(2,1)S(1)} collective-permute-done((bf16[64,1280]{1,0:T(8,128)(2,1)S(1)}, bf16[64,1280]{1,0:T(8,128)(2,1)S(1)}, u32[]{:S(2)}, u32[]{:S(2)}) %collective-permute-start.24) | collective-permute-done | bytes 163872 | tf_op jit(solution)/shard_map/ppermute | solution.py:22
  95.9 3.7 %collective-permute-done.29.refs_3_.refs_10_ = bf16[640,128]{1,0:T(8,128)(2,1)S(1)} collective-permute-done((bf16[640,128]{1,0:T(8,128)(2,1)S(1)}, bf16[640,128]{1,0:T(8,128)(2,1)S(1)}, u32[]{:S(2)}, u32[]{:S(2)}) %collective-permute-start.29) | collective-permute-done | bytes 163872 | tf_op jit(solution)/shard_map/ppermute | solution.py:27
  101.1 2.1 %shard_map.134 = (bf16[128,1280]{1,0:T(8,128)(2,1)S(1)}, bf16[320,128]{1,0:T(8,128)(2,1)S(1)}, f32[640,128]{1,0:T(8,128)S(1)}, bf16[640,128]{1,0:T(8,128)(2,1)S(...) custom-call(s32[3]{0:T(128)S(1)} %pad_add_fusion.refs_0_, f32[2,1280]{1,0:T(2,128)S(1)} %bitcast.36, ...), custom_call_target="tpu_custom_call" | custom-call | flops 1024 | bytes 1024 | tf_op jit(solution)/shard_map/pallas_call | solution.py:64
  103.8 2.2 %collective-permute-start.31 = (bf16[64,1280]{1,0:T(8,128)(2,1)S(1)}, bf16[64,1280]{1,0:T(8,128)(2,1)S(1)}, u32[]{:S(2)}, u32[]{:S(2)}) collective-permute-start(bf16[64,1280]{1,0:T(8,128)(2,1)S(1)} %get-tuple-element.218), channel_id=1, source_target_pairs={{0,1},{1,0},{2,3},{3,2},{4,5},{5,4},{6,7},{7,6},{8,9},{9,8},{10,11... | collective-permute-start | bytes 491528 | tf_op jit(solution)/shard_map/ppermute | solution.py:22
  111.9 4.1 %collective-permute-start.33 = (bf16[64,1280]{1,0:T(8,128)(2,1)S(1)}, bf16[64,1280]{1,0:T(8,128)(2,1)S(1)}, u32[]{:S(2)}, u32[]{:S(2)}) collective-permute-start(bf16[64,1280]{1,0:T(8,128)(2,1)S(1)} %get-tuple-element.225.refs_0_), channel_id=1, source_target_pairs={{0,2},{1,3},{2,0},{3,1},{4,6},{5,7},{6,4},{7,5},{8,10},{9,11},{10,... | collective-permute-start | bytes 491528 | tf_op jit(solution)/shard_map/ppermute | solution.py:22
  118.8 4.3 %collective-permute-start.36 = (bf16[64,1280]{1,0:T(8,128)(2,1)S(1)}, bf16[64,1280]{1,0:T(8,128)(2,1)S(1)}, u32[]{:S(2)}, u32[]{:S(2)}) collective-permute-start(bf16[64,1280]{1,0:T(8,128)(2,1)S(1)} %get-tuple-element.234.refs_0_), channel_id=1, source_target_pairs={{0,2},{1,3},{2,0},{3,1},{4,6},{5,7},{6,4},{7,5},{8,10},{9,11},{10,... | collective-permute-start | bytes 491528 | tf_op jit(solution)/shard_map/ppermute | solution.py:22
  123.1 5.7 %collective-permute-start.35 = (bf16[64,1280]{1,0:T(8,128)(2,1)S(1)}, bf16[64,1280]{1,0:T(8,128)(2,1)S(1)}, u32[]{:S(2)}, u32[]{:S(2)}) collective-permute-start(bf16[64,1280]{1,0:T(8,128)(2,1)S(1)} %get-tuple-element.233.refs_3_), channel_id=1, source_target_pairs={{0,1},{1,0},{2,3},{3,2},{4,5},{5,4},{6,7},{7,6},{8,9},{9,8},{10,11... | collective-permute-start | bytes 491528 | tf_op jit(solution)/shard_map/ppermute | solution.py:22
  128.7 2.2 %shard_map.141 = (bf16[640,1280]{1,0:T(8,128)(2,1)}, f32[8,128]{1,0:T(8,128)S(1)}) custom-call(bf16[128,640]{1,0:T(8,128)(2,1)S(1)} %get-tuple-element.237.refs_0_, bf16[128,1920]{1,0:T(8,128)(2,1)S(1)} %get-tuple-element.133.refs_1_, bf16[128,1920]{1,0:T(8,128)(2,1)S(1)} %collective-permute-done.6.refs_5_.refs_2_.refs_3_, ...), custom_call_target="tpu_custom_call" | custom-call | flops 1024 | bytes 1024 | tf_op jit(solution)/shard_map/pallas_call | solution.py:64
  131.0 2.2 %shard_map.142 = (bf16[640,1280]{1,0:T(8,128)(2,1)}, f32[8,128]{1,0:T(8,128)S(1)}) custom-call(bf16[128,640]{1,0:T(8,128)(2,1)S(1)} %get-tuple-element.235.refs_0_, bf16[128,1920]{1,0:T(8,128)(2,1)S(1)} %get-tuple-element.151.refs_1_, bf16[128,1920]{1,0:T(8,128)(2,1)S(1)} %collective-permute-done.3.refs_6_.refs_3_.refs_2_, ...), custom_call_target="tpu_custom_call" | custom-call | flops 1024 | bytes 1024 | tf_op jit(solution)/shard_map/pallas_call | solution.py:64
  135.3 2.4 %shard_map.145 = (bf16[960,640]{1,0:T(8,128)(2,1)}, bf16[320,640]{1,0:T(8,128)(2,1)}, f32[8,128]{1,0:T(8,128)S(1)}) custom-call(bf16[128,1280]{1,0:T(8,128)(2,1)S(1)} %get-tuple-element.248.refs_0_, bf16[128,1280]{1,0:T(8,128)(2,1)S(1)} %collective-permute-done.22.refs_8_.refs_1_, bf16[128,1280]{1,0:T(8,128)(2,1)S(1)} %get-tuple-element.249.refs_2_, ...), custom_call_target="tpu_custom_call" | custom-call | flops 1024 | bytes 1024 | tf_op jit(solution)/shard_map/pallas_call | solution.py:64
  (106 shorter events, 63.8 us)
Async XLA Ops:
  9.6 22.8 %collective-permute-start.3 = (bf16[128,1920]{1,0:T(8,128)(2,1)S(1)}, bf16[128,1920]{1,0:T(8,128)(2,1)S(1)}, u32[]{:S(2)}, u32[]{:S(2)}) collective-permute-start(bf16[128,1920]{1,0:T(8,128)(2,1)S(1)} %get-tuple-element.133.refs_1_), channel_id=1, source_target_pairs={{0,4},{4,0},{1,5},{5,1},{2,6},{6,2},{3,7},{7,3},{8,12},{12,8},{9,1... | collective-permute-start | bytes 1474568 | tf_op jit(solution)/shard_map/ppermute | solution.py:27
  13.8 9.9 %collective-permute-start.1 = (bf16[64,1280]{1,0:T(8,128)(2,1)S(1)}, bf16[64,1280]{1,0:T(8,128)(2,1)S(1)}, u32[]{:S(2)}, u32[]{:S(2)}) collective-permute-start(bf16[64,1280]{1,0:T(8,128)(2,1)S(1)} %get-tuple-element.142.refs_0_), channel_id=1, source_target_pairs={{0,2},{1,3},{2,0},{3,1},{4,6},{5,7},{6,4},{7,5},{8,10},{9,11},{10,... | collective-permute-start | bytes 491528 | tf_op jit(solution)/shard_map/ppermute | solution.py:22
  16.6 19.0 %collective-permute-start.6 = (bf16[128,1920]{1,0:T(8,128)(2,1)S(1)}, bf16[128,1920]{1,0:T(8,128)(2,1)S(1)}, u32[]{:S(2)}, u32[]{:S(2)}) collective-permute-start(bf16[128,1920]{1,0:T(8,128)(2,1)S(1)} %get-tuple-element.151.refs_1_), channel_id=1, source_target_pairs={{0,4},{4,0},{1,5},{5,1},{2,6},{6,2},{3,7},{7,3},{8,12},{12,8},{9,1... | collective-permute-start | bytes 1474568 | tf_op jit(solution)/shard_map/ppermute | solution.py:27
  23.8 8.6 %collective-permute-start.2 = (bf16[64,1280]{1,0:T(8,128)(2,1)S(1)}, bf16[64,1280]{1,0:T(8,128)(2,1)S(1)}, u32[]{:S(2)}, u32[]{:S(2)}) collective-permute-start(bf16[64,1280]{1,0:T(8,128)(2,1)S(1)} %get-tuple-element.144.refs_3_), channel_id=1, source_target_pairs={{0,1},{1,0},{2,3},{3,2},{4,5},{5,4},{6,7},{7,6},{8,9},{9,8},{10,11... | collective-permute-start | bytes 491528 | tf_op jit(solution)/shard_map/ppermute | solution.py:22
  25.4 10.0 %collective-permute-start.7 = (bf16[64,1280]{1,0:T(8,128)(2,1)S(1)}, bf16[64,1280]{1,0:T(8,128)(2,1)S(1)}, u32[]{:S(2)}, u32[]{:S(2)}) collective-permute-start(bf16[64,1280]{1,0:T(8,128)(2,1)S(1)} %get-tuple-element.152.refs_0_), channel_id=1, source_target_pairs={{0,2},{1,3},{2,0},{3,1},{4,6},{5,7},{6,4},{7,5},{8,10},{9,11},{10,... | collective-permute-start | bytes 491528 | tf_op jit(solution)/shard_map/ppermute | solution.py:22
  51.0 7.5 %collective-permute-start.14 = (bf16[64,1280]{1,0:T(8,128)(2,1)S(1)}, bf16[64,1280]{1,0:T(8,128)(2,1)S(1)}, u32[]{:S(2)}, u32[]{:S(2)}) collective-permute-start(bf16[64,1280]{1,0:T(8,128)(2,1)S(1)} %get-tuple-element.174), channel_id=1, source_target_pairs={{0,1},{1,0},{2,3},{3,2},{4,5},{5,4},{6,7},{7,6},{8,9},{9,8},{10,11... | collective-permute-start | bytes 491528 | tf_op jit(solution)/shard_map/ppermute | solution.py:22
  57.7 15.9 %collective-permute-start.21 = (bf16[1280,128]{1,0:T(8,128)(2,1)S(1)}, bf16[1280,128]{1,0:T(8,128)(2,1)S(1)}, u32[]{:S(2)}, u32[]{:S(2)}) collective-permute-start(bf16[1280,128]{1,0:T(8,128)(2,1)S(1)} %get-tuple-element.190.refs_4_), channel_id=1, source_target_pairs={{0,4},{4,0},{1,5},{5,1},{2,6},{6,2},{3,7},{7,3},{8,12},{12,8},{9,1... | collective-permute-start | bytes 983048 | tf_op jit(solution)/shard_map/ppermute | solution.py:27
  58.5 11.5 %collective-permute-start.16 = (bf16[64,1280]{1,0:T(8,128)(2,1)S(1)}, bf16[64,1280]{1,0:T(8,128)(2,1)S(1)}, u32[]{:S(2)}, u32[]{:S(2)}) collective-permute-start(bf16[64,1280]{1,0:T(8,128)(2,1)S(1)} %get-tuple-element.183.refs_5_), channel_id=1, source_target_pairs={{0,2},{1,3},{2,0},{3,1},{4,6},{5,7},{6,4},{7,5},{8,10},{9,11},{10,... | collective-permute-start | bytes 491528 | tf_op jit(solution)/shard_map/ppermute | solution.py:22
  59.4 20.1 %collective-permute-start.22 = (bf16[128,1280]{1,0:T(8,128)(2,1)S(1)}, bf16[128,1280]{1,0:T(8,128)(2,1)S(1)}, u32[]{:S(2)}, u32[]{:S(2)}) collective-permute-start(bf16[128,1280]{1,0:T(8,128)(2,1)S(1)} %get-tuple-element.191), channel_id=1, source_target_pairs={{0,4},{4,0},{1,5},{5,1},{2,6},{6,2},{3,7},{7,3},{8,12},{12,8},{9,1... | collective-permute-start | bytes 983048 | tf_op jit(solution)/shard_map/ppermute | solution.py:27
  64.3 9.1 %collective-permute-start.15 = (bf16[64,1280]{1,0:T(8,128)(2,1)S(1)}, bf16[64,1280]{1,0:T(8,128)(2,1)S(1)}, u32[]{:S(2)}, u32[]{:S(2)}) collective-permute-start(bf16[64,1280]{1,0:T(8,128)(2,1)S(1)} %get-tuple-element.179), channel_id=1, source_target_pairs={{0,1},{1,0},{2,3},{3,2},{4,5},{5,4},{6,7},{7,6},{8,9},{9,8},{10,11... | collective-permute-start | bytes 491528 | tf_op jit(solution)/shard_map/ppermute | solution.py:22
  72.1 7.4 %collective-permute-start.20 = (bf16[64,1280]{1,0:T(8,128)(2,1)S(1)}, bf16[64,1280]{1,0:T(8,128)(2,1)S(1)}, u32[]{:S(2)}, u32[]{:S(2)}) collective-permute-start(bf16[64,1280]{1,0:T(8,128)(2,1)S(1)} %get-tuple-element.188), channel_id=1, source_target_pairs={{8,1},{9,0},{10,3},{11,2},{16,9},{17,8},{18,11},{19,10},{24,17},{2... | collective-permute-start | bytes 491528 | tf_op jit(solution)/shard_map/ppermute | solution.py:40
  73.5 10.5 %collective-permute-start.18 = (bf16[64,1280]{1,0:T(8,128)(2,1)S(1)}, bf16[64,1280]{1,0:T(8,128)(2,1)S(1)}, u32[]{:S(2)}, u32[]{:S(2)}) collective-permute-start(bf16[64,1280]{1,0:T(8,128)(2,1)S(1)} %get-tuple-element.187.refs_0_), channel_id=1, source_target_pairs={{0,2},{1,3},{2,0},{3,1},{4,6},{5,7},{6,4},{7,5},{8,10},{9,11},{10,... | collective-permute-start | bytes 491528 | tf_op jit(solution)/shard_map/ppermute | solution.py:22
  73.6 20.9 %collective-permute-start.27 = (bf16[128,1920]{1,0:T(8,128)(2,1)S(1)}, bf16[128,1920]{1,0:T(8,128)(2,1)S(1)}, u32[]{:S(2)}, u32[]{:S(2)}) collective-permute-start(bf16[128,1920]{1,0:T(8,128)(2,1)S(1)} %get-tuple-element.204.refs_5_), channel_id=1, source_target_pairs={{0,4},{4,0},{1,5},{5,1},{2,6},{6,2},{3,7},{7,3},{8,12},{12,8},{9,1... | collective-permute-start | bytes 1474568 | tf_op jit(solution)/shard_map/ppermute | solution.py:27
  74.3 16.4 %collective-permute-start.17 = (bf16[128,1280]{1,0:T(8,128)(2,1)S(1)}, bf16[128,1280]{1,0:T(8,128)(2,1)S(1)}, u32[]{:S(2)}, u32[]{:S(2)}) collective-permute-start(bf16[128,1280]{1,0:T(8,128)(2,1)S(1)} %get-tuple-element.186), channel_id=1, source_target_pairs={{8,0},{16,8},{24,16},{9,1},{17,9},{25,17},{10,2},{18,10},{26,18},{... | collective-permute-start | bytes 983048 | tf_op jit(solution)/shard_map/ppermute | solution.py:32
  84.1 17.0 %collective-permute-start.30 = (bf16[128,1920]{1,0:T(8,128)(2,1)S(1)}, bf16[128,1920]{1,0:T(8,128)(2,1)S(1)}, u32[]{:S(2)}, u32[]{:S(2)}) collective-permute-start(bf16[128,1920]{1,0:T(8,128)(2,1)S(1)} %get-tuple-element.211.refs_5_), channel_id=1, source_target_pairs={{0,4},{4,0},{1,5},{5,1},{2,6},{6,2},{3,7},{7,3},{8,12},{12,8},{9,1... | collective-permute-start | bytes 1474568 | tf_op jit(solution)/shard_map/ppermute | solution.py:27
  87.1 7.4 %collective-permute-start.26 = (bf16[64,1280]{1,0:T(8,128)(2,1)S(1)}, bf16[64,1280]{1,0:T(8,128)(2,1)S(1)}, u32[]{:S(2)}, u32[]{:S(2)}) collective-permute-start(bf16[64,1280]{1,0:T(8,128)(2,1)S(1)} %get-tuple-element.203.refs_0_), channel_id=1, source_target_pairs={{0,2},{1,3},{2,0},{3,1},{4,6},{5,7},{6,4},{7,5},{8,10},{9,11},{10,... | collective-permute-start | bytes 491528 | tf_op jit(solution)/shard_map/ppermute | solution.py:22
  89.5 11.7 %collective-permute-start.25 = (bf16[128,1280]{1,0:T(8,128)(2,1)S(1)}, bf16[128,1280]{1,0:T(8,128)(2,1)S(1)}, u32[]{:S(2)}, u32[]{:S(2)}) collective-permute-start(bf16[128,1280]{1,0:T(8,128)(2,1)S(1)} %get-tuple-element.200), channel_id=1, source_target_pairs={{8,0},{16,8},{24,16},{9,1},{17,9},{25,17},{10,2},{18,10},{26,18},{... | collective-permute-start | bytes 983048 | tf_op jit(solution)/shard_map/ppermute | solution.py:32
  103.8 8.1 %collective-permute-start.31 = (bf16[64,1280]{1,0:T(8,128)(2,1)S(1)}, bf16[64,1280]{1,0:T(8,128)(2,1)S(1)}, u32[]{:S(2)}, u32[]{:S(2)}) collective-permute-start(bf16[64,1280]{1,0:T(8,128)(2,1)S(1)} %get-tuple-element.218), channel_id=1, source_target_pairs={{0,1},{1,0},{2,3},{3,2},{4,5},{5,4},{6,7},{7,6},{8,9},{9,8},{10,11... | collective-permute-start | bytes 491528 | tf_op jit(solution)/shard_map/ppermute | solution.py:22
  109.8 8.9 %collective-permute-start.34 = (bf16[64,1280]{1,0:T(8,128)(2,1)S(1)}, bf16[64,1280]{1,0:T(8,128)(2,1)S(1)}, u32[]{:S(2)}, u32[]{:S(2)}) collective-permute-start(bf16[64,1280]{1,0:T(8,128)(2,1)S(1)} %get-tuple-element.227), channel_id=1, source_target_pairs={{0,1},{1,0},{2,3},{3,2},{4,5},{5,4},{6,7},{7,6},{8,9},{9,8},{10,11... | collective-permute-start | bytes 491528 | tf_op jit(solution)/shard_map/ppermute | solution.py:22
  111.9 11.1 %collective-permute-start.33 = (bf16[64,1280]{1,0:T(8,128)(2,1)S(1)}, bf16[64,1280]{1,0:T(8,128)(2,1)S(1)}, u32[]{:S(2)}, u32[]{:S(2)}) collective-permute-start(bf16[64,1280]{1,0:T(8,128)(2,1)S(1)} %get-tuple-element.225.refs_0_), channel_id=1, source_target_pairs={{0,2},{1,3},{2,0},{3,1},{4,6},{5,7},{6,4},{7,5},{8,10},{9,11},{10,... | collective-permute-start | bytes 491528 | tf_op jit(solution)/shard_map/ppermute | solution.py:22
  116.6 18.7 %collective-permute-start.38 = (bf16[128,1280]{1,0:T(8,128)(2,1)S(1)}, bf16[128,1280]{1,0:T(8,128)(2,1)S(1)}, u32[]{:S(2)}, u32[]{:S(2)}) collective-permute-start(bf16[128,1280]{1,0:T(8,128)(2,1)S(1)} %get-tuple-element.250), channel_id=1, source_target_pairs={{0,4},{4,0},{1,5},{5,1},{2,6},{6,2},{3,7},{7,3},{8,12},{12,8},{9,1... | collective-permute-start | bytes 983048 | tf_op jit(solution)/shard_map/ppermute | solution.py:27
  117.2 18.2 %collective-permute-start.39 = (bf16[1280,128]{1,0:T(8,128)(2,1)S(1)}, bf16[1280,128]{1,0:T(8,128)(2,1)S(1)}, u32[]{:S(2)}, u32[]{:S(2)}) collective-permute-start(bf16[1280,128]{1,0:T(8,128)(2,1)S(1)} %get-tuple-element.251.refs_6_), channel_id=1, source_target_pairs={{0,4},{4,0},{1,5},{5,1},{2,6},{6,2},{3,7},{7,3},{8,12},{12,8},{9,1... | collective-permute-start | bytes 983048 | tf_op jit(solution)/shard_map/ppermute | solution.py:27
  118.8 14.5 %collective-permute-start.36 = (bf16[64,1280]{1,0:T(8,128)(2,1)S(1)}, bf16[64,1280]{1,0:T(8,128)(2,1)S(1)}, u32[]{:S(2)}, u32[]{:S(2)}) collective-permute-start(bf16[64,1280]{1,0:T(8,128)(2,1)S(1)} %get-tuple-element.234.refs_0_), channel_id=1, source_target_pairs={{0,2},{1,3},{2,0},{3,1},{4,6},{5,7},{6,4},{7,5},{8,10},{9,11},{10,... | collective-permute-start | bytes 491528 | tf_op jit(solution)/shard_map/ppermute | solution.py:22
  123.1 10.7 %collective-permute-start.35 = (bf16[64,1280]{1,0:T(8,128)(2,1)S(1)}, bf16[64,1280]{1,0:T(8,128)(2,1)S(1)}, u32[]{:S(2)}, u32[]{:S(2)}) collective-permute-start(bf16[64,1280]{1,0:T(8,128)(2,1)S(1)} %get-tuple-element.233.refs_3_), channel_id=1, source_target_pairs={{0,1},{1,0},{2,3},{3,2},{4,5},{5,4},{6,7},{7,6},{8,9},{9,8},{10,11... | collective-permute-start | bytes 491528 | tf_op jit(solution)/shard_map/ppermute | solution.py:22
  (22 other events, 183.1 us)
